TPU v7x, 32 devices: a whole 2x2x4 slice. The times are simulated.
32 devices in a mesh: dp: 8 (over y, x, core), fsdp: 4 (over z).
Axes of the slice: x: 2, y: 2, z: 4, core: 2. Of those that a mesh axis runs over, the one named last changes fastest.
Arguments:
- query: bfloat16 [1024, 4096], P('dp', 'fsdp'), may hold values from -6 to 6
- key: bfloat16 [1024, 4096], P('dp', 'fsdp'), may hold values from -6 to 6
- value: bfloat16 [1024, 4096], P('dp', 'fsdp'), may hold values from -6 to 6
- upstream: bfloat16 [1024, 4096], P('dp', 'fsdp'), may hold values from -480 to 480
- reward: int32 [1024], P('dp'), may hold values from -4 to 4
- lengths: int32 [4], replicated, may hold values from 1 to 16, 32 in all
- se_filter: bfloat16 [3, 7, 4096], P(None, None, 'fsdp'), may hold values from -2 to 2
- mr_filter: bfloat16 [128, 256], P(None, 'fsdp'), may hold values from -0.5 to 0.5
Outputs:
- grad_se: float32 [3, 7, 4096], P(None, None, 'fsdp')
- grad_mr: float32 [128, 256], P(None, 'fsdp')
Inputs may be any that keep to these rules, and one draw needn't show every extreme that they name: The sequence packs 4 whole documents in order; entry i is the length of document i in blocks of 32 tokens; the lengths sum to 32 and the longest is exactly 16. A token's reward weight is its level divided by 4.
All inputs are finite; a program needn't handle non-finite values.
Results may differ from a plain program's by a relative error of at most 0.0041.
Values may be sent and summed in bfloat16 or wider, within the bound.
No kernel may reach another device: no remote copies, remote signals or barrier semaphores. Data moves between devices by JAX's collectives and lax.ppermute only.
A program may use at most 64 MiB of HBM per device.

v0:
```python
import jax
import jax.numpy as jnp
from jax import lax
from jax.sharding import PartitionSpec as P

CH = 4096
BLOCK = 32


def passed_along(value, axis, steps):
    count = lax.axis_size(axis)
    leading, last = (max(0, -steps), min(count, count - steps))
    return lax.ppermute(value, axis, [(source, source + steps) for source in range(leading, last)])


def block_docs(length_row, block_pos):
    ends = jnp.cumsum(length_row)
    counts = jnp.sum((block_pos[:, None] >= ends[None, :]).astype(jnp.int32), axis=1)
    return jnp.where(block_pos >= 0, counts, -1)


def band_matrix(vector, row_count):
    group_here, vec_len = vector.shape
    win_len = vec_len - 1
    tiled = jnp.tile(vector, (1, row_count))[:, : row_count * win_len]
    return tiled.reshape(group_here, row_count, win_len)


def forward_vector(medium_taps, block_rows):
    group_here = medium_taps.shape[1]
    head = jnp.zeros((group_here, 1), medium_taps.dtype)
    tail = jnp.zeros((group_here, block_rows), medium_taps.dtype)
    return jnp.concatenate([head, jnp.flip(medium_taps.T, axis=1), tail], axis=1)


def backward_vector(medium_taps, block_rows):
    group_here = medium_taps.shape[1]
    tail = jnp.zeros((group_here, block_rows + 1), medium_taps.dtype)
    return jnp.concatenate([medium_taps.T, tail], axis=1)


def diagonal_sums(products, filter_len):
    group_here, block_rows, win_len = products.shape
    flat = products.reshape(group_here, block_rows * win_len)
    flat = jnp.pad(flat, ((0, 0), (0, block_rows)))
    skewed = flat.reshape(group_here, block_rows, win_len + 1)
    totals = jnp.sum(skewed[:, :, 1 : filter_len + 1], axis=1)
    return jnp.flip(totals, axis=1).T


def block_windows(extended, sub_count, span_blocks, block_rows):
    channels = extended.shape[1]
    pieces = extended.reshape(sub_count + span_blocks, block_rows, channels)
    return jnp.stack(
        [pieces[shift_idx : shift_idx + sub_count] for shift_idx in range(span_blocks + 1)], axis=1
    )


def short_filter(extended, token_docs, taps, row_count):
    edge = taps.shape[0] - 1
    result = jnp.zeros((row_count, extended.shape[1]), jnp.float32)
    for shift_idx in range(taps.shape[0]):
        begin = edge - shift_idx
        same_doc = (token_docs[edge:] == token_docs[begin : begin + row_count]).astype(jnp.float32)
        result = (
            result
            + taps[shift_idx].astype(jnp.float32)[None, :]
            * extended[begin : begin + row_count].astype(jnp.float32)
            * same_doc[:, None]
        )
    return result


def short_grads(cotangent, extended, token_docs, tap_count, row_count):
    edge = tap_count - 1
    rows_out = []
    for shift_idx in range(tap_count):
        begin = edge - shift_idx
        same_doc = (token_docs[edge:] == token_docs[begin : begin + row_count]).astype(jnp.float32)
        rows_out.append(
            jnp.sum(
                cotangent
                * extended[begin : begin + row_count].astype(jnp.float32)
                * same_doc[:, None],
                axis=0,
            )
        )
    return jnp.stack(rows_out, axis=0)


def on_device(query, key, value, upstream, reward, lengths, se_filter, mr_filter):
    row_count = query.shape[0]
    channels = query.shape[1]
    filter_len = mr_filter.shape[0]
    group_all = mr_filter.shape[1]
    group_width = channels // group_all
    tap_count = se_filter.shape[1]
    edge = tap_count - 1
    block_rows = BLOCK
    sub_count = row_count // block_rows
    span_blocks = filter_len // block_rows
    win_len = block_rows + filter_len
    up_float = upstream.astype(jnp.float32)
    total_sq = lax.psum(jnp.sum(up_float * up_float, axis=1), "fsdp")
    inv_norm = lax.rsqrt(total_sq / CH + 1e-06)
    rims = passed_along(
        (query[row_count - edge :], key[row_count - edge :], value[row_count - edge :]), "dp", 1
    )
    lane_index = lax.axis_index("dp")
    block_pos = lane_index * sub_count + jnp.arange(
        -span_blocks, sub_count + span_blocks, dtype=jnp.int32
    )
    docs_all = block_docs(lengths, block_pos)
    own_docs = docs_all[span_blocks : span_blocks + sub_count]
    fwd_mask = jnp.stack(
        [own_docs == docs_all[idx : idx + sub_count] for idx in range(span_blocks + 1)], axis=1
    )
    token_docs = jnp.repeat(docs_all[span_blocks - 1 : span_blocks + sub_count], block_rows)[
        block_rows - edge :
    ]
    q_ext = jnp.concatenate([rims[0], query], axis=0)
    k_ext = jnp.concatenate([rims[1], key], axis=0)
    v_ext = jnp.concatenate([rims[2], value], axis=0)
    q_short = short_filter(q_ext, token_docs, se_filter[0], row_count)
    k_short = short_filter(k_ext, token_docs, se_filter[1], row_count)
    v_short = short_filter(v_ext, token_docs, se_filter[2], row_count)
    products = (k_short * v_short).astype(jnp.bfloat16)
    weight_rows = reward.astype(jnp.float32) * 0.25 * inv_norm
    cotangent = weight_rows[:, None] * up_float
    dm_rows = (cotangent * q_short).astype(jnp.bfloat16)
    dm_four = dm_rows.reshape(sub_count, block_rows, group_all, group_width)
    z_rim = passed_along(products, "dp", 1)
    z_ext = jnp.concatenate([z_rim, products], axis=0)
    z_win = block_windows(z_ext, sub_count, span_blocks, block_rows) * fwd_mask[
        :, :, None, None
    ].astype(jnp.bfloat16)
    z_win = z_win.reshape(sub_count, win_len, group_all, group_width)
    fwd_band = band_matrix(forward_vector(mr_filter, block_rows), block_rows)
    medium = jnp.einsum(
        "gpr,nrgc->npgc", fwd_band, z_win, preferred_element_type=jnp.float32
    ).reshape(row_count, channels)
    pair = jnp.einsum("npgc,nrgc->gpr", dm_four, z_win, preferred_element_type=jnp.float32)
    local_medium = diagonal_sums(pair, filter_len)
    dm_next = passed_along(dm_rows, "dp", -1)
    dm_ext = jnp.concatenate([dm_rows, dm_next], axis=0)
    bwd_mask = jnp.stack(
        [
            own_docs == docs_all[span_blocks + idx : span_blocks + idx + sub_count]
            for idx in range(span_blocks + 1)
        ],
        axis=1,
    )
    dm_win = block_windows(dm_ext, sub_count, span_blocks, block_rows) * bwd_mask[
        :, :, None, None
    ].astype(jnp.bfloat16)
    dm_win = dm_win.reshape(sub_count, win_len, group_all, group_width)
    bwd_band = band_matrix(backward_vector(mr_filter, block_rows), block_rows)
    dz_rows = jnp.einsum(
        "gpr,nrgc->npgc", bwd_band, dm_win, preferred_element_type=jnp.float32
    ).reshape(row_count, channels)
    cot_query = cotangent * medium
    cot_key = dz_rows * v_short
    cot_value = dz_rows * k_short
    local_short = jnp.stack(
        [
            short_grads(cot_query, q_ext, token_docs, tap_count, row_count),
            short_grads(cot_key, k_ext, token_docs, tap_count, row_count),
            short_grads(cot_value, v_ext, token_docs, tap_count, row_count),
        ],
        axis=0,
    )
    total_short, total_medium = lax.psum((local_short, local_medium), "dp")
    return (total_short / row_count, total_medium / row_count)


def solution(mesh):
    in_specs = (
        P("dp", "fsdp"),
        P("dp", "fsdp"),
        P("dp", "fsdp"),
        P("dp", "fsdp"),
        P("dp"),
        P(),
        P(None, None, "fsdp"),
        P(None, "fsdp"),
    )
    out_specs = (P(None, None, "fsdp"), P(None, "fsdp"))
    return jax.shard_map(
        on_device, mesh=mesh, in_specs=in_specs, out_specs=out_specs, check_vma=False
    )
```

profile of v0, /device:TPU:0, one launch (start us, length us, event | category | flops | bytes accessed | tf_op | source)
XLA Modules:
  0.0 173.3 jit_solution(3251825825417772161)
XLA Ops:
  7.9 2.3 %collective-permute-start.1 = (bf16[6,1024]{1,0:T(8,128)(2,1)S(1)}, bf16[6,1024]{1,0:T(8,128)(2,1)S(1)}, u32[]{:S(2)}, u32[]{:S(2)}) collective-permute-start(bf16[6,1024]{1,0:T(8,128)(2,1)S(1)} %slice.396), channel_id=1, source_target_pairs={{0,4},{4,8},{8,12},{12,16},{16,20},{20,24},{24,28},{1,5},{5,9},{9,... | collective-permute-start | bytes 36872 | tf_op jit(solution)/shard_map/ppermute | solution.py:13
  11.0 4.5 %collective-permute-start.3 = (bf16[6,1024]{1,0:T(8,128)(2,1)S(1)}, bf16[6,1024]{1,0:T(8,128)(2,1)S(1)}, u32[]{:S(2)}, u32[]{:S(2)}) collective-permute-start(bf16[6,1024]{1,0:T(8,128)(2,1)S(1)} %slice.416), channel_id=1, source_target_pairs={{0,4},{4,8},{8,12},{12,16},{16,20},{20,24},{24,28},{1,5},{5,9},{9,... | collective-permute-start | bytes 36872 | tf_op jit(solution)/shard_map/ppermute | solution.py:13
  16.2 1.9 %collective-permute-start = (bf16[6,1024]{1,0:T(8,128)(2,1)S(1)}, bf16[6,1024]{1,0:T(8,128)(2,1)S(1)}, u32[]{:S(2)}, u32[]{:S(2)}) collective-permute-start(bf16[6,1024]{1,0:T(8,128)(2,1)S(1)} %slice.373), channel_id=1, source_target_pairs={{0,4},{4,8},{8,12},{12,16},{16,20},{20,24},{24,28},{1,5},{5,9},{9,... | collective-permute-start | bytes 36872 | tf_op jit(solution)/shard_map/ppermute | solution.py:13
  22.8 12.0 %psum.21 = f32[128]{0:T(128)S(1)} all-reduce(f32[128]{0:T(128)S(1)} %fusion.21), channel_id=1, replica_groups=mesh['dp'=8,'fsdp'=4] {'fsdp'}, use_global_device_ids=true, to_apply=%region_1.0 | all-reduce | flops 128 | bytes 1024 | tf_op jit(solution)/shard_map/psum | solution.py:104
  38.7 2.3 %reshape.398 = bf16[64,32,160,1]{2,1,0,3:T(8,128)(2,1)} reshape(bf16[64,5120]{1,0:T(8,128)(2,1)S(1)} %slice.478) | data formatting | bytes 1310720 | tf_op jit(solution)/shard_map/reshape | solution.py:26
  43.3 2.4 %reshape.397 = bf16[64,32,160,1]{2,1,0,3:T(8,128)(2,1)} reshape(bf16[64,5120]{1,0:T(8,128)(2,1)S(1)} %slice.463) | data formatting | bytes 1310720 | tf_op jit(solution)/shard_map/reshape | solution.py:26
  48.5 2.2 %multiply_convert_fusion = (bf16[128,1024]{1,0:T(8,128)(2,1)}, f32[128,1024]{1,0:T(8,128)}, f32[128,1024]{1,0:T(8,128)}) fusion(f32[128]{0:T(128)S(1)} %get-tuple-element.54, bf16[128,1024]{1,0:T(8,128)(2,1)S(1)} %copy-done.1, bf16[6,1024]{1,0:T(8,128)(2,1)S(1)} %collective-permute-done.1, f32[1024]{0:T(1024)S(1)} %bitcast.113, ...), kind=kLoop, calls=%fused_computation.161 | loop fusion | flops 11796480 | bytes 1920000 | tf_op jit(solution)/shard_map/convert_element_type | solution.py:127
  50.9 3.7 %collective-permute-start.2 = (bf16[128,1024]{1,0:T(8,128)(2,1)}, bf16[128,1024]{1,0:T(8,128)(2,1)}, u32[]{:S(2)}, u32[]{:S(2)}) collective-permute-start(bf16[128,1024]{1,0:T(8,128)(2,1)} %get-tuple-element.21), channel_id=1, source_target_pairs={{0,4},{4,8},{8,12},{12,16},{16,20},{20,24},{24,28},{1,5},{5,9},{9,... | collective-permute-start | bytes 786440 | tf_op jit(solution)/shard_map/ppermute | solution.py:13
  57.2 7.6 %copy.77 = bf16[4,5,32,1024]{2,1,3,0:T(8,128)(2,1)} copy(bf16[4,5,32,1024]{3,2,0,1:T(8,128)(2,1)S(1)} %constant_dynamic-update-slice_fusion.5) | data formatting | bytes 2621440 | tf_op jit(solution)/shard_map/stack | solution.py:54
  64.9 8.8 %stack.186 = bf16[4,160,64,16]{1,3,2,0:T(8,128)(2,1)S(1)} reshape(bf16[4,5,32,1024]{2,1,3,0:T(8,128)(2,1)} %copy.77) | data formatting | bytes 2621440 | tf_op jit(solution)/shard_map/stack | solution.py:54
  73.7 1.9 %fusion.12 = f32[4,32,64,16]{1,3,0,2:T(8,128)S(1)} fusion(bf16[64,32,160,1]{2,1,0,3:T(8,128)(2,1)} %reshape.398, bf16[4,160,64,16]{1,3,2,0:T(8,128)(2,1)S(1)} %stack.186, bf16[4,160]{1,0:T(4,128)(2,1)S(1)} %mul.641), kind=kOutput, calls=%fused_computation.8 | convolution fusion | flops 42598400 | bytes 2491648 | tf_op jit(solution)/shard_map/gpr,nrgc->npgc/dot_general | solution.py:158
  79.6 2.9 %fusion.71 = (f32[1024]{0:T(1024)S(1)}, f32[1024]{0:T(1024)S(1)}, f32[1024]{0:T(1024)S(1)}, f32[1024]{0:T(1024)S(1)}, f32[1024]{0:T(1024)S(1)}, /*index=5*/f32[1024]{0:T(1024)S(1)}, f32[128,1024]{1,0:T(8,128)S(1)}) fusion(bf16[128,1024]{1,0:T(8,128)(2,1)} %param.10, bf16[6,1024]{1,0:T(8,128)(2,1)S(1)} %collective-permute-done.1, ...), kind=kLoop, calls=%fused_computation.135 | loop fusion | flops 5629952 | bytes 1874944 | tf_op jit(solution)/shard_map/reduce_sum | solution.py:81
  86.6 7.6 %copy.69 = bf16[4,5,32,1024]{2,1,3,0:T(8,128)(2,1)} copy(bf16[4,5,32,1024]{3,2,0,1:T(8,128)(2,1)S(1)} %constant_dynamic-update-slice_fusion) | data formatting | bytes 2621440 | tf_op jit(solution)/shard_map/stack | solution.py:54
  94.3 8.8 %stack.164 = bf16[4,160,64,16]{1,3,2,0:T(8,128)(2,1)S(1)} reshape(bf16[4,5,32,1024]{2,1,3,0:T(8,128)(2,1)} %copy.69) | data formatting | bytes 2621440 | tf_op jit(solution)/shard_map/stack | solution.py:54
  103.1 1.9 %fusion.6 = f32[4,32,64,16]{1,3,0,2:T(8,128)S(1)} fusion(bf16[64,32,160,1]{2,1,0,3:T(8,128)(2,1)} %reshape.397, bf16[4,160,64,16]{1,3,2,0:T(8,128)(2,1)S(1)} %stack.164, bf16[4,160]{1,0:T(4,128)(2,1)S(1)} %mul.602), kind=kOutput, calls=%fused_computation.6 | convolution fusion | flops 42598400 | bytes 2491648 | tf_op jit(solution)/shard_map/gpr,nrgc->npgc/dot_general | solution.py:139
  105.0 2.3 %copy.75 = f32[4,32,64,16]{1,0,3,2:T(4,128)} copy(f32[4,32,64,16]{1,3,0,2:T(8,128)S(1)} %fusion.6) | data formatting | bytes 1048576 | tf_op jit(solution)/shard_map/gpr,nrgc->npgc/transpose | solution.py:139
  107.3 3.1 %reshape.370 = f32[128,1024]{0,1:T(8,128)} reshape(f32[4,32,64,16]{1,0,3,2:T(4,128)} %copy.75) | data formatting | bytes 1048576 | tf_op jit(solution)/shard_map/reshape | solution.py:141
  110.4 2.0 %copy.76 = f32[128,1024]{1,0:T(8,128)} copy(f32[128,1024]{0,1:T(8,128)} %reshape.370) | data formatting | bytes 1048576 | tf_op jit(solution)/shard_map/reshape | solution.py:141
  112.4 1.8 %fusion.95 = (f32[1024]{0:T(1024)S(1)}, f32[1024]{0:T(1024)S(1)}, f32[1024]{0:T(1024)S(1)}, f32[1024]{0:T(1024)S(1)}, f32[1024]{0:T(1024)S(1)}, /*index=5*/f32[1024]{0:T(1024)S(1)}, f32[128,1024]{1,0:T(8,128)S(1)}) fusion(bf16[128,1024]{1,0:T(8,128)(2,1)S(1)} %copy-done, bf16[6,1024]{1,0:T(8,128)(2,1)S(1)} %collective-permute-done.3, ...), kind=kLoop, calls=%fused_computation.159 | loop fusion | flops 5892096 | bytes 1613312 | tf_op jit(solution)/shard_map/reduce_sum | solution.py:81
  115.2 2.0 %fusion.9 = f32[64,32,160]{2,1,0:T(8,128)} fusion(bf16[4,32,64,16]{1,0,3,2:T(4,128)(2,1)S(1)} %reshape.373, bf16[4,160,64,16]{1,3,2,0:T(8,128)(2,1)S(1)} %stack.164, bf16[4,160]{1,0:T(4,128)(2,1)S(1)} %mul.602), kind=kOutput, calls=%fused_computation.7 | convolution fusion | flops 42598400 | bytes 2884864 | tf_op jit(solution)/shard_map/npgc,nrgc->gpr/dot_general | solution.py:142
  117.2 2.6 %reshape.374 = f32[64,5120]{1,0:T(8,128)S(1)} reshape(f32[64,32,160]{2,1,0:T(8,128)} %fusion.9) | data formatting | bytes 2621440 | tf_op jit(solution)/shard_map/reshape | solution.py:44
  119.9 2.9 %reshape.375 = f32[64,32,161]{2,1,0:T(8,128)S(1)} reshape(f32[64,5152]{1,0:T(8,128)S(1)} %pad.5) | data formatting | bytes 2637824 | tf_op jit(solution)/shard_map/reshape | solution.py:46
  123.2 22.8 %psum.23 = f32[128,64]{0,1:T(8,128)S(1)} all-reduce(f32[128,64]{0,1:T(8,128)S(1)} %bitcast.106), channel_id=1, replica_groups=mesh['dp'=8,'fsdp'=4] {'dp'}, use_global_device_ids=true, to_apply=%region_27.28 | all-reduce | flops 8192 | bytes 65536 | tf_op jit(solution)/shard_map/psum | solution.py:172
  146.6 18.3 %all-reduce.4.cloned.1.call-done = f32[3,7,1024]{2,1,0:T(8,128)} async-done(((f32[3,7,1024]{2,1,0:T(8,128)}), f32[3,7,1024]{2,1,0:T(8,128)}) %all-reduce.4.cloned.1.call-update) | async-done | bytes 86032 | tf_op jit(solution)/shard_map/psum | solution.py:172
  (101 shorter events, 30.1 us)
Async XLA Ops:
  7.2 157.7 %all-reduce.4.cloned.1.call-start = ((), (), s32[]{:S(2)}) async-start(), calls=%async_computation | async-start | bytes 196608 | tf_op jit(solution)/shard_map/psum | solution.py:172
  7.9 40.5 %collective-permute-start.1 = (bf16[6,1024]{1,0:T(8,128)(2,1)S(1)}, bf16[6,1024]{1,0:T(8,128)(2,1)S(1)}, u32[]{:S(2)}, u32[]{:S(2)}) collective-permute-start(bf16[6,1024]{1,0:T(8,128)(2,1)S(1)} %slice.396), channel_id=1, source_target_pairs={{0,4},{4,8},{8,12},{12,16},{16,20},{20,24},{24,28},{1,5},{5,9},{9,... | collective-permute-start | bytes 36872 | tf_op jit(solution)/shard_map/ppermute | solution.py:13
  11.0 35.3 %collective-permute-start.3 = (bf16[6,1024]{1,0:T(8,128)(2,1)S(1)}, bf16[6,1024]{1,0:T(8,128)(2,1)S(1)}, u32[]{:S(2)}, u32[]{:S(2)}) collective-permute-start(bf16[6,1024]{1,0:T(8,128)(2,1)S(1)} %slice.416), channel_id=1, source_target_pairs={{0,4},{4,8},{8,12},{12,16},{16,20},{20,24},{24,28},{1,5},{5,9},{9,... | collective-permute-start | bytes 36872 | tf_op jit(solution)/shard_map/ppermute | solution.py:13
  16.2 32.2 %collective-permute-start = (bf16[6,1024]{1,0:T(8,128)(2,1)S(1)}, bf16[6,1024]{1,0:T(8,128)(2,1)S(1)}, u32[]{:S(2)}, u32[]{:S(2)}) collective-permute-start(bf16[6,1024]{1,0:T(8,128)(2,1)S(1)} %slice.373), channel_id=1, source_target_pairs={{0,4},{4,8},{8,12},{12,16},{16,20},{20,24},{24,28},{1,5},{5,9},{9,... | collective-permute-start | bytes 36872 | tf_op jit(solution)/shard_map/ppermute | solution.py:13
  41.8 4.6 %copy-start = (bf16[128,1024]{1,0:T(8,128)(2,1)S(1)}, bf16[128,1024]{1,0:T(8,128)(2,1)}, u32[]{:S(2)}) copy-start(bf16[128,1024]{1,0:T(8,128)(2,1)} %param.8) | copy-start | bytes 786436
  41.8 4.6 %copy-start.5 = (bf16[128,1024]{1,0:T(8,128)(2,1)S(1)}, bf16[128,1024]{1,0:T(8,128)(2,1)}, u32[]{:S(2)}) copy-start(bf16[128,1024]{1,0:T(8,128)(2,1)} %param.11) | copy-start | bytes 786436
  43.2 5.3 %copy-start.1 = (bf16[128,1024]{1,0:T(8,128)(2,1)S(1)}, bf16[128,1024]{1,0:T(8,128)(2,1)}, u32[]{:S(2)}) copy-start(bf16[128,1024]{1,0:T(8,128)(2,1)} %param.10) | copy-start | bytes 786436
  43.2 5.3 %copy-start.3 = (bf16[128,1024]{1,0:T(8,128)(2,1)S(1)}, bf16[128,1024]{1,0:T(8,128)(2,1)}, u32[]{:S(2)}) copy-start(bf16[128,1024]{1,0:T(8,128)(2,1)} %param.9) | copy-start | bytes 786436
  47.1 7.9 %collective-permute-start.4 = (bf16[128,1024]{1,0:T(8,128)(2,1)S(1)}, bf16[128,1024]{1,0:T(8,128)(2,1)}, u32[]{:S(2)}, u32[]{:S(2)}) collective-permute-start(bf16[128,1024]{1,0:T(8,128)(2,1)S(1)} %fusion.20), channel_id=1, source_target_pairs={{4,0},{8,4},{12,8},{16,12},{20,16},{24,20},{28,24},{5,1},{9,5},{13... | collective-permute-start | bytes 786440 | tf_op jit(solution)/shard_map/ppermute | solution.py:13
  50.9 32.5 %collective-permute-start.2 = (bf16[128,1024]{1,0:T(8,128)(2,1)}, bf16[128,1024]{1,0:T(8,128)(2,1)}, u32[]{:S(2)}, u32[]{:S(2)}) collective-permute-start(bf16[128,1024]{1,0:T(8,128)(2,1)} %get-tuple-element.21), channel_id=1, source_target_pairs={{0,4},{4,8},{8,12},{12,16},{16,20},{20,24},{24,28},{1,5},{5,9},{9,... | collective-permute-start | bytes 786440 | tf_op jit(solution)/shard_map/ppermute | solution.py:13
  78.3 4.2 %copy-start.4 = (bf16[128,1024]{1,0:T(8,128)(2,1)S(1)}, bf16[128,1024]{1,0:T(8,128)(2,1)}, u32[]{:S(2)}) copy-start(bf16[128,1024]{1,0:T(8,128)(2,1)} %param.9) | copy-start | bytes 786436
  79.6 2.9 %copy-start.6 = (f32[128,1024]{1,0:T(8,128)S(1)}, f32[128,1024]{1,0:T(8,128)}, u32[]{:S(2)}) copy-start(f32[128,1024]{1,0:T(8,128)} %get-tuple-element.22) | copy-start | bytes 1572868
  79.6 3.6 %copy-start.2 = (bf16[128,1024]{1,0:T(8,128)(2,1)S(1)}, bf16[128,1024]{1,0:T(8,128)(2,1)}, u32[]{:S(2)}) copy-start(bf16[128,1024]{1,0:T(8,128)(2,1)} %param.10) | copy-start | bytes 786436
Sparse Core Ops, SparseCore 0:
  115.3 49.5 all-reduce.3
where the time goes:
time: 175 us; the launch traced here: 173 us
  local copies, waits for them, and re-layouts  67 us (38%)
  blocking collectives  34.8 us (20%)
  other arithmetic  19.1 us (11%)
  waiting for transfers between devices  18.3 us (10%)
  between operations  14.5 us (8%)
  starting transfers between devices  13.8 us (8%)
  matrix products  5.8 us (3%)
    another operation x6, local copies, waits for them, and re-layouts, block_windows(): jnp.stack([pieces[shift_idx:shift_idx + sub_count] for shift_idx in range...  34.8 us
    psum x1, blocking collectives, on_device(): total_short, total_medium = lax.psum((local_short, local_medium), 'dp')  22.8 us
    psum x1, waiting for transfers between devices, on_device(): total_short, total_medium = lax.psum((local_short, local_medium), 'dp')  18.3 us
    ppermute x5, starting transfers between devices, passed_along(): lax.ppermute(value, axis, [(source, source + steps) for source in range(l...  13.8 us
    psum x1, blocking collectives, on_device(): total_sq = lax.psum(jnp.sum(up_float * up_float, axis=1), 'fsdp')  12 us
    reduce_sum x6, other arithmetic, short_grads(): jnp.sum(cotangent * extended[begin:begin + row_count].astype(jnp.float32)...  5.59 us
    reshape x2, local copies, waits for them, and re-layouts, on_device(): medium = jnp.einsum('gpr,nrgc->npgc', fwd_band, z_win, preferred_element_...  5.1 us
    reshape x2, local copies, waits for them, and re-layouts, band_matrix(): return tiled.reshape(group_here, row_count, win_len)  4.67 us
  transfers between devices with their start and end apart: 6, of which 1 were waited for; matrix products, arithmetic and copies ran while one was open for 33% of the time, Pallas kernels for 0%

commit v1 on v0

v1 whole, which is shorter than its diff:
```python
import functools

import jax
import jax.numpy as jnp
from jax import lax
from jax.experimental import pallas as pl
from jax.experimental.pallas import tpu as pltpu
from jax.sharding import PartitionSpec as P

BLOCK = 32
LANES = 128
TAIL = 16
PRE = 8
SLOT = PRE + BLOCK
F32 = jnp.float32
BF16 = jnp.bfloat16


def spec(space=pltpu.VMEM):
    return pl.BlockSpec(memory_space=space)


def dot(a, b, contract, precision=None):
    return lax.dot_general(
        a, b, ((contract[0], contract[1]), ((), ())), precision=precision, preferred_element_type=F32
    )


def pack_kernel(q_ref, k_ref, v_ref, up_ref, near_ref, far_ref, sq_ref):
    rows, channels = q_ref.shape
    near_ref[0:rows] = k_ref[...]
    near_ref[rows : 2 * rows] = v_ref[...]
    near_ref[2 * rows : 2 * rows + TAIL] = q_ref[rows - TAIL : rows]
    far_ref[0:TAIL] = k_ref[rows - TAIL : rows]
    far_ref[TAIL : 2 * TAIL] = v_ref[rows - TAIL : rows]
    total = jnp.zeros((rows, LANES), F32)
    for tile in range(channels // LANES):
        part = up_ref[:, tile * LANES : (tile + 1) * LANES].astype(F32)
        total = total + part * part
    sq_ref[...] = jnp.sum(total.T, axis=0, keepdims=True)


def band_kernel(h_ref, band_ref, band_t_ref, row_ref):
    taps, groups = h_ref.shape
    tiles = band_ref.shape[0]
    per_tile = groups // tiles
    width = band_ref.shape[2]
    tap = lax.broadcasted_iota(jnp.int32, (taps, width), 0)
    lane = lax.broadcasted_iota(jnp.int32, (taps, width), 1)
    flip = jnp.where(tap + lane == taps, 1.0, 0.0).astype(F32)
    row_ref[...] = dot(h_ref[...].astype(F32).T.astype(BF16), flip.astype(BF16), ((1,), (0,)))

    def one(tile, carry):
        rows = row_ref[pl.ds(pl.multiple_of(tile * per_tile, per_tile), per_tile), :]
        parts = [
            pltpu.roll(
                jnp.broadcast_to(rows[g : g + 1], (BLOCK, width)), 0, 1, stride=1, stride_axis=0
            )
            for g in range(per_tile)
        ]
        band = jnp.concatenate(parts, axis=0)
        band_ref[tile] = band.astype(BF16)
        band_t_ref[tile] = band.T[0 : taps + BLOCK].astype(BF16)
        return carry

    lax.fori_loop(0, tiles, one, 0)


def doc_of(lengths_ref, block):
    count = jnp.int32(0)
    end = jnp.int32(0)
    for i in range(lengths_ref.shape[0]):
        end = end + lengths_ref[i]
        count = count + jnp.where(block >= end, 1, 0)
    return jnp.where(block >= 0, count, -1)


def main_kernel(
    all_channels,
    lengths_ref,
    q_ref,
    k_ref,
    v_ref,
    up_ref,
    near_ref,
    far_ref,
    sq_ref,
    reward_ref,
    se_ref,
    band_ref,
    band_t_ref,
    out_ref,
    xq_ref,
    xk_ref,
    xv_ref,
    ks_ref,
    vs_ref,
    z_ref,
    zw_ref,
    dm_ref,
    dz_ref,
    cot_ref,
    w_ref,
):
    rows, channels = q_ref.shape
    own = rows // BLOCK
    taps = band_t_ref.shape[1] - BLOCK
    span = taps // BLOCK
    window = span + own
    tiles = channels // LANES
    per_tile = band_ref.shape[1] // BLOCK
    width = LANES // per_tile
    tap_count = se_ref.shape[1]

    first = lax.axis_index("dp") * own
    docs = [doc_of(lengths_ref, first + b) for b in range(-span - 1, own)]
    joined = [(docs[b + 1] == docs[b]) & (docs[b] >= 0) for b in range(window)]
    joined = [jnp.where(flag, 1.0, 0.0).astype(F32) for flag in joined]
    docs = docs[1:]
    same = [
        [jnp.where(docs[n + s] == docs[n + span], 1.0, 0.0).astype(F32) for s in range(span + 1)]
        for n in range(own)
    ]

    weight = (
        reward_ref[...].astype(F32) * 0.25 * lax.rsqrt(sq_ref[...] / all_channels + 1e-06)
    )
    w_ref[...] = jnp.broadcast_to(weight, (LANES, rows)).T

    lane_group = lax.broadcasted_iota(jnp.int32, (BLOCK, LANES), 1) // width
    picks = [lane_group == g for g in range(per_tile)]
    masks = [jnp.where(pick, 1.0, 0.0).astype(BF16) for pick in picks]
    row_index = lax.broadcasted_iota(jnp.int32, (per_tile * 8, 2 * LANES), 0)
    z_ref[window * BLOCK :] = jnp.zeros((z_ref.shape[0] - window * BLOCK, LANES), BF16)

    def fill(x_ref, pieces, before, first_block):
        for b, piece in enumerate(pieces):
            at = SLOT * b
            x_ref[at : at + PRE] = before * joined[first_block + b]
            x_ref[at + PRE : at + SLOT] = piece
            before = piece[BLOCK - PRE :]

    def shifted(x_ref, b, j):
        at = SLOT * b + PRE - j
        return x_ref[at : at + BLOCK, :]

    def short(x_ref, b, taps_now):
        total = taps_now[0:1] * shifted(x_ref, b, 0)
        for j in range(1, tap_count):
            total = total + taps_now[j : j + 1] * shifted(x_ref, b, j)
        return total

    def fold(x):
        return jnp.sum(x.reshape(BLOCK // 8, 8, LANES), axis=0)

    def one(tile, carry):
        at = pl.ds(pl.multiple_of(tile * LANES, LANES), LANES)
        q_taps = se_ref[0, :, at].astype(F32)
        k_taps = se_ref[1, :, at].astype(F32)
        v_taps = se_ref[2, :, at].astype(F32)

        def blocks_of(ref, start, count):
            return [
                ref[start + BLOCK * b : start + BLOCK * (b + 1), at].astype(F32) for b in range(count)
            ]

        q_before = near_ref[2 * rows : 2 * rows + TAIL, at].astype(F32)[TAIL - PRE :]
        k_before = far_ref[0:TAIL, at].astype(F32)[TAIL - PRE :]
        v_before = far_ref[TAIL : 2 * TAIL, at].astype(F32)[TAIL - PRE :]
        fill(xq_ref, blocks_of(q_ref, 0, own), q_before, span)
        fill(
            xk_ref,
            blocks_of(near_ref, rows - span * BLOCK, span) + blocks_of(k_ref, 0, own),
            k_before,
            0,
        )
        fill(
            xv_ref,
            blocks_of(near_ref, 2 * rows - span * BLOCK, span) + blocks_of(v_ref, 0, own),
            v_before,
            0,
        )
        for b in range(window):
            at_b = slice(BLOCK * b, BLOCK * (b + 1))
            ks = short(xk_ref, b, k_taps)
            vs = short(xv_ref, b, v_taps)
            ks_ref[at_b] = ks
            vs_ref[at_b] = vs
            z_ref[at_b] = (ks * vs).astype(BF16)
        for n in range(own):
            at_n = slice(BLOCK * n, BLOCK * (n + 1))
            cot = w_ref[at_n] * up_ref[at_n, at].astype(F32)
            cot_ref[at_n] = cot
            dm = (cot * short(xq_ref, n, q_taps)).astype(BF16)
            lanes = slice(LANES * (n % 2), LANES * (n % 2 + 1))
            for g in range(per_tile):
                dm_ref[n // 2, BLOCK * g : BLOCK * (g + 1), lanes] = dm * masks[g]
            for s in range(2 * LANES // BLOCK):
                piece = z_ref[BLOCK * (n + s) : BLOCK * (n + s + 1)]
                if s < span:
                    piece = piece * same[n][s].astype(BF16)
                zw_ref[n // 2, BLOCK * s : BLOCK * (s + 1), lanes] = piece

        band = band_ref[tile]
        band_t = band_t_ref[tile]
        pair = jnp.zeros((per_tile * BLOCK, 2 * LANES), F32)
        gq = [jnp.zeros((8, LANES), F32) for _ in range(tap_count)]
        dz_ref[...] = jnp.zeros_like(dz_ref)
        for half in range(own // 2):
            dms = dm_ref[half]
            zws = zw_ref[half]
            wide = dot(band, zws, ((1,), (0,)))
            back = dot(band_t, dms, ((1,), (0,)))
            pair = pair + dot(dms, zws, ((1,), (1,)))
            for side in range(2):
                n = 2 * half + side
                lanes = slice(LANES * side, LANES * (side + 1))
                m = wide[0:BLOCK, lanes]
                for g in range(1, per_tile):
                    m = jnp.where(picks[g], wide[BLOCK * g : BLOCK * (g + 1), lanes], m)
                cot_q = cot_ref[BLOCK * n : BLOCK * (n + 1)] * m
                for j in range(tap_count):
                    gq[j] = gq[j] + fold(cot_q * shifted(xq_ref, n, j))
                for s in range(span + 1):
                    at_s = slice(BLOCK * (n + s), BLOCK * (n + s + 1))
                    dz_ref[at_s] += back[BLOCK * s : BLOCK * (s + 1), lanes] * same[n][s]
        gk = [jnp.zeros((8, LANES), F32) for _ in range(tap_count)]
        gv = [jnp.zeros((8, LANES), F32) for _ in range(tap_count)]
        for b in range(window):
            at_b = slice(BLOCK * b, BLOCK * (b + 1))
            dz = dz_ref[at_b]
            cot_k = dz * vs_ref[at_b]
            cot_v = dz * ks_ref[at_b]
            for j in range(tap_count):
                gk[j] = gk[j] + fold(cot_k * shifted(xk_ref, b, j))
                gv[j] = gv[j] + fold(cot_v * shifted(xv_ref, b, j))
        for i, sums in enumerate((gq, gk, gv)):
            for j in range(tap_count):
                out_ref[8 * i + j : 8 * i + j + 1, at] = jnp.sum(sums[j], axis=0, keepdims=True)
            out_ref[8 * i + tap_count : 8 * i + 8, at] = jnp.zeros((8 - tap_count, LANES), F32)
        lined = pair.reshape(per_tile, BLOCK // 8, 8, 2 * LANES)
        skew = jnp.zeros((per_tile * 8, 2 * LANES), F32)
        for r in range(BLOCK // 8):
            rows_r = lined[:, r].reshape(per_tile * 8, 2 * LANES)
            skew = skew + pltpu.roll(rows_r, 2 * LANES - 1 - 8 * r, 1)
        for bit in range(3):
            moved = pltpu.roll(skew, 2 * LANES - (1 << bit), 1)
            skew = jnp.where((row_index >> bit) & 1 == 1, moved, skew)
        out_ref[24 : 24 + per_tile, at] = jnp.sum(
            skew[:, 0:LANES].reshape(per_tile, 8, LANES), axis=1
        )
        return carry

    lax.fori_loop(0, tiles, one, 0)


def last_kernel(scale, a_ref, b_ref, se_ref, mr_ref):
    total = (a_ref[...].astype(F32) + b_ref[...].astype(F32)) * scale
    tap_count = se_ref.shape[1]
    channels = total.shape[1]
    for i in range(3):
        se_ref[i] = total[8 * i : 8 * i + tap_count]
    flat = jnp.concatenate(
        [total[24:, t * LANES : (t + 1) * LANES] for t in range(channels // LANES)], axis=0
    )
    tap = lax.broadcasted_iota(jnp.int32, (LANES, LANES), 0)
    lane = lax.broadcasted_iota(jnp.int32, (LANES, LANES), 1)
    flip = jnp.where(tap + lane == LANES - 1, 1.0, 0.0).astype(F32)
    mr_ref[...] = dot(flip, flat, ((1,), (1,)), lax.Precision.HIGHEST)


def swapped(value, axis, distance):
    count = lax.axis_size(axis)
    return lax.ppermute(value, axis, [(i, i ^ distance) for i in range(count)])


def summed_small(value, axis):
    count = lax.axis_size(axis)
    if count & (count - 1):
        return lax.psum(value, axis)
    distance = 1
    while distance < count:
        value = value + swapped(value, axis, distance)
        distance *= 2
    return value


def moved_up(value, axis, steps):
    count = lax.axis_size(axis)
    return lax.ppermute(value, axis, [(i, i + steps) for i in range(count - steps)])


def on_device(query, key, value, upstream, reward, lengths, se_filter, mr_filter):
    rows, channels = query.shape
    taps, groups = mr_filter.shape
    tap_count = se_filter.shape[1]
    tiles = channels // LANES
    per_tile = groups // tiles
    stack = per_tile * BLOCK
    own = rows // BLOCK
    window = own + taps // BLOCK
    dp = lax.axis_size("dp")

    near, far, sq = pl.pallas_call(
        pack_kernel,
        out_shape=(
            jax.ShapeDtypeStruct((2 * rows + TAIL, channels), BF16),
            jax.ShapeDtypeStruct((2 * TAIL, channels), BF16),
            jax.ShapeDtypeStruct((1, rows), F32),
        ),
        in_specs=[spec()] * 4,
        out_specs=(spec(),) * 3,
        name="pack",
    )(query, key, value, upstream)
    near = moved_up(near, "dp", 1)
    far = moved_up(far, "dp", 2)
    sq = summed_small(sq, "fsdp")

    band, band_t = pl.pallas_call(
        band_kernel,
        out_shape=(
            jax.ShapeDtypeStruct((tiles, stack, 2 * LANES), BF16),
            jax.ShapeDtypeStruct((tiles, taps + BLOCK, stack), BF16),
        ),
        in_specs=[spec()],
        out_specs=(spec(),) * 2,
        scratch_shapes=[pltpu.VMEM((groups, 2 * LANES), F32)],
        name="band",
    )(mr_filter)

    part = pl.pallas_call(
        functools.partial(main_kernel, float(channels * lax.axis_size("fsdp"))),
        out_shape=jax.ShapeDtypeStruct((24 + per_tile, channels), F32),
        in_specs=[spec(pltpu.SMEM)] + [spec()] * 11,
        out_specs=spec(),
        scratch_shapes=[
            pltpu.VMEM((own * SLOT, LANES), F32),
            pltpu.VMEM((window * SLOT, LANES), F32),
            pltpu.VMEM((window * SLOT, LANES), F32),
            pltpu.VMEM((window * BLOCK, LANES), F32),
            pltpu.VMEM((window * BLOCK, LANES), F32),
            pltpu.VMEM(((own - 1) * BLOCK + 2 * LANES, LANES), BF16),
            pltpu.VMEM((own // 2, 2 * LANES, 2 * LANES), BF16),
            pltpu.VMEM((own // 2, stack, 2 * LANES), BF16),
            pltpu.VMEM((window * BLOCK, LANES), F32),
            pltpu.VMEM((rows, LANES), F32),
            pltpu.VMEM((rows, LANES), F32),
        ],
        compiler_params=pltpu.CompilerParams(vmem_limit_bytes=32 * 1024 * 1024),
        name="main",
    )(
        lengths,
        query,
        key,
        value,
        upstream,
        near,
        far,
        sq,
        reward.reshape(1, rows),
        se_filter,
        band,
        band_t,
    )

    if dp & (dp - 1):
        part = lax.psum(part, "dp")
        other = jnp.zeros_like(part)
    else:
        distance = 1
        other = jnp.zeros_like(part)
        while distance < dp:
            other = swapped(part, "dp", distance)
            distance *= 2
            if distance < dp:
                part = (part.astype(F32) + other.astype(F32)).astype(BF16)
    grad_se, grad_mr = pl.pallas_call(
        functools.partial(last_kernel, 1.0 / rows),
        out_shape=(
            jax.ShapeDtypeStruct((3, tap_count, channels), F32),
            jax.ShapeDtypeStruct((taps, groups), F32),
        ),
        in_specs=[spec()] * 2,
        out_specs=(spec(),) * 2,
        name="last",
    )(part, other)
    return grad_se, grad_mr


def solution(mesh):
    in_specs = (
        P("dp", "fsdp"),
        P("dp", "fsdp"),
        P("dp", "fsdp"),
        P("dp", "fsdp"),
        P("dp"),
        P(),
        P(None, None, "fsdp"),
        P(None, "fsdp"),
    )
    out_specs = (P(None, None, "fsdp"), P(None, "fsdp"))
    return jax.shard_map(
        on_device, mesh=mesh, in_specs=in_specs, out_specs=out_specs, check_vma=False
    )
```

time: 175 us -> 47.4 us (0.27)
  local copies, waits for them, and re-layouts: 67 us -> 5.82 us
  blocking collectives: 34.8 us -> 0 us
  other arithmetic: 19.1 us -> 0.7 us
  Pallas kernels: 0 us -> 16.3 us
  between operations: 14.5 us -> 0.79 us
  waiting for transfers between devices: 18.3 us -> 8.96 us
  matrix products: 5.8 us -> 0 us
    another operation x24 -> x0, local copies, waits for them, and re-layouts: 39 us -> none  [the longest x6 34.8 us: block_windows(): jnp.stack([pieces[shift_idx:shift_idx + sub_count] for shift_idx in range...]
    psum x2 -> x0, blocking collectives: 34.8 us -> none  [the longest x1 22.8 us: on_device(): total_short, total_medium = lax.psum((local_short, local_medium), 'dp')]
    reshape x10 -> x0, local copies, waits for them, and re-layouts: 18.7 us -> none  [the longest x2 5.1 us: on_device(): medium = jnp.einsum('gpr,nrgc->npgc', fwd_band, z_win, preferred_element_...]
    psum x1 -> x0, waiting for transfers between devices: 18.3 us -> none  [on_device(): total_short, total_medium = lax.psum((local_short, local_medium), 'dp')]
    pallas_call x0 -> x4, Pallas kernels: none -> 16.3 us  [the longest x1 8.8 us: on_device(): pl.pallas_call(functools.partial(main_kernel, float(channels * lax.axis_s...]
    ppermute x5 -> x7, waiting for transfers between devices: 0.01 us -> 8.96 us  [the longest x5 8.95 us: swapped(): return lax.ppermute(value, axis, [(i, i ^ distance) for i in range(count)])]
    reduce_sum x9 -> x0, other arithmetic: 7.12 us -> none  [the longest x6 5.59 us: short_grads(): jnp.sum(cotangent * extended[begin:begin + row_count].astype(jnp.float32)...]
    dot_general x3 -> x0, matrix products: 5.8 us -> none  [the longest x1 1.98 us: on_device(): jnp.einsum('npgc,nrgc->gpr', dm_four, z_win, preferred_element_type=jnp.f...]
  transfers between devices with their start and end apart: 6 -> 7, of which waited for: 1 -> 4; matrix products, arithmetic and copies ran while one was open for 33% -> 3% of each run, Pallas kernels for 0% -> 8%
where the time goes in v1:
time: 47.4 us; the launch traced here: 46.9 us
  Pallas kernels  16.3 us (34%)
  starting transfers between devices  14.3 us (30%)
  waiting for transfers between devices  8.96 us (19%)
  local copies, waits for them, and re-layouts  5.82 us (12%)
  between operations  0.79 us (2%)
  other arithmetic  0.7 us (1%)
    ppermute x5, waiting for transfers between devices, swapped(): return lax.ppermute(value, axis, [(i, i ^ distance) for i in range(count)])  8.95 us
    pallas_call x1, Pallas kernels, on_device(): pl.pallas_call(functools.partial(main_kernel, float(channels * lax.axis_s...  8.8 us
    ppermute x5, starting transfers between devices, swapped(): return lax.ppermute(value, axis, [(i, i ^ distance) for i in range(count)])  7.45 us
    ppermute x2, starting transfers between devices, moved_up(): lax.ppermute(value, axis, [(i, i + steps) for i in range(count - steps)])  6.89 us
    unnamed x25, local copies, waits for them, and re-layouts  4.29 us
    pallas_call x1, Pallas kernels, on_device(): pl.pallas_call(band_kernel, out_shape=(jax.ShapeDtypeStruct((tiles, stack...  3.62 us
    pallas_call x1, Pallas kernels, on_device(): pl.pallas_call(pack_kernel, out_shape=(jax.ShapeDtypeStruct((2 * rows + T...  2.17 us
    pallas_call x1, Pallas kernels, on_device(): pl.pallas_call(functools.partial(last_kernel, 1.0 / rows), out_shape=(jax...  1.69 us
  transfers between devices with their start and end apart: 7, of which 4 were waited for; matrix products, arithmetic and copies ran while one was open for 3% of the time, Pallas kernels for 8%

profile of v1, /device:TPU:0, one launch (start us, length us, event | category | flops | bytes accessed | tf_op | source)
XLA Modules:
  0.0 46.9 jit_solution(4849866707837190611)
XLA Ops:
  0.7 2.2 %pack.1 = (bf16[272,1024]{1,0:T(8,128)(2,1)}, bf16[32,1024]{1,0:T(8,128)(2,1)}, f32[1,128]{1,0:T(1,128)}) custom-call(bf16[128,1024]{1,0:T(8,128)(2,1)} %q_ref.3, bf16[128,1024]{1,0:T(8,128)(2,1)} %k_ref.3, bf16[128,1024]{1,0:T(8,128)(2,1)} %v_ref.3, bf16[128,1024]{1,0:T(8,128)(2,1)} %up_ref.3), custom_call_target="tpu_custom_call" | custom-call | tf_op jit(solution)/shard_map/pack/pallas_call | solution.py:304
  2.9 2.5 %collective-permute-start = (bf16[272,1024]{1,0:T(8,128)(2,1)}, bf16[272,1024]{1,0:T(8,128)(2,1)S(1)}, u32[]{:S(2)}, u32[]{:S(2)}) collective-permute-start(bf16[272,1024]{1,0:T(8,128)(2,1)} %get-tuple-element.7), channel_id=1, source_target_pairs={{0,4},{4,8},{8,12},{12,16},{16,20},{20,24},{24,28},{1,5},{5,9},{9,... | collective-permute-start | bytes 1671176 | tf_op jit(solution)/shard_map/ppermute | solution.py:290
  5.4 4.4 %collective-permute-start.1 = (bf16[32,1024]{1,0:T(8,128)(2,1)}, bf16[32,1024]{1,0:T(8,128)(2,1)S(1)}, u32[]{:S(2)}, u32[]{:S(2)}) collective-permute-start(bf16[32,1024]{1,0:T(8,128)(2,1)} %get-tuple-element.8), channel_id=1, source_target_pairs={{0,8},{4,12},{8,16},{12,20},{16,24},{20,28},{1,9},{5,13},{9,17},{1... | collective-permute-start | bytes 196616 | tf_op jit(solution)/shard_map/ppermute | solution.py:290
  9.8 1.6 %collective-permute-start.2 = (f32[1,128]{1,0:T(1,128)}, f32[1,128]{1,0:T(1,128)S(1)}, u32[]{:S(2)}, u32[]{:S(2)}) collective-permute-start(f32[1,128]{1,0:T(1,128)} %get-tuple-element.9), channel_id=1, source_target_pairs={{0,1},{1,0},{2,3},{3,2},{4,5},{5,4},{6,7},{7,6},{8,9},{9,8},{10,11... | collective-permute-start | bytes 1544 | tf_op jit(solution)/shard_map/ppermute | solution.py:274
  11.4 2.1 %collective-permute-done.2 = f32[1,128]{1,0:T(1,128)S(1)} collective-permute-done((f32[1,128]{1,0:T(1,128)}, f32[1,128]{1,0:T(1,128)S(1)}, u32[]{:S(2)}, u32[]{:S(2)}) %collective-permute-start.2) | collective-permute-done | bytes 544 | tf_op jit(solution)/shard_map/ppermute | solution.py:274
  13.5 0.7 %add.12 = f32[1,128]{1,0:T(1,128)S(1)} add(f32[1,128]{1,0:T(1,128)} %get-tuple-element.9, f32[1,128]{1,0:T(1,128)S(1)} %collective-permute-done.2) | non-fusion elementwise | flops 128 | bytes 1536 | tf_op jit(solution)/shard_map/add | solution.py:283
  14.2 2.6 %collective-permute-start.3 = (f32[1,128]{1,0:T(1,128)S(1)}, f32[1,128]{1,0:T(1,128)S(1)}, u32[]{:S(2)}, u32[]{:S(2)}) collective-permute-start(f32[1,128]{1,0:T(1,128)S(1)} %add.12), channel_id=1, source_target_pairs={{0,2},{1,3},{2,0},{3,1},{4,6},{5,7},{6,4},{7,5},{8,10},{9,11},{10,... | collective-permute-start | bytes 1544 | tf_op jit(solution)/shard_map/ppermute | solution.py:274
  16.7 0.7 %copy.10.h_ref = bf16[128,64]{1,0:T(8,128)(2,1)} copy(bf16[128,64]{0,1:T(8,128)(2,1)S(1)} %copy-done.11) | data formatting | bytes 32768 | tf_op args[7]
  17.5 3.6 %band.1 = (bf16[8,256,256]{2,1,0:T(8,128)(2,1)}, bf16[8,160,256]{2,1,0:T(8,128)(2,1)}) custom-call(bf16[128,64]{1,0:T(8,128)(2,1)} %copy.10.h_ref), custom_call_target="tpu_custom_call" | custom-call | tf_op jit(solution)/shard_map/band/pallas_call | solution.py:319
  21.1 0.0 copy-start.7
  21.2 0.6 %copy-done.7 = s32[4]{0:T(128)S(1)} copy-done((s32[4]{0:T(128)S(1)}, s32[4]{0:T(128)}, u32[]{:S(2)}) %copy-start.7) | copy-done | bytes 40
  21.8 0.0 copy-done.8
  21.8 1.2 %copy-done = bf16[8,256,256]{2,1,0:T(8,128)(2,1)S(1)} copy-done((bf16[8,256,256]{2,1,0:T(8,128)(2,1)S(1)}, bf16[8,256,256]{2,1,0:T(8,128)(2,1)}, u32[]{:S(2)}) %copy-start) | copy-done | bytes 1048600
  23.0 1.1 %copy-done.5 = bf16[8,160,256]{2,1,0:T(8,128)(2,1)S(1)} copy-done((bf16[8,160,256]{2,1,0:T(8,128)(2,1)S(1)}, bf16[8,160,256]{2,1,0:T(8,128)(2,1)}, u32[]{:S(2)}) %copy-start.5) | copy-done | bytes 655384
  24.1 8.8 %main.1 = f32[32,1024]{1,0:T(8,128)S(1)} custom-call(s32[4]{0:T(128)S(1)} %copy-done.7, bf16[128,1024]{1,0:T(8,128)(2,1)S(1)} %copy-done.1, bf16[128,1024]{1,0:T(8,128)(2,1)S(1)} %copy-done.2, bf16[128,1024]{1,0:T(8,128)(2,1)S(1)} %copy-done.3, bf16[128,1024]{1,0:T(8,128)(2,1)S(1)} %copy-done.4, bf16[272,1024]{1,0:T(8,128)(2,1)S(1)} %collective-permute-done.near_ref, ...), custom_call_target="tpu_custom_call" | custom-call | tf_op jit(solution)/shard_map/main/pallas_call | solution.py:331
  32.9 0.1 collective-permute-start.4
  33.0 1.3 %collective-permute-done.4 = f32[32,1024]{1,0:T(8,128)S(1)} collective-permute-done((f32[32,1024]{1,0:T(8,128)S(1)}, f32[32,1024]{1,0:T(8,128)S(1)}, u32[]{:S(2)}, u32[]{:S(2)}) %collective-permute-start.4) | collective-permute-done | bytes 131104 | tf_op jit(solution)/shard_map/ppermute | solution.py:274
  34.3 1.6 %collective-permute-start.5 = (bf16[32,1024]{1,0:T(8,128)(2,1)S(1)}, bf16[32,1024]{1,0:T(8,128)(2,1)S(1)}, u32[]{:S(2)}, u32[]{:S(2)}) collective-permute-start(bf16[32,1024]{1,0:T(8,128)(2,1)S(1)} %add_convert_fusion.1), channel_id=1, source_target_pairs={{0,8},{4,12},{8,0},{12,4},{16,24},{20,28},{24,16},{28,20},{1,9},{5... | collective-permute-start | bytes 196616 | tf_op jit(solution)/shard_map/ppermute | solution.py:274
  35.9 2.8 %collective-permute-done.5 = bf16[32,1024]{1,0:T(8,128)(2,1)S(1)} collective-permute-done((bf16[32,1024]{1,0:T(8,128)(2,1)S(1)}, bf16[32,1024]{1,0:T(8,128)(2,1)S(1)}, u32[]{:S(2)}, u32[]{:S(2)}) %collective-permute-start.5) | collective-permute-done | bytes 65568 | tf_op jit(solution)/shard_map/ppermute | solution.py:274
  38.7 1.6 %collective-permute-start.6 = (bf16[32,1024]{1,0:T(8,128)(2,1)S(1)}, bf16[32,1024]{1,0:T(8,128)(2,1)S(1)}, u32[]{:S(2)}, u32[]{:S(2)}) collective-permute-start(bf16[32,1024]{1,0:T(8,128)(2,1)S(1)} %add_convert_fusion.a_ref), channel_id=1, source_target_pairs={{0,16},{4,20},{8,24},{12,28},{16,0},{20,4},{24,8},{28,12},{1,17},{... | collective-permute-start | bytes 196616 | tf_op jit(solution)/shard_map/ppermute | solution.py:274
  40.3 2.7 %collective-permute-done.6.b_ref = bf16[32,1024]{1,0:T(8,128)(2,1)S(1)} collective-permute-done((bf16[32,1024]{1,0:T(8,128)(2,1)S(1)}, bf16[32,1024]{1,0:T(8,128)(2,1)S(1)}, u32[]{:S(2)}, u32[]{:S(2)}) %collective-permute-start.6) | collective-permute-done | bytes 65568 | tf_op jit(solution)/shard_map/ppermute | solution.py:274
  43.0 0.6 %copy-done.10 = bf16[32,1024]{1,0:T(8,128)(2,1)} copy-done((bf16[32,1024]{1,0:T(8,128)(2,1)}, bf16[32,1024]{1,0:T(8,128)(2,1)S(1)}, u32[]{:S(2)}) %copy-start.10) | copy-done | bytes 65560
  43.7 1.7 %last.1 = (f32[3,7,1024]{2,1,0:T(8,128)}, f32[128,64]{1,0:T(8,128)}) custom-call(bf16[32,1024]{1,0:T(8,128)(2,1)} %copy-done.9, bf16[32,1024]{1,0:T(8,128)(2,1)} %copy-done.10), custom_call_target="tpu_custom_call" | custom-call | tf_op jit(solution)/shard_map/last/pallas_call | solution.py:377
  45.4 1.5 %copy.11 = f32[128,64]{0,1:T(8,128)} copy(f32[128,64]{1,0:T(8,128)} %get-tuple-element.13) | data formatting | bytes 65536 | tf_op jit(solution)/shard_map/last/pallas_call | solution.py:377
  (24 shorter events, 0.1 us)
Async XLA Ops:
  0.6 16.1 %copy-start.11 = (bf16[128,64]{0,1:T(8,128)(2,1)S(1)}, bf16[128,64]{0,1:T(8,128)(2,1)}, u32[]{:S(2)}) copy-start(bf16[128,64]{0,1:T(8,128)(2,1)} %param.15) | copy-start | bytes 49156
  0.6 20.5 %copy-start.1 = (bf16[128,1024]{1,0:T(8,128)(2,1)S(1)}, bf16[128,1024]{1,0:T(8,128)(2,1)}, u32[]{:S(2)}) copy-start(bf16[128,1024]{1,0:T(8,128)(2,1)} %q_ref.3) | copy-start | bytes 786436
  0.7 20.5 %copy-start.2 = (bf16[128,1024]{1,0:T(8,128)(2,1)S(1)}, bf16[128,1024]{1,0:T(8,128)(2,1)}, u32[]{:S(2)}) copy-start(bf16[128,1024]{1,0:T(8,128)(2,1)} %k_ref.3) | copy-start | bytes 786436
  0.7 20.5 %copy-start.3 = (bf16[128,1024]{1,0:T(8,128)(2,1)S(1)}, bf16[128,1024]{1,0:T(8,128)(2,1)}, u32[]{:S(2)}) copy-start(bf16[128,1024]{1,0:T(8,128)(2,1)} %v_ref.3) | copy-start | bytes 786436
  0.7 20.5 %copy-start.4 = (bf16[128,1024]{1,0:T(8,128)(2,1)S(1)}, bf16[128,1024]{1,0:T(8,128)(2,1)}, u32[]{:S(2)}) copy-start(bf16[128,1024]{1,0:T(8,128)(2,1)} %up_ref.3) | copy-start | bytes 786436
  2.9 18.3 %copy-start.6 = (bf16[3,7,1024]{2,1,0:T(8,128)(2,1)S(1)}, bf16[3,7,1024]{2,1,0:T(8,128)(2,1)}, u32[]{:S(2)}) copy-start(bf16[3,7,1024]{2,1,0:T(8,128)(2,1)} %se_ref.1) | copy-start | bytes 129028
  2.9 18.3 %collective-permute-start = (bf16[272,1024]{1,0:T(8,128)(2,1)}, bf16[272,1024]{1,0:T(8,128)(2,1)S(1)}, u32[]{:S(2)}, u32[]{:S(2)}) collective-permute-start(bf16[272,1024]{1,0:T(8,128)(2,1)} %get-tuple-element.7), channel_id=1, source_target_pairs={{0,4},{4,8},{8,12},{12,16},{16,20},{20,24},{24,28},{1,5},{5,9},{9,... | collective-permute-start | bytes 1671176 | tf_op jit(solution)/shard_map/ppermute | solution.py:290
  5.4 15.7 %collective-permute-start.1 = (bf16[32,1024]{1,0:T(8,128)(2,1)}, bf16[32,1024]{1,0:T(8,128)(2,1)S(1)}, u32[]{:S(2)}, u32[]{:S(2)}) collective-permute-start(bf16[32,1024]{1,0:T(8,128)(2,1)} %get-tuple-element.8), channel_id=1, source_target_pairs={{0,8},{4,12},{8,16},{12,20},{16,24},{20,28},{1,9},{5,13},{9,17},{1... | collective-permute-start | bytes 196616 | tf_op jit(solution)/shard_map/ppermute | solution.py:290
  9.8 3.7 %collective-permute-start.2 = (f32[1,128]{1,0:T(1,128)}, f32[1,128]{1,0:T(1,128)S(1)}, u32[]{:S(2)}, u32[]{:S(2)}) collective-permute-start(f32[1,128]{1,0:T(1,128)} %get-tuple-element.9), channel_id=1, source_target_pairs={{0,1},{1,0},{2,3},{3,2},{4,5},{5,4},{6,7},{7,6},{8,9},{9,8},{10,11... | collective-permute-start | bytes 1544 | tf_op jit(solution)/shard_map/ppermute | solution.py:274
  14.2 6.9 %collective-permute-start.3 = (f32[1,128]{1,0:T(1,128)S(1)}, f32[1,128]{1,0:T(1,128)S(1)}, u32[]{:S(2)}, u32[]{:S(2)}) collective-permute-start(f32[1,128]{1,0:T(1,128)S(1)} %add.12), channel_id=1, source_target_pairs={{0,2},{1,3},{2,0},{3,1},{4,6},{5,7},{6,4},{7,5},{8,10},{9,11},{10,... | collective-permute-start | bytes 1544 | tf_op jit(solution)/shard_map/ppermute | solution.py:274
  21.1 0.7 %copy-start.7 = (s32[4]{0:T(128)S(1)}, s32[4]{0:T(128)}, u32[]{:S(2)}) copy-start(s32[4]{0:T(128)} %lengths_ref.1) | copy-start | bytes 52
  21.1 0.7 %copy-start.8 = (s32[128]{0:T(128)S(1)}, s32[128]{0:T(128)}, u32[]{:S(2)}) copy-start(s32[128]{0:T(128)} %param.12) | copy-start | bytes 1540
  21.8 1.2 %copy-start = (bf16[8,256,256]{2,1,0:T(8,128)(2,1)S(1)}, bf16[8,256,256]{2,1,0:T(8,128)(2,1)}, u32[]{:S(2)}) copy-start(bf16[8,256,256]{2,1,0:T(8,128)(2,1)} %get-tuple-element.10.band_ref) | copy-start | bytes 3145732
  23.0 1.1 %copy-start.5 = (bf16[8,160,256]{2,1,0:T(8,128)(2,1)S(1)}, bf16[8,160,256]{2,1,0:T(8,128)(2,1)}, u32[]{:S(2)}) copy-start(bf16[8,160,256]{2,1,0:T(8,128)(2,1)} %get-tuple-element.11.band_t_ref) | copy-start | bytes 1966084
  32.9 1.4 %collective-permute-start.4 = (f32[32,1024]{1,0:T(8,128)S(1)}, f32[32,1024]{1,0:T(8,128)S(1)}, u32[]{:S(2)}, u32[]{:S(2)}) collective-permute-start(f32[32,1024]{1,0:T(8,128)S(1)} %main.1), channel_id=1, source_target_pairs={{0,4},{4,0},{8,12},{12,8},{16,20},{20,16},{24,28},{28,24},{1,5},{5... | collective-permute-start | bytes 393224 | tf_op jit(solution)/shard_map/ppermute | solution.py:274
  34.3 4.3 %collective-permute-start.5 = (bf16[32,1024]{1,0:T(8,128)(2,1)S(1)}, bf16[32,1024]{1,0:T(8,128)(2,1)S(1)}, u32[]{:S(2)}, u32[]{:S(2)}) collective-permute-start(bf16[32,1024]{1,0:T(8,128)(2,1)S(1)} %add_convert_fusion.1), channel_id=1, source_target_pairs={{0,8},{4,12},{8,0},{12,4},{16,24},{20,28},{24,16},{28,20},{1,9},{5... | collective-permute-start | bytes 196616 | tf_op jit(solution)/shard_map/ppermute | solution.py:274
  38.7 4.3 %copy-start.9 = (bf16[32,1024]{1,0:T(8,128)(2,1)}, bf16[32,1024]{1,0:T(8,128)(2,1)S(1)}, u32[]{:S(2)}) copy-start(bf16[32,1024]{1,0:T(8,128)(2,1)S(1)} %add_convert_fusion.a_ref) | copy-start | bytes 196612
  38.7 4.3 %collective-permute-start.6 = (bf16[32,1024]{1,0:T(8,128)(2,1)S(1)}, bf16[32,1024]{1,0:T(8,128)(2,1)S(1)}, u32[]{:S(2)}, u32[]{:S(2)}) collective-permute-start(bf16[32,1024]{1,0:T(8,128)(2,1)S(1)} %add_convert_fusion.a_ref), channel_id=1, source_target_pairs={{0,16},{4,20},{8,24},{12,28},{16,0},{20,4},{24,8},{28,12},{1,17},{... | collective-permute-start | bytes 196616 | tf_op jit(solution)/shard_map/ppermute | solution.py:274
  43.0 0.6 %copy-start.10 = (bf16[32,1024]{1,0:T(8,128)(2,1)}, bf16[32,1024]{1,0:T(8,128)(2,1)S(1)}, u32[]{:S(2)}) copy-start(bf16[32,1024]{1,0:T(8,128)(2,1)S(1)} %collective-permute-done.6.b_ref) | copy-start | bytes 196612

commit v2 on v1

v2 whole, which is shorter than its diff:
```python
import functools

import jax
import jax.numpy as jnp
from jax import lax
from jax.experimental import pallas as pl
from jax.experimental.pallas import tpu as pltpu
from jax.sharding import PartitionSpec as P

BLOCK = 32
LANES = 128
TAIL = 16
PRE = 8
SLOT = PRE + BLOCK
LIMIT = 24 * 1024 * 1024
MOST = 60 * 1024 * 1024
F32 = jnp.float32
BF16 = jnp.bfloat16


def spec(space=pltpu.VMEM):
    return pl.BlockSpec(memory_space=space)


def dot(a, b, contract, precision=None):
    return lax.dot_general(
        a, b, ((contract[0], contract[1]), ((), ())), precision=precision, preferred_element_type=F32
    )


def doc_of(lengths_ref, block):
    count = jnp.int32(0)
    end = jnp.int32(0)
    for i in range(lengths_ref.shape[0]):
        end = end + lengths_ref[i]
        count = count + jnp.where(block >= end, 1, 0)
    return jnp.where(block >= 0, count, -1)


def first_kernel(
    span,
    lengths_ref,
    reward_ref,
    q_ref,
    k_ref,
    v_ref,
    up_ref,
    near_ref,
    far_ref,
    sq_ref,
    note_ref,
    up_here,
    near_here,
    sems,
):
    rows, channels = k_ref.shape
    tail = pl.ds(rows - TAIL, TAIL)
    k_rows, v_rows, q_rows = pl.ds(0, rows), pl.ds(rows, rows), pl.ds(2 * rows, TAIL)
    coming = [
        pltpu.make_async_copy(source, target, sems.at[i])
        for i, (source, target) in enumerate(
            (
                (k_ref, near_here.at[k_rows]),
                (v_ref, near_here.at[v_rows]),
                (q_ref.at[tail], near_here.at[q_rows]),
                (up_ref, up_here),
            )
        )
    ]
    going = [
        pltpu.make_async_copy(source, target, sems.at[4 + i])
        for i, (source, target) in enumerate(
            (
                (near_here, near_ref),
                (near_here.at[pl.ds(rows - TAIL, TAIL)], far_ref.at[pl.ds(0, TAIL)]),
                (near_here.at[pl.ds(2 * rows - TAIL, TAIL)], far_ref.at[pl.ds(TAIL, TAIL)]),
            )
        )
    ]
    for copy in coming:
        copy.start()
    own = rows // BLOCK
    window = span + own
    first = lax.axis_index("dp") * own
    docs = [doc_of(lengths_ref, first + b) for b in range(-span - 1, own)]
    notes = [(docs[b + 1] == docs[b]) & (docs[b] >= 0) for b in range(window)]
    docs = docs[1:]
    notes = notes + [docs[n + s] == docs[n + span] for n in range(own) for s in range(span)]
    for i, note in enumerate(notes):
        note_ref[i : i + 1] = jnp.full((1, rows), jnp.where(note, 1.0, 0.0).astype(F32))
    note_ref[len(notes) : len(notes) + 1] = reward_ref[...].astype(F32) * 0.25
    for copy in coming[0:3]:
        copy.wait()
    for copy in going:
        copy.start()
    coming[3].wait()
    total = jnp.zeros((rows, LANES), F32)
    for tile in range(channels // LANES):
        part = up_here[:, tile * LANES : (tile + 1) * LANES].astype(F32)
        total = total + part * part
    sq_ref[...] = jnp.sum(total.T, axis=0, keepdims=True)
    for copy in going:
        copy.wait()


def band_kernel(h_ref, band_ref, band_t_ref, row_ref):
    groups, taps = h_ref.shape
    tiles = band_ref.shape[0]
    per_tile = groups // tiles
    width = band_ref.shape[2]
    tap = lax.broadcasted_iota(jnp.int32, (taps, width), 0)
    lane = lax.broadcasted_iota(jnp.int32, (taps, width), 1)
    flip = jnp.where(tap + lane == taps, 1.0, 0.0).astype(F32)
    row_ref[...] = dot(h_ref[...], flip.astype(BF16), ((1,), (0,)))

    def one(tile, carry):
        rows = row_ref[pl.ds(pl.multiple_of(tile * per_tile, per_tile), per_tile), :]
        parts = [
            pltpu.roll(
                jnp.broadcast_to(rows[g : g + 1], (BLOCK, width)), 0, 1, stride=1, stride_axis=0
            )
            for g in range(per_tile)
        ]
        band = jnp.concatenate(parts, axis=0)
        band_ref[tile] = band.astype(BF16)
        band_t_ref[tile] = band.T[0 : taps + BLOCK].astype(BF16)
        return carry

    lax.fori_loop(0, tiles, one, 0)


def main_kernel(
    all_channels,
    q_ref,
    k_ref,
    v_ref,
    up_ref,
    near_ref,
    far_ref,
    sq_ref,
    note_ref,
    se_ref,
    band_ref,
    band_t_ref,
    out_ref,
    xq_ref,
    xk_ref,
    xv_ref,
    ks_ref,
    vs_ref,
    z_ref,
    zw_ref,
    dm_ref,
    dz_ref,
    cot_ref,
    skew_ref,
    w_ref,
):
    rows, channels = q_ref.shape
    own = rows // BLOCK
    taps = band_t_ref.shape[1] - BLOCK
    span = taps // BLOCK
    window = span + own
    tiles = channels // LANES
    per_tile = band_ref.shape[1] // BLOCK
    width = LANES // per_tile
    tap_count = se_ref.shape[1]

    joined = [note_ref[b : b + 1, 0:LANES] for b in range(window)]
    same = [
        [note_ref[window + n * span + s : window + n * span + s + 1, 0:LANES] for s in range(span)]
        for n in range(own)
    ]
    reward_row = window + own * span
    weight = note_ref[reward_row : reward_row + 1] * lax.rsqrt(sq_ref[...] / all_channels + 1e-06)
    w_ref[...] = jnp.broadcast_to(weight, (LANES, rows)).T

    lane_group = lax.broadcasted_iota(jnp.int32, (BLOCK, LANES), 1) // width
    picks = [lane_group == g for g in range(per_tile)]
    masks = [jnp.where(pick, 1.0, 0.0).astype(BF16) for pick in picks]
    beside = z_ref.shape[0]
    for side in range(beside):
        z_ref[side, window * BLOCK :] = jnp.zeros((z_ref.shape[1] - window * BLOCK, LANES), BF16)

    def fill(x_ref, side, pieces, before, first_block):
        for b, piece in enumerate(pieces):
            at = SLOT * b
            x_ref[side, at : at + PRE] = before * joined[first_block + b]
            x_ref[side, at + PRE : at + SLOT] = piece
            before = piece[BLOCK - PRE :]

    def shifted(x_ref, side, b, j):
        at = SLOT * b + PRE - j
        return x_ref[side, at : at + BLOCK, :]

    def short(x_ref, side, b, taps_now):
        total = taps_now[0:1] * shifted(x_ref, side, b, 0)
        for j in range(1, tap_count):
            total = total + taps_now[j : j + 1] * shifted(x_ref, side, b, j)
        return total

    def fold(x):
        return jnp.sum(x.reshape(BLOCK // 8, 8, LANES), axis=0)

    def first_half(tile, side):
        at = pl.ds(pl.multiple_of(tile * LANES, LANES), LANES)
        q_taps = se_ref[0, :, at].astype(F32)
        k_taps = se_ref[1, :, at].astype(F32)
        v_taps = se_ref[2, :, at].astype(F32)

        def blocks_of(ref, start, count):
            return [
                ref[start + BLOCK * b : start + BLOCK * (b + 1), at].astype(F32) for b in range(count)
            ]

        q_before = near_ref[2 * rows : 2 * rows + TAIL, at].astype(F32)[TAIL - PRE :]
        k_before = far_ref[0:TAIL, at].astype(F32)[TAIL - PRE :]
        v_before = far_ref[TAIL : 2 * TAIL, at].astype(F32)[TAIL - PRE :]
        k_halo = blocks_of(near_ref, rows - span * BLOCK, span)
        v_halo = blocks_of(near_ref, 2 * rows - span * BLOCK, span)
        fill(xk_ref, side, k_halo + blocks_of(k_ref, 0, own), k_before, 0)
        fill(xv_ref, side, v_halo + blocks_of(v_ref, 0, own), v_before, 0)
        fill(xq_ref, side, blocks_of(q_ref, 0, own), q_before, span)
        for b in range(window):
            at_b = slice(BLOCK * b, BLOCK * (b + 1))
            ks = short(xk_ref, side, b, k_taps)
            vs = short(xv_ref, side, b, v_taps)
            ks_ref[side, at_b] = ks
            vs_ref[side, at_b] = vs
            z_ref[side, at_b] = (ks * vs).astype(BF16)
        for n in range(own):
            at_n = slice(BLOCK * n, BLOCK * (n + 1))
            cot = w_ref[at_n] * up_ref[at_n, at].astype(F32)
            cot_ref[side, at_n] = cot
            dm = (cot * short(xq_ref, side, n, q_taps)).astype(BF16)
            lanes = slice(LANES * (n % 2), LANES * (n % 2 + 1))
            for g in range(per_tile):
                dm_ref[side, n // 2, BLOCK * g : BLOCK * (g + 1), lanes] = dm * masks[g]
            for s in range(2 * LANES // BLOCK):
                piece = z_ref[side, BLOCK * (n + s) : BLOCK * (n + s + 1)]
                if s < span:
                    piece = piece * same[n][s].astype(BF16)
                zw_ref[side, n // 2, BLOCK * s : BLOCK * (s + 1), lanes] = piece

    def middle(tile, side):
        band = band_ref[tile]
        band_t = band_t_ref[tile]
        pair = None
        gq = [jnp.zeros((8, LANES), F32) for _ in range(tap_count)]
        for half in range(own // 2):
            dms = dm_ref[side, half]
            zws = zw_ref[side, half]
            wide = dot(band, zws, ((1,), (0,)))
            back = dot(band_t, dms, ((1,), (0,)))
            both = dot(dms, zws, ((1,), (1,)))
            pair = both if pair is None else pair + both
            for part in range(2):
                n = 2 * half + part
                lanes = slice(LANES * part, LANES * (part + 1))
                m = wide[0:BLOCK, lanes]
                for g in range(1, per_tile):
                    m = jnp.where(picks[g], wide[BLOCK * g : BLOCK * (g + 1), lanes], m)
                cot_q = cot_ref[side, BLOCK * n : BLOCK * (n + 1)] * m
                for j in range(tap_count):
                    gq[j] = gq[j] + fold(cot_q * shifted(xq_ref, side, n, j))
                for s in range(span + 1):
                    at_s = slice(BLOCK * (n + s), BLOCK * (n + s + 1))
                    term = back[BLOCK * s : BLOCK * (s + 1), lanes]
                    if s < span:
                        term = term * same[n][s]
                    if n == 0 or s == span:
                        dz_ref[side, at_s] = term
                    else:
                        dz_ref[side, at_s] += term
        lined = pair.reshape(per_tile, BLOCK // 8, 8, 2 * LANES)
        skew = None
        for r in range(BLOCK // 8):
            rows_r = lined[:, r].reshape(per_tile * 8, 2 * LANES)
            moved = pltpu.roll(rows_r, 2 * LANES - 1 - 8 * r, 1)
            skew = moved if skew is None else skew + moved
        skew_ref[tile] = skew
        return gq

    def last_half(tile, side, gq):
        at = pl.ds(pl.multiple_of(tile * LANES, LANES), LANES)
        gk = [jnp.zeros((8, LANES), F32) for _ in range(tap_count)]
        gv = [jnp.zeros((8, LANES), F32) for _ in range(tap_count)]
        for b in range(window):
            at_b = slice(BLOCK * b, BLOCK * (b + 1))
            dz = dz_ref[side, at_b]
            cot_k = dz * vs_ref[side, at_b]
            cot_v = dz * ks_ref[side, at_b]
            for j in range(tap_count):
                gk[j] = gk[j] + fold(cot_k * shifted(xk_ref, side, b, j))
                gv[j] = gv[j] + fold(cot_v * shifted(xv_ref, side, b, j))
        for i, sums in enumerate((gq, gk, gv)):
            for j in range(tap_count):
                out_ref[8 * i + j : 8 * i + j + 1, at] = jnp.sum(sums[j], axis=0, keepdims=True)
            out_ref[8 * i + tap_count : 8 * i + 8, at] = jnp.zeros((8 - tap_count, LANES), F32)

    def some(step, carry):
        now = [step * beside + side for side in range(beside)]
        for side, tile in enumerate(now):
            first_half(tile, side)
        sums = [middle(tile, side) for side, tile in enumerate(now)]
        for side, tile in enumerate(now):
            last_half(tile, side, sums[side])
        return carry

    lax.fori_loop(0, tiles // beside, some, 0)
    skew = skew_ref[...].reshape(tiles * per_tile * 8, 2 * LANES)
    row_index = lax.broadcasted_iota(jnp.int32, skew.shape, 0)
    for bit in range(3):
        moved = pltpu.roll(skew, 2 * LANES - (1 << bit), 1)
        skew = jnp.where((row_index >> bit) & 1 == 1, moved, skew)
    totals = jnp.sum(skew[:, 0:LANES].reshape(tiles * per_tile, 8, LANES), axis=1)
    for tile in range(tiles):
        out_ref[24 : 24 + per_tile, LANES * tile : LANES * (tile + 1)] = totals[
            per_tile * tile : per_tile * (tile + 1)
        ]


def last_kernel(scale, *refs):
    *part_refs, se_ref, mr_ref = refs
    parts = [ref[...].astype(F32) for ref in part_refs]
    while len(parts) > 1:
        parts = [a + b for a, b in zip(parts[::2], parts[1::2])]
    total = parts[0] * scale
    tap_count = se_ref.shape[1]
    channels = total.shape[1]
    for i in range(3):
        se_ref[i] = total[8 * i : 8 * i + tap_count]
    flat = jnp.concatenate(
        [total[24:, t * LANES : (t + 1) * LANES] for t in range(channels // LANES)], axis=0
    )
    tap = lax.broadcasted_iota(jnp.int32, (LANES, LANES), 0)
    lane = lax.broadcasted_iota(jnp.int32, (LANES, LANES), 1)
    flip = jnp.where(tap + lane == LANES - 1, 1.0, 0.0).astype(F32)
    mr_ref[...] = dot(flat, flip, ((1,), (0,)), lax.Precision.HIGHEST)


def swapped(value, axis, distance):
    count = lax.axis_size(axis)
    return lax.ppermute(value, axis, [(i, i ^ distance) for i in range(count)])


def summed_small(value, axis):
    count = lax.axis_size(axis)
    if count & (count - 1):
        return lax.psum(value, axis)
    distance = 1
    while distance < count:
        value = value + swapped(value, axis, distance)
        distance *= 2
    return value


def spread(part, axis):
    count = lax.axis_size(axis)
    if count & (count - 1) or count < 8:
        return [lax.psum(part, axis)]
    mine = (part + swapped(part, axis, 1)).astype(BF16)
    distance = 8
    while distance < count:
        mine = (mine.astype(F32) + swapped(mine, axis, distance).astype(F32)).astype(BF16)
        distance *= 2
    return [mine] + [swapped(mine, axis, d) for d in (2, 4, 6)]


def moved_up(value, axis, steps):
    count = lax.axis_size(axis)
    return lax.ppermute(value, axis, [(i, (i + steps) % count) for i in range(count)])


def on_device(query, key, value, upstream, reward, lengths, se_filter, mr_filter):
    rows, channels = query.shape
    taps, groups = mr_filter.shape
    tap_count = se_filter.shape[1]
    tiles = channels // LANES
    per_tile = groups // tiles
    stack = per_tile * BLOCK
    own = rows // BLOCK
    window = own + taps // BLOCK
    beside = 2 if tiles % 2 == 0 else 1
    dp = lax.axis_size("dp")

    near, far, sq, notes = pl.pallas_call(
        functools.partial(first_kernel, taps // BLOCK),
        out_shape=(
            jax.ShapeDtypeStruct((2 * rows + TAIL, channels), BF16),
            jax.ShapeDtypeStruct((2 * TAIL, channels), BF16),
            jax.ShapeDtypeStruct((1, rows), F32),
            jax.ShapeDtypeStruct((window + own * (taps // BLOCK) + 1, rows), F32),
        ),
        in_specs=[spec(pltpu.SMEM), spec()] + [spec(pl.ANY)] * 4,
        out_specs=(spec(pl.ANY), spec(pl.ANY), spec(), spec()),
        scratch_shapes=[
            pltpu.VMEM((rows, channels), BF16),
            pltpu.VMEM((2 * rows + TAIL, channels), BF16),
            pltpu.SemaphoreType.DMA((7,)),
        ],
        compiler_params=pltpu.CompilerParams(vmem_limit_bytes=MOST),
        name="first",
    )(lengths, reward.reshape(1, rows), query, key, value, upstream)
    near = moved_up(near, "dp", 1)
    far = moved_up(far, "dp", 2)
    sq = summed_small(sq, "fsdp")

    band, band_t = pl.pallas_call(
        band_kernel,
        out_shape=(
            jax.ShapeDtypeStruct((tiles, stack, 2 * LANES), BF16),
            jax.ShapeDtypeStruct((tiles, taps + BLOCK, stack), BF16),
        ),
        in_specs=[spec()],
        out_specs=(spec(),) * 2,
        scratch_shapes=[pltpu.VMEM((groups, 2 * LANES), F32)],
        compiler_params=pltpu.CompilerParams(vmem_limit_bytes=LIMIT),
        name="band",
    )(mr_filter.T)

    part = pl.pallas_call(
        functools.partial(main_kernel, float(channels * lax.axis_size("fsdp"))),
        out_shape=jax.ShapeDtypeStruct((24 + per_tile, channels), F32),
        in_specs=[spec()] * 11,
        out_specs=spec(),
        scratch_shapes=[
            pltpu.VMEM((beside, own * SLOT, LANES), F32),
            pltpu.VMEM((beside, window * SLOT, LANES), F32),
            pltpu.VMEM((beside, window * SLOT, LANES), F32),
            pltpu.VMEM((beside, window * BLOCK, LANES), F32),
            pltpu.VMEM((beside, window * BLOCK, LANES), F32),
            pltpu.VMEM((beside, (own - 1) * BLOCK + 2 * LANES, LANES), BF16),
            pltpu.VMEM((beside, own // 2, 2 * LANES, 2 * LANES), BF16),
            pltpu.VMEM((beside, own // 2, stack, 2 * LANES), BF16),
            pltpu.VMEM((beside, window * BLOCK, LANES), F32),
            pltpu.VMEM((beside, rows, LANES), F32),
            pltpu.VMEM((tiles, per_tile * 8, 2 * LANES), F32),
            pltpu.VMEM((rows, LANES), F32),
        ],
        compiler_params=pltpu.CompilerParams(vmem_limit_bytes=LIMIT),
        name="main",
    )(
        query,
        key,
        value,
        upstream,
        near,
        far,
        sq,
        notes,
        se_filter,
        band,
        band_t,
    )

    parts = spread(part, "dp")
    grad_se, grad_mr = pl.pallas_call(
        functools.partial(last_kernel, 1.0 / rows),
        out_shape=(
            jax.ShapeDtypeStruct((3, tap_count, channels), F32),
            jax.ShapeDtypeStruct((groups, taps), F32),
        ),
        in_specs=[spec()] * len(parts),
        out_specs=(spec(),) * 2,
        compiler_params=pltpu.CompilerParams(vmem_limit_bytes=LIMIT),
        name="last",
    )(*parts)
    return grad_se, grad_mr.T


def solution(mesh):
    in_specs = (
        P("dp", "fsdp"),
        P("dp", "fsdp"),
        P("dp", "fsdp"),
        P("dp", "fsdp"),
        P("dp"),
        P(),
        P(None, None, "fsdp"),
        P(None, "fsdp"),
    )
    out_specs = (P(None, None, "fsdp"), P(None, "fsdp"))
    return jax.shard_map(
        on_device, mesh=mesh, in_specs=in_specs, out_specs=out_specs, check_vma=False
    )
```

time: 47.4 us -> 32.8 us (0.69)
  local copies, waits for them, and re-layouts: 5.82 us -> 0.82 us
  Pallas kernels: 16.3 us -> 12 us
  starting transfers between devices: 14.3 us -> 11 us
  waiting for transfers between devices: 8.96 us -> 7.28 us
    ppermute x2, starting transfers between devices: 6.89 us -> 3.06 us  [moved_up(): lax.ppermute(value, axis, [(i, (i + steps) % count) for i in range(count)])]
    unnamed x25 -> x14, local copies, waits for them, and re-layouts: 4.29 us -> 0.82 us
    pallas_call x1, Pallas kernels: 8.8 us -> 6.25 us  [on_device(): pl.pallas_call(functools.partial(main_kernel, float(channels * lax.axis_s...]
    pallas_call x1, Pallas kernels: 3.62 us -> 1.66 us  [on_device(): pl.pallas_call(band_kernel, out_shape=(jax.ShapeDtypeStruct((tiles, stack...]
    ppermute x5 -> x6, waiting for transfers between devices: 8.95 us -> 7.27 us  [swapped(): return lax.ppermute(value, axis, [(i, i ^ distance) for i in range(count)])]
    pallas_call x1 -> x0, local copies, waits for them, and re-layouts: 1.54 us -> none  [on_device(): pl.pallas_call(functools.partial(last_kernel, 1.0 / rows), out_shape=(jax...]
    pallas_call x1, Pallas kernels: 2.17 us -> 3.31 us  [on_device(): pl.pallas_call(functools.partial(first_kernel, taps // BLOCK), out_shape=...]
    pallas_call x1, Pallas kernels: 1.69 us -> 0.8 us  [on_device(): pl.pallas_call(functools.partial(last_kernel, 1.0 / rows), out_shape=(jax...]
  transfers between devices with their start and end apart: 7 -> 8, of which waited for: 4 -> 6; matrix products, arithmetic and copies ran while one was open for 3% -> 2% of each run, Pallas kernels for 8% -> 5%
where the time goes in v2:
time: 32.8 us; the launch traced here: 32.6 us
  Pallas kernels  12 us (37%)
  starting transfers between devices  11 us (34%)
  waiting for transfers between devices  7.28 us (22%)
  local copies, waits for them, and re-layouts  0.82 us (2%)
  between operations  0.77 us (2%)
  other arithmetic  0.64 us (2%)
    ppermute x6, starting transfers between devices, swapped(): return lax.ppermute(value, axis, [(i, i ^ distance) for i in range(count)])  7.98 us
    ppermute x6, waiting for transfers between devices, swapped(): return lax.ppermute(value, axis, [(i, i ^ distance) for i in range(count)])  7.27 us
    pallas_call x1, Pallas kernels, on_device(): pl.pallas_call(functools.partial(main_kernel, float(channels * lax.axis_s...  6.25 us
    pallas_call x1, Pallas kernels, on_device(): pl.pallas_call(functools.partial(first_kernel, taps // BLOCK), out_shape=...  3.31 us
    ppermute x2, starting transfers between devices, moved_up(): lax.ppermute(value, axis, [(i, (i + steps) % count) for i in range(count)])  3.06 us
    pallas_call x1, Pallas kernels, on_device(): pl.pallas_call(band_kernel, out_shape=(jax.ShapeDtypeStruct((tiles, stack...  1.66 us
    unnamed x14, local copies, waits for them, and re-layouts  0.82 us
    pallas_call x1, Pallas kernels, on_device(): pl.pallas_call(functools.partial(last_kernel, 1.0 / rows), out_shape=(jax...  0.8 us
  transfers between devices with their start and end apart: 8, of which 6 were waited for; matrix products, arithmetic and copies ran while one was open for 2% of the time, Pallas kernels for 5%

profile of v2, /device:TPU:0, one launch (start us, length us, event | category | flops | bytes accessed | tf_op | source)
XLA Modules:
  0.0 32.6 jit_solution(11772205065951241391)
XLA Ops:
  0.7 3.3 %first.1 = (bf16[272,1024]{1,0:T(8,128)(2,1)}, bf16[32,1024]{1,0:T(8,128)(2,1)}, f32[1,128]{1,0:T(1,128)}, f32[25,128]{1,0:T(8,128)}) custom-call(s32[4]{0:T(128)} %lengths_ref.1, s32[1,128]{1,0:T(1,128)} %bitcast.4, bf16[128,1024]{1,0:T(8,128)(2,1)} %q_ref.3, bf16[128,1024]{1,0:T(8,128)(2,1)} %k_ref.3, bf16[128,1024]{1,0:T(8,128)(2,1)} %v_ref.3, ...), custom_call_target="tpu_custom_call" | custom-call | tf_op jit(solution)/shard_map/first/pallas_call | solution.py:387
  4.0 0.0 copy-start.5
  4.0 0.5 %collective-permute-start = (bf16[272,1024]{1,0:T(8,128)(2,1)}, bf16[272,1024]{1,0:T(8,128)(2,1)S(1)}, u32[]{:S(2)}, u32[]{:S(2)}) collective-permute-start(bf16[272,1024]{1,0:T(8,128)(2,1)} %get-tuple-element.10), channel_id=1, source_target_pairs={{0,4},{4,8},{8,12},{12,16},{16,20},{20,24},{24,28},{28,0},{1,5},{5... | collective-permute-start | bytes 1671176 | tf_op jit(solution)/shard_map/ppermute | solution.py:372
  4.5 2.6 %collective-permute-start.1 = (bf16[32,1024]{1,0:T(8,128)(2,1)}, bf16[32,1024]{1,0:T(8,128)(2,1)S(1)}, u32[]{:S(2)}, u32[]{:S(2)}) collective-permute-start(bf16[32,1024]{1,0:T(8,128)(2,1)} %get-tuple-element.11), channel_id=1, source_target_pairs={{0,8},{4,12},{8,16},{12,20},{16,24},{20,28},{24,0},{28,4},{1,9},{5... | collective-permute-start | bytes 196616 | tf_op jit(solution)/shard_map/ppermute | solution.py:372
  7.1 1.6 %collective-permute-start.2 = (f32[1,128]{1,0:T(1,128)}, f32[1,128]{1,0:T(1,128)S(1)}, u32[]{:S(2)}, u32[]{:S(2)}) collective-permute-start(f32[1,128]{1,0:T(1,128)} %get-tuple-element.12), channel_id=1, source_target_pairs={{0,1},{1,0},{2,3},{3,2},{4,5},{5,4},{6,7},{7,6},{8,9},{9,8},{10,11... | collective-permute-start | bytes 1544 | tf_op jit(solution)/shard_map/ppermute | solution.py:344
  8.6 2.2 %collective-permute-done.2 = f32[1,128]{1,0:T(1,128)S(1)} collective-permute-done((f32[1,128]{1,0:T(1,128)}, f32[1,128]{1,0:T(1,128)S(1)}, u32[]{:S(2)}, u32[]{:S(2)}) %collective-permute-start.2) | collective-permute-done | bytes 544 | tf_op jit(solution)/shard_map/ppermute | solution.py:344
  10.8 0.6 %add.9 = f32[1,128]{1,0:T(1,128)S(1)} add(f32[1,128]{1,0:T(1,128)} %get-tuple-element.12, f32[1,128]{1,0:T(1,128)S(1)} %collective-permute-done.2) | non-fusion elementwise | flops 128 | bytes 1536 | tf_op jit(solution)/shard_map/add | solution.py:353
  11.4 2.6 %collective-permute-start.3 = (f32[1,128]{1,0:T(1,128)S(1)}, f32[1,128]{1,0:T(1,128)S(1)}, u32[]{:S(2)}, u32[]{:S(2)}) collective-permute-start(f32[1,128]{1,0:T(1,128)S(1)} %add.9), channel_id=1, source_target_pairs={{0,2},{1,3},{2,0},{3,1},{4,6},{5,7},{6,4},{7,5},{8,10},{9,11},{10,... | collective-permute-start | bytes 1544 | tf_op jit(solution)/shard_map/ppermute | solution.py:344
  14.0 1.7 %band.1 = (bf16[8,256,256]{2,1,0:T(8,128)(2,1)S(1)}, bf16[8,160,256]{2,1,0:T(8,128)(2,1)S(1)}) custom-call(bf16[64,128]{1,0:T(8,128)(2,1)S(1)} %bitcast.3), custom_call_target="tpu_custom_call" | custom-call | tf_op jit(solution)/shard_map/band/pallas_call | solution.py:409
  15.7 0.2 collective-permute-done.3
  15.9 0.0 collective-permute-done.1.far_ref
  15.9 0.0 collective-permute-done.near_ref
  15.9 0.0 copy-start.4
  16.0 0.8 %copy-done.4 = bf16[3,7,1024]{2,1,0:T(8,128)(2,1)S(1)} copy-done((bf16[3,7,1024]{2,1,0:T(8,128)(2,1)S(1)}, bf16[3,7,1024]{2,1,0:T(8,128)(2,1)}, u32[]{:S(2)}) %copy-start.4) | copy-done | bytes 43032
  16.7 6.2 %main.1 = f32[32,1024]{1,0:T(8,128)S(1)} custom-call(bf16[128,1024]{1,0:T(8,128)(2,1)S(1)} %copy-done, bf16[128,1024]{1,0:T(8,128)(2,1)S(1)} %copy-done.1, bf16[128,1024]{1,0:T(8,128)(2,1)S(1)} %copy-done.2, bf16[128,1024]{1,0:T(8,128)(2,1)S(1)} %copy-done.3, bf16[272,1024]{1,0:T(8,128)(2,1)S(1)} %collective-permute-done.near_ref, ...), custom_call_target="tpu_custom_call" | custom-call | tf_op jit(solution)/shard_map/main/pallas_call | solution.py:422
  23.0 0.2 collective-permute-start.4
  23.2 1.2 %collective-permute-done.4 = f32[32,1024]{1,0:T(8,128)S(1)} collective-permute-done((f32[32,1024]{1,0:T(8,128)S(1)}, f32[32,1024]{1,0:T(8,128)S(1)}, u32[]{:S(2)}, u32[]{:S(2)}) %collective-permute-start.4) | collective-permute-done | bytes 131104 | tf_op jit(solution)/shard_map/ppermute | solution.py:344
  24.4 2.2 %collective-permute-start.7 = (bf16[32,1024]{1,0:T(8,128)(2,1)S(1)}, bf16[32,1024]{1,0:T(8,128)(2,1)S(1)}, u32[]{:S(2)}, u32[]{:S(2)}) collective-permute-start(bf16[32,1024]{1,0:T(8,128)(2,1)S(1)} %add_convert_fusion.refs_0_), channel_id=1, source_target_pairs={{0,24},{4,28},{8,16},{12,20},{16,8},{20,12},{24,0},{28,4},{1,25},{... | collective-permute-start | bytes 196616 | tf_op jit(solution)/shard_map/ppermute | solution.py:344
  26.6 0.9 %collective-permute-start.6 = (bf16[32,1024]{1,0:T(8,128)(2,1)S(1)}, bf16[32,1024]{1,0:T(8,128)(2,1)S(1)}, u32[]{:S(2)}, u32[]{:S(2)}) collective-permute-start(bf16[32,1024]{1,0:T(8,128)(2,1)S(1)} %add_convert_fusion.refs_0_), channel_id=1, source_target_pairs={{0,16},{4,20},{8,24},{12,28},{16,0},{20,4},{24,8},{28,12},{1,17},{... | collective-permute-start | bytes 196616 | tf_op jit(solution)/shard_map/ppermute | solution.py:344
  27.4 0.6 %collective-permute-start.5 = (bf16[32,1024]{1,0:T(8,128)(2,1)S(1)}, bf16[32,1024]{1,0:T(8,128)(2,1)S(1)}, u32[]{:S(2)}, u32[]{:S(2)}) collective-permute-start(bf16[32,1024]{1,0:T(8,128)(2,1)S(1)} %add_convert_fusion.refs_0_), channel_id=1, source_target_pairs={{0,8},{4,12},{8,0},{12,4},{16,24},{20,28},{24,16},{28,20},{1,9},{5... | collective-permute-start | bytes 196616 | tf_op jit(solution)/shard_map/ppermute | solution.py:344
  28.0 1.7 %collective-permute-done.7.refs_3_ = bf16[32,1024]{1,0:T(8,128)(2,1)S(1)} collective-permute-done((bf16[32,1024]{1,0:T(8,128)(2,1)S(1)}, bf16[32,1024]{1,0:T(8,128)(2,1)S(1)}, u32[]{:S(2)}, u32[]{:S(2)}) %collective-permute-start.7) | collective-permute-done | bytes 65568 | tf_op jit(solution)/shard_map/ppermute | solution.py:344
  29.7 1.4 %collective-permute-done.6.refs_2_ = bf16[32,1024]{1,0:T(8,128)(2,1)S(1)} collective-permute-done((bf16[32,1024]{1,0:T(8,128)(2,1)S(1)}, bf16[32,1024]{1,0:T(8,128)(2,1)S(1)}, u32[]{:S(2)}, u32[]{:S(2)}) %collective-permute-start.6) | collective-permute-done | bytes 65568 | tf_op jit(solution)/shard_map/ppermute | solution.py:344
  31.1 0.7 %collective-permute-done.5.refs_1_ = bf16[32,1024]{1,0:T(8,128)(2,1)S(1)} collective-permute-done((bf16[32,1024]{1,0:T(8,128)(2,1)S(1)}, bf16[32,1024]{1,0:T(8,128)(2,1)S(1)}, u32[]{:S(2)}, u32[]{:S(2)}) %collective-permute-start.5) | collective-permute-done | bytes 65568 | tf_op jit(solution)/shard_map/ppermute | solution.py:344
  31.8 0.8 %last.1 = (f32[3,7,1024]{2,1,0:T(8,128)}, f32[64,128]{1,0:T(8,128)}) custom-call(bf16[32,1024]{1,0:T(8,128)(2,1)S(1)} %add_convert_fusion.refs_0_, bf16[32,1024]{1,0:T(8,128)(2,1)S(1)} %collective-permute-done.5.refs_1_, bf16[32,1024]{1,0:T(8,128)(2,1)S(1)} %collective-permute-done.6.refs_2_, bf16[32,1024]{1,0:T(8,128)(2,1)S(1)} %collective-permute-done.7.refs_3_), custom_call_target="tpu_custom_call" | custom-call | tf_op jit(solution)/shard_map/last/pallas_call | solution.py:458
  (13 shorter events, 0.0 us)
Async XLA Ops:
  0.6 13.4 %copy-start.6 = (bf16[128,64]{0,1:T(8,128)(2,1)S(1)}, bf16[128,64]{0,1:T(8,128)(2,1)}, u32[]{:S(2)}) copy-start(bf16[128,64]{0,1:T(8,128)(2,1)} %param.15) | copy-start | bytes 49156
  0.6 15.3 %copy-start = (bf16[128,1024]{1,0:T(8,128)(2,1)S(1)}, bf16[128,1024]{1,0:T(8,128)(2,1)}, u32[]{:S(2)}) copy-start(bf16[128,1024]{1,0:T(8,128)(2,1)} %q_ref.3) | copy-start | bytes 786436
  0.7 15.3 %copy-start.1 = (bf16[128,1024]{1,0:T(8,128)(2,1)S(1)}, bf16[128,1024]{1,0:T(8,128)(2,1)}, u32[]{:S(2)}) copy-start(bf16[128,1024]{1,0:T(8,128)(2,1)} %k_ref.3) | copy-start | bytes 786436
  0.7 15.3 %copy-start.2 = (bf16[128,1024]{1,0:T(8,128)(2,1)S(1)}, bf16[128,1024]{1,0:T(8,128)(2,1)}, u32[]{:S(2)}) copy-start(bf16[128,1024]{1,0:T(8,128)(2,1)} %v_ref.3) | copy-start | bytes 786436
  0.7 15.3 %copy-start.3 = (bf16[128,1024]{1,0:T(8,128)(2,1)S(1)}, bf16[128,1024]{1,0:T(8,128)(2,1)}, u32[]{:S(2)}) copy-start(bf16[128,1024]{1,0:T(8,128)(2,1)} %up_ref.3) | copy-start | bytes 786436
  4.0 11.9 %copy-start.5 = (f32[25,128]{1,0:T(8,128)S(1)}, f32[25,128]{1,0:T(8,128)}, u32[]{:S(2)}) copy-start(f32[25,128]{1,0:T(8,128)} %get-tuple-element.13.note_ref) | copy-start | bytes 38404
  4.0 11.9 %collective-permute-start = (bf16[272,1024]{1,0:T(8,128)(2,1)}, bf16[272,1024]{1,0:T(8,128)(2,1)S(1)}, u32[]{:S(2)}, u32[]{:S(2)}) collective-permute-start(bf16[272,1024]{1,0:T(8,128)(2,1)} %get-tuple-element.10), channel_id=1, source_target_pairs={{0,4},{4,8},{8,12},{12,16},{16,20},{20,24},{24,28},{28,0},{1,5},{5... | collective-permute-start | bytes 1671176 | tf_op jit(solution)/shard_map/ppermute | solution.py:372
  4.5 11.4 %collective-permute-start.1 = (bf16[32,1024]{1,0:T(8,128)(2,1)}, bf16[32,1024]{1,0:T(8,128)(2,1)S(1)}, u32[]{:S(2)}, u32[]{:S(2)}) collective-permute-start(bf16[32,1024]{1,0:T(8,128)(2,1)} %get-tuple-element.11), channel_id=1, source_target_pairs={{0,8},{4,12},{8,16},{12,20},{16,24},{20,28},{24,0},{28,4},{1,9},{5... | collective-permute-start | bytes 196616 | tf_op jit(solution)/shard_map/ppermute | solution.py:372
  7.1 3.8 %collective-permute-start.2 = (f32[1,128]{1,0:T(1,128)}, f32[1,128]{1,0:T(1,128)S(1)}, u32[]{:S(2)}, u32[]{:S(2)}) collective-permute-start(f32[1,128]{1,0:T(1,128)} %get-tuple-element.12), channel_id=1, source_target_pairs={{0,1},{1,0},{2,3},{3,2},{4,5},{5,4},{6,7},{7,6},{8,9},{9,8},{10,11... | collective-permute-start | bytes 1544 | tf_op jit(solution)/shard_map/ppermute | solution.py:344
  11.4 4.4 %collective-permute-start.3 = (f32[1,128]{1,0:T(1,128)S(1)}, f32[1,128]{1,0:T(1,128)S(1)}, u32[]{:S(2)}, u32[]{:S(2)}) collective-permute-start(f32[1,128]{1,0:T(1,128)S(1)} %add.9), channel_id=1, source_target_pairs={{0,2},{1,3},{2,0},{3,1},{4,6},{5,7},{6,4},{7,5},{8,10},{9,11},{10,... | collective-permute-start | bytes 1544 | tf_op jit(solution)/shard_map/ppermute | solution.py:344
  15.9 0.8 %copy-start.4 = (bf16[3,7,1024]{2,1,0:T(8,128)(2,1)S(1)}, bf16[3,7,1024]{2,1,0:T(8,128)(2,1)}, u32[]{:S(2)}) copy-start(bf16[3,7,1024]{2,1,0:T(8,128)(2,1)} %se_ref.1) | copy-start | bytes 129028
  23.0 1.4 %collective-permute-start.4 = (f32[32,1024]{1,0:T(8,128)S(1)}, f32[32,1024]{1,0:T(8,128)S(1)}, u32[]{:S(2)}, u32[]{:S(2)}) collective-permute-start(f32[32,1024]{1,0:T(8,128)S(1)} %main.1), channel_id=1, source_target_pairs={{0,4},{4,0},{8,12},{12,8},{16,20},{20,16},{24,28},{28,24},{1,5},{5... | collective-permute-start | bytes 393224 | tf_op jit(solution)/shard_map/ppermute | solution.py:344
  24.4 5.3 %collective-permute-start.7 = (bf16[32,1024]{1,0:T(8,128)(2,1)S(1)}, bf16[32,1024]{1,0:T(8,128)(2,1)S(1)}, u32[]{:S(2)}, u32[]{:S(2)}) collective-permute-start(bf16[32,1024]{1,0:T(8,128)(2,1)S(1)} %add_convert_fusion.refs_0_), channel_id=1, source_target_pairs={{0,24},{4,28},{8,16},{12,20},{16,8},{20,12},{24,0},{28,4},{1,25},{... | collective-permute-start | bytes 196616 | tf_op jit(solution)/shard_map/ppermute | solution.py:344
  26.6 4.5 %collective-permute-start.6 = (bf16[32,1024]{1,0:T(8,128)(2,1)S(1)}, bf16[32,1024]{1,0:T(8,128)(2,1)S(1)}, u32[]{:S(2)}, u32[]{:S(2)}) collective-permute-start(bf16[32,1024]{1,0:T(8,128)(2,1)S(1)} %add_convert_fusion.refs_0_), channel_id=1, source_target_pairs={{0,16},{4,20},{8,24},{12,28},{16,0},{20,4},{24,8},{28,12},{1,17},{... | collective-permute-start | bytes 196616 | tf_op jit(solution)/shard_map/ppermute | solution.py:344
  27.4 4.3 %collective-permute-start.5 = (bf16[32,1024]{1,0:T(8,128)(2,1)S(1)}, bf16[32,1024]{1,0:T(8,128)(2,1)S(1)}, u32[]{:S(2)}, u32[]{:S(2)}) collective-permute-start(bf16[32,1024]{1,0:T(8,128)(2,1)S(1)} %add_convert_fusion.refs_0_), channel_id=1, source_target_pairs={{0,8},{4,12},{8,0},{12,4},{16,24},{20,28},{24,16},{28,20},{1,9},{5... | collective-permute-start | bytes 196616 | tf_op jit(solution)/shard_map/ppermute | solution.py:344

commit v3 on v2

v3 whole, which is shorter than its diff:
```python
import functools

import jax
import jax.numpy as jnp
from jax import lax
from jax.experimental import pallas as pl
from jax.experimental.pallas import tpu as pltpu
from jax.sharding import PartitionSpec as P

BLOCK = 32
LANES = 128
TAIL = 16
PRE = 8
SLOT = PRE + BLOCK
LIMIT = 24 * 1024 * 1024
MOST = 60 * 1024 * 1024
TL, BD, FW = 1.5, 1.6, 3.0
COPIES = 64
F32 = jnp.float32
BF16 = jnp.bfloat16


def spec(space=pltpu.VMEM):
    return pl.BlockSpec(memory_space=space)


def cost(micros):
    return pl.CostEstimate(flops=1, bytes_accessed=int(micros * 3.6e6), transcendentals=0)


def summed(parts):
    while len(parts) > 1:
        parts = [sum(parts[i + 1 : i + 2], parts[i]) for i in range(0, len(parts), 2)]
    return parts[0]


def dot(a, b, contract, precision=None):
    return lax.dot_general(
        a, b, ((contract[0], contract[1]), ((), ())), precision=precision, preferred_element_type=F32
    )


def doc_of(lengths_ref, block):
    count = jnp.int32(0)
    end = jnp.int32(0)
    for i in range(lengths_ref.shape[0]):
        end = end + lengths_ref[i]
        count = count + jnp.where(block >= end, 1, 0)
    return jnp.where(block >= 0, count, -1)


def first_kernel(
    span,
    lengths_ref,
    reward_ref,
    q_ref,
    k_ref,
    v_ref,
    up_ref,
    h_ref,
    se_ref,
    near_ref,
    far_ref,
    sq_ref,
    note_ref,
    h_out_ref,
    se_out_ref,
    up_here,
    here,
    lengths_here,
    reward_here,
    sems,
):
    rows, channels = k_ref.shape
    tail = pl.ds(rows - TAIL, TAIL)
    pieces = (
        (up_ref, up_here),
        (q_ref.at[tail], here.at[0]),
        (k_ref.at[tail], here.at[1]),
        (v_ref.at[tail], here.at[2]),
        (lengths_ref, lengths_here),
        (reward_ref, reward_here),
        (h_ref, h_out_ref),
        (se_ref, se_out_ref),
    )
    copies = [
        pltpu.make_async_copy(source, target, sems.at[i]) for i, (source, target) in enumerate(pieces)
    ]
    for copy in copies:
        copy.start()
    copies[0].wait()
    total = jnp.zeros((rows, LANES), F32)
    for tile in range(channels // LANES):
        part = up_here[:, tile * LANES : (tile + 1) * LANES].astype(F32)
        total = total + part * part
    sq_ref[...] = jnp.broadcast_to(jnp.sum(total.T, axis=0, keepdims=True), sq_ref.shape)
    for copy in copies[1:]:
        copy.wait()
    tails = [here[i].astype(F32)[TAIL - PRE :] for i in range(3)]
    near_ref[...] = here[0]
    far_ref[...] = jnp.concatenate(tails[1:], axis=0).astype(BF16)
    own = rows // BLOCK
    window = span + own
    first = lax.axis_index("dp") * own
    docs = [doc_of(lengths_here, first + b) for b in range(-span - 1, own)]
    notes = [(docs[b + 1] == docs[b]) & (docs[b] >= 0) for b in range(window)]
    docs = docs[1:]
    notes = notes + [docs[n + s] == docs[n + span] for n in range(own) for s in range(span)]
    for i, note in enumerate(notes):
        note_ref[i : i + 1] = jnp.full((1, rows), jnp.where(note, 1.0, 0.0).astype(F32))
    note_ref[len(notes) : len(notes) + 1] = reward_here[...].astype(F32) * 0.25


def band_kernel(h_ref, band_ref, band_t_ref, row_ref):
    groups, taps = h_ref.shape
    tiles = band_ref.shape[0]
    per_tile = groups // tiles
    width = band_ref.shape[2]
    tap = lax.broadcasted_iota(jnp.int32, (taps, width), 0)
    lane = lax.broadcasted_iota(jnp.int32, (taps, width), 1)
    flip = jnp.where(tap + lane == taps, 1.0, 0.0).astype(F32)
    row_ref[...] = dot(h_ref[...], flip.astype(BF16), ((1,), (0,)))

    def one(tile, carry):
        rows = row_ref[pl.ds(pl.multiple_of(tile * per_tile, per_tile), per_tile), :]
        parts = [
            pltpu.roll(
                jnp.broadcast_to(rows[g : g + 1], (BLOCK, width)), 0, 1, stride=1, stride_axis=0
            )
            for g in range(per_tile)
        ]
        band = jnp.concatenate(parts, axis=0)
        band_ref[tile] = band.astype(BF16)
        band_t_ref[tile] = band.T[0 : taps + BLOCK].astype(BF16)
        return carry

    lax.fori_loop(0, tiles, one, 0)


def notes_of(note_ref, own, span):
    window = own + span
    joined = [note_ref[b : b + 1, 0:LANES] for b in range(window)]
    same = [
        [note_ref[window + n * span + s : window + n * span + s + 1, 0:LANES] for s in range(span)]
        for n in range(own)
    ]
    reward = note_ref[window + own * span : window + own * span + 1]
    return joined, same, reward


def lane_picks(per_tile):
    lane_group = lax.broadcasted_iota(jnp.int32, (BLOCK, LANES), 1) // (LANES // per_tile)
    return [lane_group == g for g in range(per_tile)]


def shifted(x_ref, tile, b, j):
    at = SLOT * b + PRE - j
    return x_ref[tile, at : at + BLOCK, :]


def tile_lanes(tile):
    return pl.ds(pl.multiple_of(tile * LANES, LANES), LANES)


def in_groups(count, beside, stages):
    def some(step, carry):
        now = [step * beside + side for side in range(beside)]
        kept = [None] * beside
        for stage in stages:
            kept = [stage(tile, side, got) for side, (tile, got) in enumerate(zip(now, kept))]
        return carry

    lax.fori_loop(0, count // beside, some, 0)


def forward_kernel(
    beside,
    q_ref,
    k_ref,
    v_ref,
    up_ref,
    k_near_ref,
    v_near_ref,
    near_ref,
    far_ref,
    note_ref,
    se_ref,
    band_ref,
    xq_ref,
    xk_ref,
    xv_ref,
    ks_ref,
    vs_ref,
    zw_ref,
    uq_ref,
    um_ref,
    z_ref,
):
    rows, channels = q_ref.shape
    own = rows // BLOCK
    window = xk_ref.shape[1] // SLOT
    span = window - own
    tiles = channels // LANES
    per_tile = band_ref.shape[1] // BLOCK
    tap_count = se_ref.shape[1]
    joined, same, _ = notes_of(note_ref, own, span)
    picks = lane_picks(per_tile)
    for side in range(beside):
        z_ref[side, window * BLOCK :] = jnp.zeros((z_ref.shape[1] - window * BLOCK, LANES), BF16)

    def fill(x_ref, tile, pieces, before, first_block):
        for b, piece in enumerate(pieces):
            at = SLOT * b
            x_ref[tile, at : at + PRE] = before * joined[first_block + b]
            x_ref[tile, at + PRE : at + SLOT] = piece
            before = piece[BLOCK - PRE :]

    def short(x_ref, tile, b, taps_now):
        total = taps_now[0:1] * shifted(x_ref, tile, b, 0)
        for j in range(1, tap_count):
            total = total + taps_now[j : j + 1] * shifted(x_ref, tile, b, j)
        return total

    def filters(tile, side, _):
        at = tile_lanes(tile)
        q_taps = se_ref[0, :, at].astype(F32)
        k_taps = se_ref[1, :, at].astype(F32)
        v_taps = se_ref[2, :, at].astype(F32)

        def blocks_of(ref, start, count):
            return [
                ref[start + BLOCK * b : start + BLOCK * (b + 1), at].astype(F32) for b in range(count)
            ]

        q_before = near_ref[:, at].astype(F32)[TAIL - PRE :]
        k_before, v_before = jnp.split(far_ref[:, at].astype(F32), 2)
        k_halo = blocks_of(k_near_ref, rows - span * BLOCK, span)
        v_halo = blocks_of(v_near_ref, rows - span * BLOCK, span)
        fill(xk_ref, tile, k_halo + blocks_of(k_ref, 0, own), k_before, 0)
        fill(xv_ref, tile, v_halo + blocks_of(v_ref, 0, own), v_before, 0)
        fill(xq_ref, tile, blocks_of(q_ref, 0, own), q_before, span)
        for b in range(window):
            at_b = slice(BLOCK * b, BLOCK * (b + 1))
            ks = short(xk_ref, tile, b, k_taps)
            vs = short(xv_ref, tile, b, v_taps)
            ks_ref[tile, at_b] = ks
            vs_ref[tile, at_b] = vs
            z_ref[side, at_b] = (ks * vs).astype(BF16)
        for n in range(own):
            at_n = slice(BLOCK * n, BLOCK * (n + 1))
            uq_ref[tile, at_n] = up_ref[at_n, at].astype(F32) * short(xq_ref, tile, n, q_taps)
            lanes = slice(LANES * (n % 2), LANES * (n % 2 + 1))
            for s in range(2 * LANES // BLOCK):
                piece = z_ref[side, BLOCK * (n + s) : BLOCK * (n + s + 1)]
                if s < span:
                    piece = piece * same[n][s].astype(BF16)
                zw_ref[tile, n // 2, BLOCK * s : BLOCK * (s + 1), lanes] = piece

    def medium(tile, side, _):
        at = tile_lanes(tile)
        band = band_ref[tile]
        for half in range(own // 2):
            wide = dot(band, zw_ref[tile, half], ((1,), (0,)))
            for part in range(2):
                n = 2 * half + part
                at_n = slice(BLOCK * n, BLOCK * (n + 1))
                lanes = slice(LANES * part, LANES * (part + 1))
                m = wide[0:BLOCK, lanes]
                for g in range(1, per_tile):
                    m = jnp.where(picks[g], wide[BLOCK * g : BLOCK * (g + 1), lanes], m)
                um_ref[tile, at_n] = up_ref[at_n, at].astype(F32) * m

    in_groups(tiles, beside, (filters, medium))


def backward_kernel(
    all_channels,
    beside,
    count,
    xq_ref,
    xk_ref,
    xv_ref,
    ks_ref,
    vs_ref,
    zw_ref,
    uq_ref,
    um_ref,
    note_ref,
    band_t_ref,
    *rest,
):
    *sq_refs, out_ref, dm_ref, dz_ref, skew_ref, w_ref = rest
    tiles, rows = uq_ref.shape[0:2]
    own = rows // BLOCK
    window = xk_ref.shape[1] // SLOT
    span = window - own
    per_tile = band_t_ref.shape[2] // BLOCK
    _, same, reward = notes_of(note_ref, own, span)
    masks = [jnp.where(pick, 1.0, 0.0).astype(BF16) for pick in lane_picks(per_tile)]
    weight = reward * lax.rsqrt(summed([ref[0:1] for ref in sq_refs]) / all_channels + 1e-06)
    w_ref[...] = jnp.broadcast_to(weight, (LANES, rows)).T

    def fold(x):
        return jnp.sum(x.reshape(BLOCK // 8, 8, LANES), axis=0)

    def stack(tile, side, _):
        for n in range(own):
            at_n = slice(BLOCK * n, BLOCK * (n + 1))
            dm = (w_ref[at_n] * uq_ref[tile, at_n]).astype(BF16)
            lanes = slice(LANES * (n % 2), LANES * (n % 2 + 1))
            for g in range(per_tile):
                dm_ref[side, n // 2, BLOCK * g : BLOCK * (g + 1), lanes] = dm * masks[g]

    def middle(tile, side, _):
        band_t = band_t_ref[tile]
        pair = None
        for half in range(own // 2):
            dms = dm_ref[side, half]
            back = dot(band_t, dms, ((1,), (0,)))
            both = dot(dms, zw_ref[tile, half], ((1,), (1,)))
            pair = both if pair is None else pair + both
            for part in range(2):
                n = 2 * half + part
                lanes = slice(LANES * part, LANES * (part + 1))
                for s in range(span + 1):
                    at_s = slice(BLOCK * (n + s), BLOCK * (n + s + 1))
                    term = back[BLOCK * s : BLOCK * (s + 1), lanes]
                    if s < span:
                        term = term * same[n][s]
                    if n == 0 or s == span:
                        dz_ref[side, at_s] = term
                    else:
                        dz_ref[side, at_s] += term
        lined = pair.reshape(per_tile, BLOCK // 8, 8, 2 * LANES)
        skew = None
        for r in range(BLOCK // 8):
            rows_r = lined[:, r].reshape(per_tile * 8, 2 * LANES)
            moved = pltpu.roll(rows_r, 2 * LANES - 1 - 8 * r, 1)
            skew = moved if skew is None else skew + moved
        skew_ref[tile] = skew

    def grads(tile, side, _):
        at = tile_lanes(tile)
        gq, gk, gv = ([jnp.zeros((8, LANES), F32) for _ in range(count)] for _ in range(3))
        for n in range(own):
            at_n = slice(BLOCK * n, BLOCK * (n + 1))
            cot_q = w_ref[at_n] * um_ref[tile, at_n]
            for j in range(count):
                gq[j] = gq[j] + fold(cot_q * shifted(xq_ref, tile, n, j))
        for b in range(window):
            at_b = slice(BLOCK * b, BLOCK * (b + 1))
            dz = dz_ref[side, at_b]
            cot_k = dz * vs_ref[tile, at_b]
            cot_v = dz * ks_ref[tile, at_b]
            for j in range(count):
                gk[j] = gk[j] + fold(cot_k * shifted(xk_ref, tile, b, j))
                gv[j] = gv[j] + fold(cot_v * shifted(xv_ref, tile, b, j))
        for i, sums in enumerate((gq, gk, gv)):
            for j in range(count):
                out_ref[8 * i + j : 8 * i + j + 1, at] = jnp.sum(sums[j], axis=0, keepdims=True)
            out_ref[8 * i + count : 8 * i + 8, at] = jnp.zeros((8 - count, LANES), F32)

    in_groups(tiles, beside, (stack, middle, grads))
    skew = skew_ref[...].reshape(tiles * per_tile * 8, 2 * LANES)
    row_index = lax.broadcasted_iota(jnp.int32, skew.shape, 0)
    for bit in range(3):
        moved = pltpu.roll(skew, 2 * LANES - (1 << bit), 1)
        skew = jnp.where((row_index >> bit) & 1 == 1, moved, skew)
    totals = jnp.sum(skew[:, 0:LANES].reshape(tiles * per_tile, 8, LANES), axis=1)
    for tile in range(tiles):
        out_ref[24 : 24 + per_tile, LANES * tile : LANES * (tile + 1)] = totals[
            per_tile * tile : per_tile * (tile + 1)
        ]


def last_kernel(scale, *refs):
    *part_refs, se_ref, mr_ref = refs
    total = summed([ref[...].astype(F32) for ref in part_refs]) * scale
    tap_count = se_ref.shape[1]
    channels = total.shape[1]
    for i in range(3):
        se_ref[i] = total[8 * i : 8 * i + tap_count]
    flat = jnp.concatenate(
        [total[24:, t * LANES : (t + 1) * LANES] for t in range(channels // LANES)], axis=0
    )
    tap = lax.broadcasted_iota(jnp.int32, (LANES, LANES), 0)
    lane = lax.broadcasted_iota(jnp.int32, (LANES, LANES), 1)
    flip = jnp.where(tap + lane == LANES - 1, 1.0, 0.0).astype(F32)
    mr_ref[...] = dot(flat, flip, ((1,), (0,)), lax.Precision.HIGHEST)


def swapped(value, axis, distance):
    count = lax.axis_size(axis)
    return lax.ppermute(value, axis, [(i, i ^ distance) for i in range(count)])


def summed_small(value, axis, beside):
    count = lax.axis_size(axis)
    if count & (count - 1):
        return [lax.psum(value, axis)], beside
    distance = 1
    while 2 * distance < count:
        got = swapped(value, axis, distance)
        if distance == 1:
            got, beside = lax.optimization_barrier((got, beside))
        value = value + got
        distance *= 2
    return [value, swapped(value, axis, distance)], beside


def spread(part, axis):
    count = lax.axis_size(axis)
    if count & (count - 1) or count < 8:
        return [lax.psum(part, axis)]
    mine = (part + swapped(part, axis, 1)).astype(BF16)
    distance = 8
    while distance < count:
        mine = (mine.astype(F32) + swapped(mine, axis, distance).astype(F32)).astype(BF16)
        distance *= 2
    return [mine] + [swapped(mine, axis, d) for d in (2, 4, 6)]


def moved_up(value, axis, steps):
    count = lax.axis_size(axis)
    return lax.ppermute(value, axis, [(i, (i + steps) % count) for i in range(count)])


def on_device(query, key, value, upstream, reward, lengths, se_filter, mr_filter):
    rows, channels = query.shape
    taps, groups = mr_filter.shape
    tap_count = se_filter.shape[1]
    tiles = channels // LANES
    per_tile = groups // tiles
    stack = per_tile * BLOCK
    own = rows // BLOCK
    span = taps // BLOCK
    window = own + span
    beside = 2 if tiles % 2 == 0 else 1
    dp = lax.axis_size("dp")

    k_near = moved_up(key, "dp", 1)
    v_near = moved_up(value, "dp", 1)
    near, far, sq, notes, medium_taps, short_taps = pl.pallas_call(
        functools.partial(first_kernel, span),
        out_shape=(
            jax.ShapeDtypeStruct((TAIL, channels), BF16),
            jax.ShapeDtypeStruct((2 * PRE, channels), BF16),
            jax.ShapeDtypeStruct((COPIES, rows), F32),
            jax.ShapeDtypeStruct((window + own * span + 1, rows), F32),
            jax.ShapeDtypeStruct((groups, taps), BF16),
            jax.ShapeDtypeStruct(se_filter.shape, BF16),
        ),
        in_specs=[spec(pl.ANY)] * 8,
        out_specs=(spec(),) * 6,
        scratch_shapes=[
            pltpu.VMEM((rows, channels), BF16),
            pltpu.VMEM((3, TAIL, channels), BF16),
            pltpu.SMEM(lengths.shape, jnp.int32),
            pltpu.VMEM((1, rows), jnp.int32),
            pltpu.SemaphoreType.DMA((8,)),
        ],
        compiler_params=pltpu.CompilerParams(vmem_limit_bytes=LIMIT),
        cost_estimate=cost(TL),
        name="first",
    )(
        *[
            pltpu.with_memory_space_constraint(x, pltpu.HBM)
            for x in (
                lengths,
                reward.reshape(1, rows),
                query,
                key,
                value,
                upstream,
                mr_filter.T,
                se_filter,
            )
        ]
    )
    near = moved_up(near, "dp", 1)
    far = moved_up(far, "dp", 2)

    band, band_t = pl.pallas_call(
        band_kernel,
        out_shape=(
            jax.ShapeDtypeStruct((tiles, stack, 2 * LANES), BF16),
            jax.ShapeDtypeStruct((tiles, taps + BLOCK, stack), BF16),
        ),
        in_specs=[spec()],
        out_specs=(spec(),) * 2,
        scratch_shapes=[pltpu.VMEM((groups, 2 * LANES), F32)],
        compiler_params=pltpu.CompilerParams(vmem_limit_bytes=LIMIT),
        cost_estimate=cost(BD),
        name="band",
    )(medium_taps)

    squares, (band, band_t) = summed_small(sq, "fsdp", (band, band_t))
    kept = pl.pallas_call(
        functools.partial(forward_kernel, beside),
        out_shape=(
            jax.ShapeDtypeStruct((tiles, own * SLOT, LANES), F32),
            jax.ShapeDtypeStruct((tiles, window * SLOT, LANES), F32),
            jax.ShapeDtypeStruct((tiles, window * SLOT, LANES), F32),
            jax.ShapeDtypeStruct((tiles, window * BLOCK, LANES), F32),
            jax.ShapeDtypeStruct((tiles, window * BLOCK, LANES), F32),
            jax.ShapeDtypeStruct((tiles, own // 2, 2 * LANES, 2 * LANES), BF16),
            jax.ShapeDtypeStruct((tiles, rows, LANES), F32),
            jax.ShapeDtypeStruct((tiles, rows, LANES), F32),
        ),
        in_specs=[spec()] * 11,
        out_specs=(spec(),) * 8,
        scratch_shapes=[pltpu.VMEM((beside, (own - 1) * BLOCK + 2 * LANES, LANES), BF16)],
        compiler_params=pltpu.CompilerParams(vmem_limit_bytes=LIMIT),
        cost_estimate=cost(FW),
        name="forward",
    )(query, key, value, upstream, k_near, v_near, near, far, notes, short_taps, band)
    part = pl.pallas_call(
        functools.partial(
            backward_kernel, float(channels * lax.axis_size("fsdp")), beside, tap_count
        ),
        out_shape=jax.ShapeDtypeStruct((24 + per_tile, channels), F32),
        in_specs=[spec()] * (10 + len(squares)),
        out_specs=spec(),
        scratch_shapes=[
            pltpu.VMEM((beside, own // 2, stack, 2 * LANES), BF16),
            pltpu.VMEM((beside, window * BLOCK, LANES), F32),
            pltpu.VMEM((tiles, per_tile * 8, 2 * LANES), F32),
            pltpu.VMEM((rows, LANES), F32),
        ],
        compiler_params=pltpu.CompilerParams(vmem_limit_bytes=LIMIT),
        name="backward",
    )(*kept, notes, band_t, *squares)

    parts = spread(part, "dp")
    grad_se, grad_mr = pl.pallas_call(
        functools.partial(last_kernel, 1.0 / rows),
        out_shape=(
            jax.ShapeDtypeStruct((3, tap_count, channels), F32),
            jax.ShapeDtypeStruct((groups, taps), F32),
        ),
        in_specs=[spec()] * len(parts),
        out_specs=(spec(),) * 2,
        compiler_params=pltpu.CompilerParams(vmem_limit_bytes=LIMIT),
        name="last",
    )(*parts)
    return grad_se, grad_mr.T


def solution(mesh):
    in_specs = (
        P("dp", "fsdp"),
        P("dp", "fsdp"),
        P("dp", "fsdp"),
        P("dp", "fsdp"),
        P("dp"),
        P(),
        P(None, None, "fsdp"),
        P(None, "fsdp"),
    )
    out_specs = (P(None, None, "fsdp"), P(None, "fsdp"))
    return jax.shard_map(
        on_device, mesh=mesh, in_specs=in_specs, out_specs=out_specs, check_vma=False
    )
```

time: 32.8 us -> 29.9 us (0.912)
  waiting for transfers between devices: 7.28 us -> 4.16 us
  starting transfers between devices: 11 us -> 13.6 us
  Pallas kernels: 12 us -> 11.2 us
  local copies, waits for them, and re-layouts: 0.82 us -> 0.02 us
  other arithmetic: 0.64 us -> 0.02 us
    ppermute x6, waiting for transfers between devices: 7.27 us -> 4.15 us  [swapped(): return lax.ppermute(value, axis, [(i, i ^ distance) for i in range(count)])]
    ppermute x2 -> x4, starting transfers between devices: 3.06 us -> 4.63 us  [moved_up(): lax.ppermute(value, axis, [(i, (i + steps) % count) for i in range(count)])]
    ppermute x6, starting transfers between devices: 7.98 us -> 8.94 us  [swapped(): return lax.ppermute(value, axis, [(i, i ^ distance) for i in range(count)])]
    pallas_call x2 -> x3, Pallas kernels: 9.55 us -> 8.73 us  [the longest x1 4.37 us: on_device(): pl.pallas_call(functools.partial(backward_kernel, float(channels * lax.ax...]
    unnamed x14 -> x8, local copies, waits for them, and re-layouts: 0.82 us -> 0.02 us
    add x2 -> x1, other arithmetic: 0.62 us -> 0.01 us  [summed_small(): value = value + got]
  transfers between devices with their start and end apart: 8 -> 10, of which waited for: 6 -> 3; matrix products, arithmetic and copies ran while one was open for 2% -> 0% of each run, Pallas kernels for 5% -> 20%
where the time goes in v3:
time: 29.9 us; the launch traced here: 29.7 us
  starting transfers between devices  13.6 us (45%)
  Pallas kernels  11.2 us (37%)
  waiting for transfers between devices  4.16 us (14%)
  between operations  0.77 us (3%)
    ppermute x6, starting transfers between devices, swapped(): return lax.ppermute(value, axis, [(i, i ^ distance) for i in range(count)])  8.94 us
    ppermute x4, starting transfers between devices, moved_up(): lax.ppermute(value, axis, [(i, (i + steps) % count) for i in range(count)])  4.63 us
    pallas_call x1, Pallas kernels, on_device(): pl.pallas_call(functools.partial(backward_kernel, float(channels * lax.ax...  4.37 us
    ppermute x6, waiting for transfers between devices, swapped(): return lax.ppermute(value, axis, [(i, i ^ distance) for i in range(count)])  4.15 us
    pallas_call x1, Pallas kernels, on_device(): pl.pallas_call(functools.partial(forward_kernel, beside), out_shape=(jax....  3.11 us
    pallas_call x1, Pallas kernels, on_device(): pl.pallas_call(band_kernel, out_shape=(jax.ShapeDtypeStruct((tiles, stack...  1.66 us
    pallas_call x1, Pallas kernels, on_device(): pl.pallas_call(functools.partial(first_kernel, span), out_shape=(jax.Shap...  1.24 us
    pallas_call x1, Pallas kernels, on_device(): pl.pallas_call(functools.partial(last_kernel, 1.0 / rows), out_shape=(jax...  0.8 us
  transfers between devices with their start and end apart: 10, of which 3 were waited for; matrix products, arithmetic and copies ran while one was open for 0% of the time, Pallas kernels for 20%

profile of v3, /device:TPU:0, one launch (start us, length us, event | category | flops | bytes accessed | tf_op | source)
XLA Modules:
  0.0 29.7 jit_solution(12577842820234563002)
XLA Ops:
  0.7 0.5 %collective-permute-start = (bf16[128,1024]{1,0:T(8,128)(2,1)}, bf16[128,1024]{1,0:T(8,128)(2,1)S(1)}, u32[]{:S(2)}, u32[]{:S(2)}) collective-permute-start(bf16[128,1024]{1,0:T(8,128)(2,1)} %k_ref.3), channel_id=1, source_target_pairs={{0,4},{4,8},{8,12},{12,16},{16,20},{20,24},{24,28},{28,0},{1,5},{5... | collective-permute-start | bytes 786440 | tf_op jit(solution)/shard_map/ppermute | solution.py:425
  1.2 2.6 %collective-permute-start.1 = (bf16[128,1024]{1,0:T(8,128)(2,1)}, bf16[128,1024]{1,0:T(8,128)(2,1)S(1)}, u32[]{:S(2)}, u32[]{:S(2)}) collective-permute-start(bf16[128,1024]{1,0:T(8,128)(2,1)} %v_ref.3), channel_id=1, source_target_pairs={{0,4},{4,8},{8,12},{12,16},{16,20},{20,24},{24,28},{28,0},{1,5},{5... | collective-permute-start | bytes 786440 | tf_op jit(solution)/shard_map/ppermute | solution.py:425
  3.8 1.2 %first.1 = (bf16[16,1024]{1,0:T(8,128)(2,1)S(1)}, bf16[16,1024]{1,0:T(8,128)(2,1)S(1)}, f32[64,128]{1,0:T(8,128)S(1)}, f32[25,128]{1,0:T(8,128)S(1)}, bf16[64,12...) custom-call(s32[4]{0:T(128)} %lengths_ref.1, s32[1,128]{1,0:T(1,128)} %bitcast.4, bf16[128,1024]{1,0:T(8,128)(2,1)} %q_ref.3, ...), custom_call_target="tpu_custom_call" | custom-call | flops 1 | bytes 5400000 | tf_op jit(solution)/shard_map/first/pallas_call | solution.py:443
  5.0 1.6 %collective-permute-start.4 = (f32[64,128]{1,0:T(8,128)S(1)}, f32[64,128]{1,0:T(8,128)S(1)}, u32[]{:S(2)}, u32[]{:S(2)}) collective-permute-start(f32[64,128]{1,0:T(8,128)S(1)} %get-tuple-element.27), channel_id=1, source_target_pairs={{0,1},{1,0},{2,3},{3,2},{4,5},{5,4},{6,7},{7,6},{8,9},{9,8},{10,11... | collective-permute-start | bytes 98312 | tf_op jit(solution)/shard_map/ppermute | solution.py:394
  6.7 0.0 collective-permute-start.2
  6.7 1.5 %collective-permute-start.3 = (bf16[16,1024]{1,0:T(8,128)(2,1)S(1)}, bf16[16,1024]{1,0:T(8,128)(2,1)S(1)}, u32[]{:S(2)}, u32[]{:S(2)}) collective-permute-start(bf16[16,1024]{1,0:T(8,128)(2,1)S(1)} %get-tuple-element.24), channel_id=1, source_target_pairs={{0,8},{4,12},{8,16},{12,20},{16,24},{20,28},{24,0},{28,4},{1,9},{5... | collective-permute-start | bytes 98312 | tf_op jit(solution)/shard_map/ppermute | solution.py:425
  8.2 1.7 %band.1 = (bf16[8,256,256]{2,1,0:T(8,128)(2,1)S(1)}, bf16[8,160,256]{2,1,0:T(8,128)(2,1)S(1)}) custom-call(bf16[64,128]{1,0:T(8,128)(2,1)S(1)} %get-tuple-element.28.h_ref), custom_call_target="tpu_custom_call" | custom-call | flops 1 | bytes 5760000 | tf_op jit(solution)/shard_map/band/pallas_call | solution.py:483
  9.9 0.0 collective-permute-done.4
  9.9 2.7 %collective-permute-start.5 = (f32[64,128]{1,0:T(8,128)S(1)}, f32[64,128]{1,0:T(8,128)S(1)}, u32[]{:S(2)}, u32[]{:S(2)}) collective-permute-start(f32[64,128]{1,0:T(8,128)S(1)} %add.6.rest_0_), channel_id=1, source_target_pairs={{0,2},{1,3},{2,0},{3,1},{4,6},{5,7},{6,4},{7,5},{8,10},{9,11},{10,... | collective-permute-start | bytes 98312 | tf_op jit(solution)/shard_map/ppermute | solution.py:394
  12.5 0.0 collective-permute-done.2.near_ref
  12.5 0.0 collective-permute-done.3.far_ref
  12.6 0.0 collective-permute-done.k_near_ref
  12.6 3.1 %forward.1 = (f32[8,160,128]{2,1,0:T(8,128)S(1)}, f32[8,320,128]{2,1,0:T(8,128)S(1)}, f32[8,320,128]{2,1,0:T(8,128)S(1)}, f32[8,256,128]{2,1,0:T(8,128)S(1)}, f3...) custom-call(bf16[128,1024]{1,0:T(8,128)(2,1)S(1)} %copy-done, ...), custom_call_target="tpu_custom_call" | custom-call | flops 1 | bytes 10800000 | tf_op jit(solution)/shard_map/forward/pallas_call | solution.py:498
  15.7 0.0 collective-permute-done.5.rest_1_
  15.7 4.4 %backward.1 = f32[32,1024]{1,0:T(8,128)S(1)} custom-call(f32[8,160,128]{2,1,0:T(8,128)S(1)} %get-tuple-element.32.xq_ref, f32[8,320,128]{2,1,0:T(8,128)S(1)} %get-tuple-element.33.xk_ref, f32[8,320,128]{2,1,0:T(8,128)S(1)} %get-tuple-element.34.xv_ref, f32[8,256,128]{2,1,0:T(8,128)S(1)} %get-tuple-element.35.ks_ref, ...), custom_call_target="tpu_custom_call" | custom-call | tf_op jit(solution)/shard_map/backward/pallas_call | solution.py:517
  20.1 1.1 %collective-permute-start.6 = (f32[32,1024]{1,0:T(8,128)S(1)}, f32[32,1024]{1,0:T(8,128)S(1)}, u32[]{:S(2)}, u32[]{:S(2)}) collective-permute-start(f32[32,1024]{1,0:T(8,128)S(1)} %backward.1), channel_id=1, source_target_pairs={{0,4},{4,0},{8,12},{12,8},{16,20},{20,16},{24,28},{28,24},{1,5},{5... | collective-permute-start | bytes 393224 | tf_op jit(solution)/shard_map/ppermute | solution.py:394
  21.2 1.0 %collective-permute-done.6 = f32[32,1024]{1,0:T(8,128)S(1)} collective-permute-done((f32[32,1024]{1,0:T(8,128)S(1)}, f32[32,1024]{1,0:T(8,128)S(1)}, u32[]{:S(2)}, u32[]{:S(2)}) %collective-permute-start.6) | collective-permute-done | bytes 131104 | tf_op jit(solution)/shard_map/ppermute | solution.py:394
  22.2 1.5 %collective-permute-start.9 = (bf16[32,1024]{1,0:T(8,128)(2,1)S(1)}, bf16[32,1024]{1,0:T(8,128)(2,1)S(1)}, u32[]{:S(2)}, u32[]{:S(2)}) collective-permute-start(bf16[32,1024]{1,0:T(8,128)(2,1)S(1)} %add_convert_fusion.refs_0_), channel_id=1, source_target_pairs={{0,24},{4,28},{8,16},{12,20},{16,8},{20,12},{24,0},{28,4},{1,25},{... | collective-permute-start | bytes 196616 | tf_op jit(solution)/shard_map/ppermute | solution.py:394
  23.7 0.9 %collective-permute-start.8 = (bf16[32,1024]{1,0:T(8,128)(2,1)S(1)}, bf16[32,1024]{1,0:T(8,128)(2,1)S(1)}, u32[]{:S(2)}, u32[]{:S(2)}) collective-permute-start(bf16[32,1024]{1,0:T(8,128)(2,1)S(1)} %add_convert_fusion.refs_0_), channel_id=1, source_target_pairs={{0,16},{4,20},{8,24},{12,28},{16,0},{20,4},{24,8},{28,12},{1,17},{... | collective-permute-start | bytes 196616 | tf_op jit(solution)/shard_map/ppermute | solution.py:394
  24.6 1.2 %collective-permute-start.7 = (bf16[32,1024]{1,0:T(8,128)(2,1)S(1)}, bf16[32,1024]{1,0:T(8,128)(2,1)S(1)}, u32[]{:S(2)}, u32[]{:S(2)}) collective-permute-start(bf16[32,1024]{1,0:T(8,128)(2,1)S(1)} %add_convert_fusion.refs_0_), channel_id=1, source_target_pairs={{0,8},{4,12},{8,0},{12,4},{16,24},{20,28},{24,16},{28,20},{1,9},{5... | collective-permute-start | bytes 196616 | tf_op jit(solution)/shard_map/ppermute | solution.py:394
  25.8 1.9 %collective-permute-done.9.refs_3_ = bf16[32,1024]{1,0:T(8,128)(2,1)S(1)} collective-permute-done((bf16[32,1024]{1,0:T(8,128)(2,1)S(1)}, bf16[32,1024]{1,0:T(8,128)(2,1)S(1)}, u32[]{:S(2)}, u32[]{:S(2)}) %collective-permute-start.9) | collective-permute-done | bytes 65568 | tf_op jit(solution)/shard_map/ppermute | solution.py:394
  27.6 1.3 %collective-permute-done.8.refs_2_ = bf16[32,1024]{1,0:T(8,128)(2,1)S(1)} collective-permute-done((bf16[32,1024]{1,0:T(8,128)(2,1)S(1)}, bf16[32,1024]{1,0:T(8,128)(2,1)S(1)}, u32[]{:S(2)}, u32[]{:S(2)}) %collective-permute-start.8) | collective-permute-done | bytes 65568 | tf_op jit(solution)/shard_map/ppermute | solution.py:394
  28.9 0.0 collective-permute-done.7.refs_1_
  28.9 0.8 %last.1 = (f32[3,7,1024]{2,1,0:T(8,128)}, f32[64,128]{1,0:T(8,128)}) custom-call(bf16[32,1024]{1,0:T(8,128)(2,1)S(1)} %add_convert_fusion.refs_0_, bf16[32,1024]{1,0:T(8,128)(2,1)S(1)} %collective-permute-done.7.refs_1_, bf16[32,1024]{1,0:T(8,128)(2,1)S(1)} %collective-permute-done.8.refs_2_, bf16[32,1024]{1,0:T(8,128)(2,1)S(1)} %collective-permute-done.9.refs_3_), custom_call_target="tpu_custom_call" | custom-call | tf_op jit(solution)/shard_map/last/pallas_call | solution.py:535
  (11 shorter events, 0.0 us)
Async XLA Ops:
  0.6 11.9 %copy-start.1 = (bf16[128,1024]{1,0:T(8,128)(2,1)S(1)}, bf16[128,1024]{1,0:T(8,128)(2,1)}, u32[]{:S(2)}) copy-start(bf16[128,1024]{1,0:T(8,128)(2,1)} %k_ref.3) | copy-start | bytes 786436
  0.6 11.9 %copy-start.2 = (bf16[128,1024]{1,0:T(8,128)(2,1)S(1)}, bf16[128,1024]{1,0:T(8,128)(2,1)}, u32[]{:S(2)}) copy-start(bf16[128,1024]{1,0:T(8,128)(2,1)} %v_ref.3) | copy-start | bytes 786436
  0.7 11.9 %copy-start.3 = (bf16[128,1024]{1,0:T(8,128)(2,1)S(1)}, bf16[128,1024]{1,0:T(8,128)(2,1)}, u32[]{:S(2)}) copy-start(bf16[128,1024]{1,0:T(8,128)(2,1)} %up_ref.3) | copy-start | bytes 786436
  0.7 11.9 %copy-start = (bf16[128,1024]{1,0:T(8,128)(2,1)S(1)}, bf16[128,1024]{1,0:T(8,128)(2,1)}, u32[]{:S(2)}) copy-start(bf16[128,1024]{1,0:T(8,128)(2,1)} %q_ref.3) | copy-start | bytes 786436
  0.7 11.9 %collective-permute-start = (bf16[128,1024]{1,0:T(8,128)(2,1)}, bf16[128,1024]{1,0:T(8,128)(2,1)S(1)}, u32[]{:S(2)}, u32[]{:S(2)}) collective-permute-start(bf16[128,1024]{1,0:T(8,128)(2,1)} %k_ref.3), channel_id=1, source_target_pairs={{0,4},{4,8},{8,12},{12,16},{16,20},{20,24},{24,28},{28,0},{1,5},{5... | collective-permute-start | bytes 786440 | tf_op jit(solution)/shard_map/ppermute | solution.py:425
  1.2 11.4 %collective-permute-start.1 = (bf16[128,1024]{1,0:T(8,128)(2,1)}, bf16[128,1024]{1,0:T(8,128)(2,1)S(1)}, u32[]{:S(2)}, u32[]{:S(2)}) collective-permute-start(bf16[128,1024]{1,0:T(8,128)(2,1)} %v_ref.3), channel_id=1, source_target_pairs={{0,4},{4,8},{8,12},{12,16},{16,20},{20,24},{24,28},{28,0},{1,5},{5... | collective-permute-start | bytes 786440 | tf_op jit(solution)/shard_map/ppermute | solution.py:425
  5.0 4.8 %collective-permute-start.4 = (f32[64,128]{1,0:T(8,128)S(1)}, f32[64,128]{1,0:T(8,128)S(1)}, u32[]{:S(2)}, u32[]{:S(2)}) collective-permute-start(f32[64,128]{1,0:T(8,128)S(1)} %get-tuple-element.27), channel_id=1, source_target_pairs={{0,1},{1,0},{2,3},{3,2},{4,5},{5,4},{6,7},{7,6},{8,9},{9,8},{10,11... | collective-permute-start | bytes 98312 | tf_op jit(solution)/shard_map/ppermute | solution.py:394
  6.7 5.9 %collective-permute-start.2 = (bf16[16,1024]{1,0:T(8,128)(2,1)S(1)}, bf16[16,1024]{1,0:T(8,128)(2,1)S(1)}, u32[]{:S(2)}, u32[]{:S(2)}) collective-permute-start(bf16[16,1024]{1,0:T(8,128)(2,1)S(1)} %get-tuple-element.23), channel_id=1, source_target_pairs={{0,4},{4,8},{8,12},{12,16},{16,20},{20,24},{24,28},{28,0},{1,5},{5... | collective-permute-start | bytes 98312 | tf_op jit(solution)/shard_map/ppermute | solution.py:425
  6.7 5.9 %collective-permute-start.3 = (bf16[16,1024]{1,0:T(8,128)(2,1)S(1)}, bf16[16,1024]{1,0:T(8,128)(2,1)S(1)}, u32[]{:S(2)}, u32[]{:S(2)}) collective-permute-start(bf16[16,1024]{1,0:T(8,128)(2,1)S(1)} %get-tuple-element.24), channel_id=1, source_target_pairs={{0,8},{4,12},{8,16},{12,20},{16,24},{20,28},{24,0},{28,4},{1,9},{5... | collective-permute-start | bytes 98312 | tf_op jit(solution)/shard_map/ppermute | solution.py:425
  9.9 5.8 %collective-permute-start.5 = (f32[64,128]{1,0:T(8,128)S(1)}, f32[64,128]{1,0:T(8,128)S(1)}, u32[]{:S(2)}, u32[]{:S(2)}) collective-permute-start(f32[64,128]{1,0:T(8,128)S(1)} %add.6.rest_0_), channel_id=1, source_target_pairs={{0,2},{1,3},{2,0},{3,1},{4,6},{5,7},{6,4},{7,5},{8,10},{9,11},{10,... | collective-permute-start | bytes 98312 | tf_op jit(solution)/shard_map/ppermute | solution.py:394
  20.1 2.1 %collective-permute-start.6 = (f32[32,1024]{1,0:T(8,128)S(1)}, f32[32,1024]{1,0:T(8,128)S(1)}, u32[]{:S(2)}, u32[]{:S(2)}) collective-permute-start(f32[32,1024]{1,0:T(8,128)S(1)} %backward.1), channel_id=1, source_target_pairs={{0,4},{4,0},{8,12},{12,8},{16,20},{20,16},{24,28},{28,24},{1,5},{5... | collective-permute-start | bytes 393224 | tf_op jit(solution)/shard_map/ppermute | solution.py:394
  22.2 5.4 %collective-permute-start.9 = (bf16[32,1024]{1,0:T(8,128)(2,1)S(1)}, bf16[32,1024]{1,0:T(8,128)(2,1)S(1)}, u32[]{:S(2)}, u32[]{:S(2)}) collective-permute-start(bf16[32,1024]{1,0:T(8,128)(2,1)S(1)} %add_convert_fusion.refs_0_), channel_id=1, source_target_pairs={{0,24},{4,28},{8,16},{12,20},{16,8},{20,12},{24,0},{28,4},{1,25},{... | collective-permute-start | bytes 196616 | tf_op jit(solution)/shard_map/ppermute | solution.py:394
  23.7 5.2 %collective-permute-start.8 = (bf16[32,1024]{1,0:T(8,128)(2,1)S(1)}, bf16[32,1024]{1,0:T(8,128)(2,1)S(1)}, u32[]{:S(2)}, u32[]{:S(2)}) collective-permute-start(bf16[32,1024]{1,0:T(8,128)(2,1)S(1)} %add_convert_fusion.refs_0_), channel_id=1, source_target_pairs={{0,16},{4,20},{8,24},{12,28},{16,0},{20,4},{24,8},{28,12},{1,17},{... | collective-permute-start | bytes 196616 | tf_op jit(solution)/shard_map/ppermute | solution.py:394
  24.6 4.4 %collective-permute-start.7 = (bf16[32,1024]{1,0:T(8,128)(2,1)S(1)}, bf16[32,1024]{1,0:T(8,128)(2,1)S(1)}, u32[]{:S(2)}, u32[]{:S(2)}) collective-permute-start(bf16[32,1024]{1,0:T(8,128)(2,1)S(1)} %add_convert_fusion.refs_0_), channel_id=1, source_target_pairs={{0,8},{4,12},{8,0},{12,4},{16,24},{20,28},{24,16},{28,20},{1,9},{5... | collective-permute-start | bytes 196616 | tf_op jit(solution)/shard_map/ppermute | solution.py:394

commit v4 on v3

--- a/solution.py
+++ b/solution.py
@@ -1,4 +1,5 @@
 import functools
+import math
 
 import jax
 import jax.numpy as jnp
@@ -13,8 +14,6 @@
 PRE = 8
 SLOT = PRE + BLOCK
 LIMIT = 24 * 1024 * 1024
-MOST = 60 * 1024 * 1024
-TL, BD, FW = 1.5, 1.6, 3.0
 COPIES = 64
 F32 = jnp.float32
 BF16 = jnp.bfloat16
@@ -66,7 +65,7 @@
     h_out_ref,
     se_out_ref,
     up_here,
-    here,
+    k_here,
     lengths_here,
     reward_here,
     sems,
@@ -75,9 +74,9 @@
     tail = pl.ds(rows - TAIL, TAIL)
     pieces = (
         (up_ref, up_here),
-        (q_ref.at[tail], here.at[0]),
-        (k_ref.at[tail], here.at[1]),
-        (v_ref.at[tail], here.at[2]),
+        (v_ref, near_ref.at[pl.ds(0, rows)]),
+        (q_ref.at[tail], near_ref.at[pl.ds(rows, TAIL)]),
+        (k_ref.at[tail], k_here),
         (lengths_ref, lengths_here),
         (reward_ref, reward_here),
         (h_ref, h_out_ref),
@@ -88,17 +87,8 @@
     ]
     for copy in copies:
         copy.start()
-    copies[0].wait()
-    total = jnp.zeros((rows, LANES), F32)
-    for tile in range(channels // LANES):
-        part = up_here[:, tile * LANES : (tile + 1) * LANES].astype(F32)
-        total = total + part * part
-    sq_ref[...] = jnp.broadcast_to(jnp.sum(total.T, axis=0, keepdims=True), sq_ref.shape)
-    for copy in copies[1:]:
-        copy.wait()
-    tails = [here[i].astype(F32)[TAIL - PRE :] for i in range(3)]
-    near_ref[...] = here[0]
-    far_ref[...] = jnp.concatenate(tails[1:], axis=0).astype(BF16)
+    copies[4].wait()
+    copies[5].wait()
     own = rows // BLOCK
     window = span + own
     first = lax.axis_index("dp") * own
@@ -109,6 +99,16 @@
     for i, note in enumerate(notes):
         note_ref[i : i + 1] = jnp.full((1, rows), jnp.where(note, 1.0, 0.0).astype(F32))
     note_ref[len(notes) : len(notes) + 1] = reward_here[...].astype(F32) * 0.25
+    copies[0].wait()
+    total = jnp.zeros((rows, LANES), F32)
+    for tile in range(channels // LANES):
+        part = up_here[:, tile * LANES : (tile + 1) * LANES].astype(F32)
+        total = total + part * part
+    sq_ref[...] = jnp.broadcast_to(jnp.sum(total.T, axis=0, keepdims=True), sq_ref.shape)
+    for copy in copies[1:4] + copies[6:]:
+        copy.wait()
+    tails = [ref[...].astype(F32)[TAIL - PRE :] for ref in (k_here, near_ref.at[tail])]
+    far_ref[...] = jnp.concatenate(tails, axis=0).astype(BF16)
 
 
 def band_kernel(h_ref, band_ref, band_t_ref, row_ref):
@@ -121,8 +121,8 @@
     flip = jnp.where(tap + lane == taps, 1.0, 0.0).astype(F32)
     row_ref[...] = dot(h_ref[...], flip.astype(BF16), ((1,), (0,)))
 
-    def one(tile, carry):
-        rows = row_ref[pl.ds(pl.multiple_of(tile * per_tile, per_tile), per_tile), :]
+    for tile in range(tiles):
+        rows = row_ref[tile * per_tile : (tile + 1) * per_tile]
         parts = [
             pltpu.roll(
                 jnp.broadcast_to(rows[g : g + 1], (BLOCK, width)), 0, 1, stride=1, stride_axis=0
@@ -131,10 +131,7 @@
         ]
         band = jnp.concatenate(parts, axis=0)
         band_ref[tile] = band.astype(BF16)
-        band_t_ref[tile] = band.T[0 : taps + BLOCK].astype(BF16)
-        return carry
-
-    lax.fori_loop(0, tiles, one, 0)
+        band_t_ref[tile] = band.astype(BF16).T[0 : taps + BLOCK]
 
 
 def notes_of(note_ref, own, span):
@@ -173,23 +170,60 @@
     lax.fori_loop(0, count // beside, some, 0)
 
 
+def blocks_of(ref, at, start, count):
+    return [ref[start + BLOCK * b : start + BLOCK * (b + 1), at].astype(F32) for b in range(count)]
+
+
+def fill(x_ref, tile, pieces, before, joined):
+    for b, piece in enumerate(pieces):
+        at = SLOT * b
+        x_ref[tile, at : at + PRE] = before * joined[b]
+        x_ref[tile, at + PRE : at + SLOT] = piece
+        before = piece[BLOCK - PRE :]
+
+
+def short(x_ref, tile, b, taps_now):
+    total = taps_now[0:1] * shifted(x_ref, tile, b, 0)
+    for j in range(1, taps_now.shape[0]):
+        total = total + taps_now[j : j + 1] * shifted(x_ref, tile, b, j)
+    return total
+
+
+def key_kernel(beside, k_ref, k_near_ref, note_ref, se_ref, xk_ref, ks_ref):
+    rows, channels = k_ref.shape
+    own = rows // BLOCK
+    later = xk_ref.shape[1] // SLOT
+    span = later + 1 - own
+    joined, _, _ = notes_of(note_ref, own, span)
+
+    def filters(tile, side, _):
+        at = tile_lanes(tile)
+        k_taps = se_ref[1, :, at].astype(F32)
+        halo = blocks_of(k_near_ref, at, rows - span * BLOCK, span)
+        before = halo[0][BLOCK - PRE :]
+        fill(xk_ref, tile, halo[1:] + blocks_of(k_ref, at, 0, own), before, joined[1:])
+        for b in range(later):
+            ks_ref[tile, BLOCK * b : BLOCK * (b + 1)] = short(xk_ref, tile, b, k_taps)
+
+    in_groups(channels // LANES, beside, (filters,))
+
+
 def forward_kernel(
     beside,
     q_ref,
-    k_ref,
     v_ref,
     up_ref,
     k_near_ref,
-    v_near_ref,
     near_ref,
     far_ref,
     note_ref,
     se_ref,
     band_ref,
+    ks_ref,
     xq_ref,
     xk_ref,
     xv_ref,
-    ks_ref,
+    ks_first_ref,
     vs_ref,
     zw_ref,
     uq_ref,
@@ -198,53 +232,33 @@
 ):
     rows, channels = q_ref.shape
     own = rows // BLOCK
-    window = xk_ref.shape[1] // SLOT
+    window = xv_ref.shape[1] // SLOT
     span = window - own
     tiles = channels // LANES
     per_tile = band_ref.shape[1] // BLOCK
-    tap_count = se_ref.shape[1]
     joined, same, _ = notes_of(note_ref, own, span)
     picks = lane_picks(per_tile)
     for side in range(beside):
         z_ref[side, window * BLOCK :] = jnp.zeros((z_ref.shape[1] - window * BLOCK, LANES), BF16)
 
-    def fill(x_ref, tile, pieces, before, first_block):
-        for b, piece in enumerate(pieces):
-            at = SLOT * b
-            x_ref[tile, at : at + PRE] = before * joined[first_block + b]
-            x_ref[tile, at + PRE : at + SLOT] = piece
-            before = piece[BLOCK - PRE :]
-
-    def short(x_ref, tile, b, taps_now):
-        total = taps_now[0:1] * shifted(x_ref, tile, b, 0)
-        for j in range(1, tap_count):
-            total = total + taps_now[j : j + 1] * shifted(x_ref, tile, b, j)
-        return total
-
     def filters(tile, side, _):
         at = tile_lanes(tile)
-        q_taps = se_ref[0, :, at].astype(F32)
-        k_taps = se_ref[1, :, at].astype(F32)
-        v_taps = se_ref[2, :, at].astype(F32)
-
-        def blocks_of(ref, start, count):
-            return [
-                ref[start + BLOCK * b : start + BLOCK * (b + 1), at].astype(F32) for b in range(count)
-            ]
-
-        q_before = near_ref[:, at].astype(F32)[TAIL - PRE :]
+        q_taps, k_taps, v_taps = (se_ref[i, :, at].astype(F32) for i in range(3))
+        q_before = near_ref[rows:, at].astype(F32)[TAIL - PRE :]
         k_before, v_before = jnp.split(far_ref[:, at].astype(F32), 2)
-        k_halo = blocks_of(k_near_ref, rows - span * BLOCK, span)
-        v_halo = blocks_of(v_near_ref, rows - span * BLOCK, span)
-        fill(xk_ref, tile, k_halo + blocks_of(k_ref, 0, own), k_before, 0)
-        fill(xv_ref, tile, v_halo + blocks_of(v_ref, 0, own), v_before, 0)
-        fill(xq_ref, tile, blocks_of(q_ref, 0, own), q_before, span)
+        v_halo = blocks_of(near_ref, at, rows - span * BLOCK, span)
+        fill(xv_ref, tile, v_halo + blocks_of(v_ref, at, 0, own), v_before, joined)
+        fill(xk_ref, tile, blocks_of(k_near_ref, at, rows - span * BLOCK, 1), k_before, joined)
+        fill(xq_ref, tile, blocks_of(q_ref, at, 0, own), q_before, joined[span:])
         for b in range(window):
             at_b = slice(BLOCK * b, BLOCK * (b + 1))
-            ks = short(xk_ref, tile, b, k_taps)
             vs = short(xv_ref, tile, b, v_taps)
-            ks_ref[tile, at_b] = ks
             vs_ref[tile, at_b] = vs
+            if b == 0:
+                ks = short(xk_ref, tile, b, k_taps)
+                ks_first_ref[tile] = ks
+            else:
+                ks = ks_ref[tile, BLOCK * (b - 1) : BLOCK * b]
             z_ref[side, at_b] = (ks * vs).astype(BF16)
         for n in range(own):
             at_n = slice(BLOCK * n, BLOCK * (n + 1))
@@ -277,10 +291,12 @@
     all_channels,
     beside,
     count,
+    xk_ref,
+    ks_ref,
     xq_ref,
-    xk_ref,
+    xk_first_ref,
     xv_ref,
-    ks_ref,
+    ks_first_ref,
     vs_ref,
     zw_ref,
     uq_ref,
@@ -292,7 +308,7 @@
     *sq_refs, out_ref, dm_ref, dz_ref, skew_ref, w_ref = rest
     tiles, rows = uq_ref.shape[0:2]
     own = rows // BLOCK
-    window = xk_ref.shape[1] // SLOT
+    window = xv_ref.shape[1] // SLOT
     span = window - own
     per_tile = band_t_ref.shape[2] // BLOCK
     _, same, reward = notes_of(note_ref, own, span)
@@ -351,9 +367,11 @@
             at_b = slice(BLOCK * b, BLOCK * (b + 1))
             dz = dz_ref[side, at_b]
             cot_k = dz * vs_ref[tile, at_b]
-            cot_v = dz * ks_ref[tile, at_b]
+            ks = ks_ref[tile, BLOCK * (b - 1) : BLOCK * b] if b else ks_first_ref[tile]
+            cot_v = dz * ks
             for j in range(count):
-                gk[j] = gk[j] + fold(cot_k * shifted(xk_ref, tile, b, j))
+                k_rows = shifted(xk_ref, tile, b - 1, j) if b else shifted(xk_first_ref, tile, 0, j)
+                gk[j] = gk[j] + fold(cot_k * k_rows)
                 gv[j] = gv[j] + fold(cot_v * shifted(xv_ref, tile, b, j))
         for i, sums in enumerate((gq, gk, gv)):
             for j in range(count):
@@ -435,15 +453,14 @@
     own = rows // BLOCK
     span = taps // BLOCK
     window = own + span
-    beside = 2 if tiles % 2 == 0 else 1
+    beside = math.gcd(tiles, 8)
     dp = lax.axis_size("dp")
 
     k_near = moved_up(key, "dp", 1)
-    v_near = moved_up(value, "dp", 1)
     near, far, sq, notes, medium_taps, short_taps = pl.pallas_call(
         functools.partial(first_kernel, span),
         out_shape=(
-            jax.ShapeDtypeStruct((TAIL, channels), BF16),
+            jax.ShapeDtypeStruct((rows + TAIL, channels), BF16),
             jax.ShapeDtypeStruct((2 * PRE, channels), BF16),
             jax.ShapeDtypeStruct((COPIES, rows), F32),
             jax.ShapeDtypeStruct((window + own * span + 1, rows), F32),
@@ -454,13 +471,13 @@
         out_specs=(spec(),) * 6,
         scratch_shapes=[
             pltpu.VMEM((rows, channels), BF16),
-            pltpu.VMEM((3, TAIL, channels), BF16),
+            pltpu.VMEM((TAIL, channels), BF16),
             pltpu.SMEM(lengths.shape, jnp.int32),
             pltpu.VMEM((1, rows), jnp.int32),
             pltpu.SemaphoreType.DMA((8,)),
         ],
         compiler_params=pltpu.CompilerParams(vmem_limit_bytes=LIMIT),
-        cost_estimate=cost(TL),
+        cost_estimate=cost(1.2),
         name="first",
     )(
         *[
@@ -490,36 +507,48 @@
         out_specs=(spec(),) * 2,
         scratch_shapes=[pltpu.VMEM((groups, 2 * LANES), F32)],
         compiler_params=pltpu.CompilerParams(vmem_limit_bytes=LIMIT),
-        cost_estimate=cost(BD),
+        cost_estimate=cost(1.0),
         name="band",
     )(medium_taps)
 
-    squares, (band, band_t) = summed_small(sq, "fsdp", (band, band_t))
+    keys = pl.pallas_call(
+        functools.partial(key_kernel, beside),
+        out_shape=(
+            jax.ShapeDtypeStruct((tiles, (window - 1) * SLOT, LANES), F32),
+            jax.ShapeDtypeStruct((tiles, (window - 1) * BLOCK, LANES), F32),
+        ),
+        in_specs=[spec()] * 4,
+        out_specs=(spec(),) * 2,
+        compiler_params=pltpu.CompilerParams(vmem_limit_bytes=LIMIT),
+        cost_estimate=cost(0.5),
+        name="keys",
+    )(key, k_near, notes, short_taps)
+    squares, (band, band_t, keys) = summed_small(sq, "fsdp", (band, band_t, keys))
     kept = pl.pallas_call(
         functools.partial(forward_kernel, beside),
         out_shape=(
             jax.ShapeDtypeStruct((tiles, own * SLOT, LANES), F32),
+            jax.ShapeDtypeStruct((tiles, SLOT, LANES), F32),
             jax.ShapeDtypeStruct((tiles, window * SLOT, LANES), F32),
-            jax.ShapeDtypeStruct((tiles, window * SLOT, LANES), F32),
-            jax.ShapeDtypeStruct((tiles, window * BLOCK, LANES), F32),
+            jax.ShapeDtypeStruct((tiles, BLOCK, LANES), F32),
             jax.ShapeDtypeStruct((tiles, window * BLOCK, LANES), F32),
             jax.ShapeDtypeStruct((tiles, own // 2, 2 * LANES, 2 * LANES), BF16),
             jax.ShapeDtypeStruct((tiles, rows, LANES), F32),
             jax.ShapeDtypeStruct((tiles, rows, LANES), F32),
         ),
-        in_specs=[spec()] * 11,
+        in_specs=[spec()] * 10,
         out_specs=(spec(),) * 8,
         scratch_shapes=[pltpu.VMEM((beside, (own - 1) * BLOCK + 2 * LANES, LANES), BF16)],
         compiler_params=pltpu.CompilerParams(vmem_limit_bytes=LIMIT),
-        cost_estimate=cost(FW),
+        cost_estimate=cost(2.0),
         name="forward",
-    )(query, key, value, upstream, k_near, v_near, near, far, notes, short_taps, band)
+    )(query, value, upstream, k_near, near, far, notes, short_taps, band, keys[1])
     part = pl.pallas_call(
         functools.partial(
             backward_kernel, float(channels * lax.axis_size("fsdp")), beside, tap_count
         ),
         out_shape=jax.ShapeDtypeStruct((24 + per_tile, channels), F32),
-        in_specs=[spec()] * (10 + len(squares)),
+        in_specs=[spec()] * (12 + len(squares)),
         out_specs=spec(),
         scratch_shapes=[
             pltpu.VMEM((beside, own // 2, stack, 2 * LANES), BF16),
@@ -529,7 +558,7 @@
         ],
         compiler_params=pltpu.CompilerParams(vmem_limit_bytes=LIMIT),
         name="backward",
-    )(*kept, notes, band_t, *squares)
+    )(*keys, *kept, notes, band_t, *squares)
 
     parts = spread(part, "dp")
     grad_se, grad_mr = pl.pallas_call(

time: 29.9 us -> 27.5 us (0.920)
  Pallas kernels: 11.2 us -> 8.8 us
  starting transfers between devices: 13.6 us -> 12.5 us
  waiting for transfers between devices: 4.16 us -> 5.26 us
    pallas_call x1, Pallas kernels: 3.11 us -> 1.98 us  [on_device(): pl.pallas_call(functools.partial(forward_kernel, beside), out_shape=(jax....]
    ppermute x6, waiting for transfers between devices: 4.15 us -> 5.25 us  [swapped(): return lax.ppermute(value, axis, [(i, i ^ distance) for i in range(count)])]
    ppermute x6, starting transfers between devices: 8.94 us -> 7.88 us  [swapped(): return lax.ppermute(value, axis, [(i, i ^ distance) for i in range(count)])]
    pallas_call x1, Pallas kernels: 4.37 us -> 3.4 us  [on_device(): pl.pallas_call(functools.partial(backward_kernel, float(channels * lax.ax...]
    pallas_call x1, Pallas kernels: 1.66 us -> 0.96 us  [on_device(): pl.pallas_call(band_kernel, out_shape=(jax.ShapeDtypeStruct((tiles, stack...]
    pallas_call x0 -> x1, Pallas kernels: none -> 0.51 us  [on_device(): pl.pallas_call(functools.partial(key_kernel, beside), out_shape=(jax.Shap...]
    ppermute x4 -> x3, starting transfers between devices: 4.63 us -> 4.65 us  [moved_up(): lax.ppermute(value, axis, [(i, (i + steps) % count) for i in range(count)])]
  transfers between devices with their start and end apart: 10 -> 9, of which waited for: 3 -> 5; matrix products, arithmetic and copies ran while one was open for 0% -> 0% of each run, Pallas kernels for 20% -> 17%
where the time goes in v4:
time: 27.5 us; the launch traced here: 27.4 us
  starting transfers between devices  12.5 us (45%)
  Pallas kernels  8.8 us (32%)
  waiting for transfers between devices  5.26 us (19%)
  between operations  0.76 us (3%)
    ppermute x6, starting transfers between devices, swapped(): return lax.ppermute(value, axis, [(i, i ^ distance) for i in range(count)])  7.88 us
    ppermute x6, waiting for transfers between devices, swapped(): return lax.ppermute(value, axis, [(i, i ^ distance) for i in range(count)])  5.25 us
    ppermute x3, starting transfers between devices, moved_up(): lax.ppermute(value, axis, [(i, (i + steps) % count) for i in range(count)])  4.65 us
    pallas_call x1, Pallas kernels, on_device(): pl.pallas_call(functools.partial(backward_kernel, float(channels * lax.ax...  3.4 us
    pallas_call x1, Pallas kernels, on_device(): pl.pallas_call(functools.partial(forward_kernel, beside), out_shape=(jax....  1.98 us
    pallas_call x1, Pallas kernels, on_device(): pl.pallas_call(functools.partial(first_kernel, span), out_shape=(jax.Shap...  1.16 us
    pallas_call x1, Pallas kernels, on_device(): pl.pallas_call(band_kernel, out_shape=(jax.ShapeDtypeStruct((tiles, stack...  0.96 us
    pallas_call x1, Pallas kernels, on_device(): pl.pallas_call(functools.partial(last_kernel, 1.0 / rows), out_shape=(jax...  0.8 us
  transfers between devices with their start and end apart: 9, of which 5 were waited for; matrix products, arithmetic and copies ran while one was open for 0% of the time, Pallas kernels for 17%

profile of v4, /device:TPU:0, one launch (start us, length us, event | category | flops | bytes accessed | tf_op | source)
XLA Modules:
  0.0 27.4 jit_solution(11205501942826977050)
XLA Ops:
  0.7 0.5 %collective-permute-start.1 = (bf16[128,1024]{1,0:T(8,128)(2,1)}, bf16[128,1024]{1,0:T(8,128)(2,1)S(1)}, u32[]{:S(2)}, u32[]{:S(2)}) collective-permute-start(bf16[128,1024]{1,0:T(8,128)(2,1)} %k_ref.3), channel_id=1, source_target_pairs={{0,4},{4,8},{8,12},{12,16},{16,20},{20,24},{24,28},{28,0},{1,5},{5... | collective-permute-start | bytes 786440 | tf_op jit(solution)/shard_map/ppermute | solution.py:443
  1.2 1.2 %first.1 = (bf16[144,1024]{1,0:T(8,128)(2,1)S(1)}, bf16[16,1024]{1,0:T(8,128)(2,1)S(1)}, f32[64,128]{1,0:T(8,128)S(1)}, f32[25,128]{1,0:T(8,128)S(1)}, bf16[64,1...) custom-call(s32[4]{0:T(128)} %lengths_ref.1, s32[1,128]{1,0:T(1,128)} %bitcast.4, bf16[128,1024]{1,0:T(8,128)(2,1)} %q_ref.3, ...), custom_call_target="tpu_custom_call" | custom-call | flops 1 | bytes 4320000 | tf_op jit(solution)/shard_map/first/pallas_call | solution.py:460
  2.3 2.7 %collective-permute-start.2 = (bf16[144,1024]{1,0:T(8,128)(2,1)S(1)}, bf16[144,1024]{1,0:T(8,128)(2,1)S(1)}, u32[]{:S(2)}, u32[]{:S(2)}) collective-permute-start(bf16[144,1024]{1,0:T(8,128)(2,1)S(1)} %get-tuple-element.37), channel_id=1, source_target_pairs={{0,4},{4,8},{8,12},{12,16},{16,20},{20,24},{24,28},{28,0},{1,5},{5... | collective-permute-start | bytes 884744 | tf_op jit(solution)/shard_map/ppermute | solution.py:443
  5.0 1.6 %collective-permute-start = (f32[64,128]{1,0:T(8,128)S(1)}, f32[64,128]{1,0:T(8,128)S(1)}, u32[]{:S(2)}, u32[]{:S(2)}) collective-permute-start(f32[64,128]{1,0:T(8,128)S(1)} %get-tuple-element.27), channel_id=1, source_target_pairs={{0,1},{1,0},{2,3},{3,2},{4,5},{5,4},{6,7},{7,6},{8,9},{9,8},{10,11... | collective-permute-start | bytes 98312 | tf_op jit(solution)/shard_map/ppermute | solution.py:412
  6.6 1.5 %collective-permute-start.3 = (bf16[16,1024]{1,0:T(8,128)(2,1)S(1)}, bf16[16,1024]{1,0:T(8,128)(2,1)S(1)}, u32[]{:S(2)}, u32[]{:S(2)}) collective-permute-start(bf16[16,1024]{1,0:T(8,128)(2,1)S(1)} %get-tuple-element.38), channel_id=1, source_target_pairs={{0,8},{4,12},{8,16},{12,20},{16,24},{20,28},{24,0},{28,4},{1,9},{5... | collective-permute-start | bytes 98312 | tf_op jit(solution)/shard_map/ppermute | solution.py:443
  8.1 1.0 %band.1 = (bf16[8,256,256]{2,1,0:T(8,128)(2,1)S(1)}, bf16[8,160,256]{2,1,0:T(8,128)(2,1)S(1)}) custom-call(bf16[64,128]{1,0:T(8,128)(2,1)S(1)} %get-tuple-element.28.h_ref), custom_call_target="tpu_custom_call" | custom-call | flops 1 | bytes 3600000 | tf_op jit(solution)/shard_map/band/pallas_call | solution.py:500
  9.0 0.0 collective-permute-done.1.k_near_ref
  9.1 0.5 %keys.1 = (f32[8,280,128]{2,1,0:T(8,128)S(1)}, f32[8,224,128]{2,1,0:T(8,128)S(1)}) custom-call(bf16[128,1024]{1,0:T(8,128)(2,1)S(1)} %copy-done, bf16[128,1024]{1,0:T(8,128)(2,1)S(1)} %collective-permute-done.1.k_near_ref, f32[25,128]{1,0:T(8,128)S(1)} %get-tuple-element.31.note_ref, bf16[3,7,1024]{2,1,0:T(8,128)(2,1)S(1)} %get-tuple-element.32.se_ref), custom_call_target="tpu_custom_call" | custom-call | flops 1 | bytes 1800000 | tf_op jit(solution)/shard_map/keys/pallas_call | solution.py:514
  9.6 0.0 collective-permute-done
  9.6 2.7 %collective-permute-start.4 = (f32[64,128]{1,0:T(8,128)S(1)}, f32[64,128]{1,0:T(8,128)S(1)}, u32[]{:S(2)}, u32[]{:S(2)}) collective-permute-start(f32[64,128]{1,0:T(8,128)S(1)} %add.6.rest_0_), channel_id=1, source_target_pairs={{0,2},{1,3},{2,0},{3,1},{4,6},{5,7},{6,4},{7,5},{8,10},{9,11},{10,... | collective-permute-start | bytes 98312 | tf_op jit(solution)/shard_map/ppermute | solution.py:412
  12.3 0.0 collective-permute-done.3.far_ref
  12.3 0.0 collective-permute-done.2.near_ref
  12.3 2.0 %forward.1 = (f32[8,160,128]{2,1,0:T(8,128)S(1)}, f32[8,40,128]{2,1,0:T(8,128)S(1)}, f32[8,320,128]{2,1,0:T(8,128)S(1)}, f32[8,32,128]{2,1,0:T(8,128)S(1)}, f32[...) custom-call(bf16[128,1024]{1,0:T(8,128)(2,1)S(1)} %copy-done.1, ...), custom_call_target="tpu_custom_call" | custom-call | flops 1 | bytes 7200000 | tf_op jit(solution)/shard_map/forward/pallas_call | solution.py:527
  14.3 0.2 collective-permute-done.4.rest_1_
  14.5 3.4 %backward.1 = f32[32,1024]{1,0:T(8,128)S(1)} custom-call(f32[8,280,128]{2,1,0:T(8,128)S(1)} %get-tuple-element.35.xk_ref, f32[8,224,128]{2,1,0:T(8,128)S(1)} %get-tuple-element.36.ks_ref, f32[8,160,128]{2,1,0:T(8,128)S(1)} %get-tuple-element.40.xq_ref, f32[8,40,128]{2,1,0:T(8,128)S(1)} %get-tuple-element.41.xk_first_ref, ...), custom_call_target="tpu_custom_call" | custom-call | tf_op jit(solution)/shard_map/backward/pallas_call | solution.py:546
  17.9 0.1 collective-permute-start.5
  17.9 1.3 %collective-permute-done.5 = f32[32,1024]{1,0:T(8,128)S(1)} collective-permute-done((f32[32,1024]{1,0:T(8,128)S(1)}, f32[32,1024]{1,0:T(8,128)S(1)}, u32[]{:S(2)}, u32[]{:S(2)}) %collective-permute-start.5) | collective-permute-done | bytes 131104 | tf_op jit(solution)/shard_map/ppermute | solution.py:412
  19.3 1.7 %collective-permute-start.8 = (bf16[32,1024]{1,0:T(8,128)(2,1)S(1)}, bf16[32,1024]{1,0:T(8,128)(2,1)S(1)}, u32[]{:S(2)}, u32[]{:S(2)}) collective-permute-start(bf16[32,1024]{1,0:T(8,128)(2,1)S(1)} %add_convert_fusion.refs_0_), channel_id=1, source_target_pairs={{0,24},{4,28},{8,16},{12,20},{16,8},{20,12},{24,0},{28,4},{1,25},{... | collective-permute-start | bytes 196616 | tf_op jit(solution)/shard_map/ppermute | solution.py:412
  21.0 1.3 %collective-permute-start.7 = (bf16[32,1024]{1,0:T(8,128)(2,1)S(1)}, bf16[32,1024]{1,0:T(8,128)(2,1)S(1)}, u32[]{:S(2)}, u32[]{:S(2)}) collective-permute-start(bf16[32,1024]{1,0:T(8,128)(2,1)S(1)} %add_convert_fusion.refs_0_), channel_id=1, source_target_pairs={{0,16},{4,20},{8,24},{12,28},{16,0},{20,4},{24,8},{28,12},{1,17},{... | collective-permute-start | bytes 196616 | tf_op jit(solution)/shard_map/ppermute | solution.py:412
  22.3 0.5 %collective-permute-start.6 = (bf16[32,1024]{1,0:T(8,128)(2,1)S(1)}, bf16[32,1024]{1,0:T(8,128)(2,1)S(1)}, u32[]{:S(2)}, u32[]{:S(2)}) collective-permute-start(bf16[32,1024]{1,0:T(8,128)(2,1)S(1)} %add_convert_fusion.refs_0_), channel_id=1, source_target_pairs={{0,8},{4,12},{8,0},{12,4},{16,24},{20,28},{24,16},{28,20},{1,9},{5... | collective-permute-start | bytes 196616 | tf_op jit(solution)/shard_map/ppermute | solution.py:412
  22.9 1.7 %collective-permute-done.8.refs_3_ = bf16[32,1024]{1,0:T(8,128)(2,1)S(1)} collective-permute-done((bf16[32,1024]{1,0:T(8,128)(2,1)S(1)}, bf16[32,1024]{1,0:T(8,128)(2,1)S(1)}, u32[]{:S(2)}, u32[]{:S(2)}) %collective-permute-start.8) | collective-permute-done | bytes 65568 | tf_op jit(solution)/shard_map/ppermute | solution.py:412
  24.6 1.2 %collective-permute-done.7.refs_2_ = bf16[32,1024]{1,0:T(8,128)(2,1)S(1)} collective-permute-done((bf16[32,1024]{1,0:T(8,128)(2,1)S(1)}, bf16[32,1024]{1,0:T(8,128)(2,1)S(1)}, u32[]{:S(2)}, u32[]{:S(2)}) %collective-permute-start.7) | collective-permute-done | bytes 65568 | tf_op jit(solution)/shard_map/ppermute | solution.py:412
  25.8 0.8 %collective-permute-done.6.refs_1_ = bf16[32,1024]{1,0:T(8,128)(2,1)S(1)} collective-permute-done((bf16[32,1024]{1,0:T(8,128)(2,1)S(1)}, bf16[32,1024]{1,0:T(8,128)(2,1)S(1)}, u32[]{:S(2)}, u32[]{:S(2)}) %collective-permute-start.6) | collective-permute-done | bytes 65568 | tf_op jit(solution)/shard_map/ppermute | solution.py:412
  26.6 0.8 %last.1 = (f32[3,7,1024]{2,1,0:T(8,128)}, f32[64,128]{1,0:T(8,128)}) custom-call(bf16[32,1024]{1,0:T(8,128)(2,1)S(1)} %add_convert_fusion.refs_0_, bf16[32,1024]{1,0:T(8,128)(2,1)S(1)} %collective-permute-done.6.refs_1_, bf16[32,1024]{1,0:T(8,128)(2,1)S(1)} %collective-permute-done.7.refs_2_, bf16[32,1024]{1,0:T(8,128)(2,1)S(1)} %collective-permute-done.8.refs_3_), custom_call_target="tpu_custom_call" | custom-call | tf_op jit(solution)/shard_map/last/pallas_call | solution.py:564
  (10 shorter events, 0.0 us)
Async XLA Ops:
  0.6 8.4 %copy-start = (bf16[128,1024]{1,0:T(8,128)(2,1)S(1)}, bf16[128,1024]{1,0:T(8,128)(2,1)}, u32[]{:S(2)}) copy-start(bf16[128,1024]{1,0:T(8,128)(2,1)} %k_ref.3) | copy-start | bytes 786436
  0.6 11.6 %copy-start.3 = (bf16[128,1024]{1,0:T(8,128)(2,1)S(1)}, bf16[128,1024]{1,0:T(8,128)(2,1)}, u32[]{:S(2)}) copy-start(bf16[128,1024]{1,0:T(8,128)(2,1)} %up_ref.3) | copy-start | bytes 786436
  0.7 11.6 %copy-start.2 = (bf16[128,1024]{1,0:T(8,128)(2,1)S(1)}, bf16[128,1024]{1,0:T(8,128)(2,1)}, u32[]{:S(2)}) copy-start(bf16[128,1024]{1,0:T(8,128)(2,1)} %v_ref.3) | copy-start | bytes 786436
  0.7 11.6 %copy-start.1 = (bf16[128,1024]{1,0:T(8,128)(2,1)S(1)}, bf16[128,1024]{1,0:T(8,128)(2,1)}, u32[]{:S(2)}) copy-start(bf16[128,1024]{1,0:T(8,128)(2,1)} %q_ref.3) | copy-start | bytes 786436
  0.7 8.4 %collective-permute-start.1 = (bf16[128,1024]{1,0:T(8,128)(2,1)}, bf16[128,1024]{1,0:T(8,128)(2,1)S(1)}, u32[]{:S(2)}, u32[]{:S(2)}) collective-permute-start(bf16[128,1024]{1,0:T(8,128)(2,1)} %k_ref.3), channel_id=1, source_target_pairs={{0,4},{4,8},{8,12},{12,16},{16,20},{20,24},{24,28},{28,0},{1,5},{5... | collective-permute-start | bytes 786440 | tf_op jit(solution)/shard_map/ppermute | solution.py:443
  2.3 9.9 %collective-permute-start.2 = (bf16[144,1024]{1,0:T(8,128)(2,1)S(1)}, bf16[144,1024]{1,0:T(8,128)(2,1)S(1)}, u32[]{:S(2)}, u32[]{:S(2)}) collective-permute-start(bf16[144,1024]{1,0:T(8,128)(2,1)S(1)} %get-tuple-element.37), channel_id=1, source_target_pairs={{0,4},{4,8},{8,12},{12,16},{16,20},{20,24},{24,28},{28,0},{1,5},{5... | collective-permute-start | bytes 884744 | tf_op jit(solution)/shard_map/ppermute | solution.py:443
  5.0 4.6 %collective-permute-start = (f32[64,128]{1,0:T(8,128)S(1)}, f32[64,128]{1,0:T(8,128)S(1)}, u32[]{:S(2)}, u32[]{:S(2)}) collective-permute-start(f32[64,128]{1,0:T(8,128)S(1)} %get-tuple-element.27), channel_id=1, source_target_pairs={{0,1},{1,0},{2,3},{3,2},{4,5},{5,4},{6,7},{7,6},{8,9},{9,8},{10,11... | collective-permute-start | bytes 98312 | tf_op jit(solution)/shard_map/ppermute | solution.py:412
  6.6 5.7 %collective-permute-start.3 = (bf16[16,1024]{1,0:T(8,128)(2,1)S(1)}, bf16[16,1024]{1,0:T(8,128)(2,1)S(1)}, u32[]{:S(2)}, u32[]{:S(2)}) collective-permute-start(bf16[16,1024]{1,0:T(8,128)(2,1)S(1)} %get-tuple-element.38), channel_id=1, source_target_pairs={{0,8},{4,12},{8,16},{12,20},{16,24},{20,28},{24,0},{28,4},{1,9},{5... | collective-permute-start | bytes 98312 | tf_op jit(solution)/shard_map/ppermute | solution.py:443
  9.6 4.9 %collective-permute-start.4 = (f32[64,128]{1,0:T(8,128)S(1)}, f32[64,128]{1,0:T(8,128)S(1)}, u32[]{:S(2)}, u32[]{:S(2)}) collective-permute-start(f32[64,128]{1,0:T(8,128)S(1)} %add.6.rest_0_), channel_id=1, source_target_pairs={{0,2},{1,3},{2,0},{3,1},{4,6},{5,7},{6,4},{7,5},{8,10},{9,11},{10,... | collective-permute-start | bytes 98312 | tf_op jit(solution)/shard_map/ppermute | solution.py:412
  17.9 1.4 %collective-permute-start.5 = (f32[32,1024]{1,0:T(8,128)S(1)}, f32[32,1024]{1,0:T(8,128)S(1)}, u32[]{:S(2)}, u32[]{:S(2)}) collective-permute-start(f32[32,1024]{1,0:T(8,128)S(1)} %backward.1), channel_id=1, source_target_pairs={{0,4},{4,0},{8,12},{12,8},{16,20},{20,16},{24,28},{28,24},{1,5},{5... | collective-permute-start | bytes 393224 | tf_op jit(solution)/shard_map/ppermute | solution.py:412
  19.3 5.3 %collective-permute-start.8 = (bf16[32,1024]{1,0:T(8,128)(2,1)S(1)}, bf16[32,1024]{1,0:T(8,128)(2,1)S(1)}, u32[]{:S(2)}, u32[]{:S(2)}) collective-permute-start(bf16[32,1024]{1,0:T(8,128)(2,1)S(1)} %add_convert_fusion.refs_0_), channel_id=1, source_target_pairs={{0,24},{4,28},{8,16},{12,20},{16,8},{20,12},{24,0},{28,4},{1,25},{... | collective-permute-start | bytes 196616 | tf_op jit(solution)/shard_map/ppermute | solution.py:412
  21.0 4.8 %collective-permute-start.7 = (bf16[32,1024]{1,0:T(8,128)(2,1)S(1)}, bf16[32,1024]{1,0:T(8,128)(2,1)S(1)}, u32[]{:S(2)}, u32[]{:S(2)}) collective-permute-start(bf16[32,1024]{1,0:T(8,128)(2,1)S(1)} %add_convert_fusion.refs_0_), channel_id=1, source_target_pairs={{0,16},{4,20},{8,24},{12,28},{16,0},{20,4},{24,8},{28,12},{1,17},{... | collective-permute-start | bytes 196616 | tf_op jit(solution)/shard_map/ppermute | solution.py:412
  22.3 4.3 %collective-permute-start.6 = (bf16[32,1024]{1,0:T(8,128)(2,1)S(1)}, bf16[32,1024]{1,0:T(8,128)(2,1)S(1)}, u32[]{:S(2)}, u32[]{:S(2)}) collective-permute-start(bf16[32,1024]{1,0:T(8,128)(2,1)S(1)} %add_convert_fusion.refs_0_), channel_id=1, source_target_pairs={{0,8},{4,12},{8,0},{12,4},{16,24},{20,28},{24,16},{28,20},{1,9},{5... | collective-permute-start | bytes 196616 | tf_op jit(solution)/shard_map/ppermute | solution.py:412

commit v5 on v4

--- a/solution.py
+++ b/solution.py
@@ -159,6 +159,20 @@
     return pl.ds(pl.multiple_of(tile * LANES, LANES), LANES)
 
 
+def window_of(z_ref, tile, n, same):
+    span = len(same[n])
+    pieces = []
+    for s in range(span + 1):
+        piece = z_ref[tile, BLOCK * (n + s) : BLOCK * (n + s + 1)]
+        pieces.append(piece * same[n][s].astype(BF16) if s < span else piece)
+    pieces.append(jnp.zeros((2 * LANES - BLOCK * (span + 1), LANES), BF16))
+    return jnp.concatenate(pieces, axis=0)
+
+
+def windows_of(z_ref, tile, half, same):
+    return jnp.concatenate([window_of(z_ref, tile, 2 * half + i, same) for i in range(2)], axis=1)
+
+
 def in_groups(count, beside, stages):
     def some(step, carry):
         now = [step * beside + side for side in range(beside)]
@@ -238,8 +252,6 @@
     per_tile = band_ref.shape[1] // BLOCK
     joined, same, _ = notes_of(note_ref, own, span)
     picks = lane_picks(per_tile)
-    for side in range(beside):
-        z_ref[side, window * BLOCK :] = jnp.zeros((z_ref.shape[1] - window * BLOCK, LANES), BF16)
 
     def filters(tile, side, _):
         at = tile_lanes(tile)
@@ -263,18 +275,14 @@
         for n in range(own):
             at_n = slice(BLOCK * n, BLOCK * (n + 1))
             uq_ref[tile, at_n] = up_ref[at_n, at].astype(F32) * short(xq_ref, tile, n, q_taps)
-            lanes = slice(LANES * (n % 2), LANES * (n % 2 + 1))
-            for s in range(2 * LANES // BLOCK):
-                piece = z_ref[side, BLOCK * (n + s) : BLOCK * (n + s + 1)]
-                if s < span:
-                    piece = piece * same[n][s].astype(BF16)
-                zw_ref[tile, n // 2, BLOCK * s : BLOCK * (s + 1), lanes] = piece
 
     def medium(tile, side, _):
         at = tile_lanes(tile)
         band = band_ref[tile]
         for half in range(own // 2):
-            wide = dot(band, zw_ref[tile, half], ((1,), (0,)))
+            zws = windows_of(z_ref, side, half, same)
+            zw_ref[tile, half] = zws
+            wide = dot(band, zws, ((1,), (0,)))
             for part in range(2):
                 n = 2 * half + part
                 at_n = slice(BLOCK * n, BLOCK * (n + 1))
@@ -351,9 +359,13 @@
         skew = None
         for r in range(BLOCK // 8):
             rows_r = lined[:, r].reshape(per_tile * 8, 2 * LANES)
-            moved = pltpu.roll(rows_r, 2 * LANES - 1 - 8 * r, 1)
+            moved = pltpu.roll(rows_r, 2 * LANES - 8 * r, 1) if r else rows_r
             skew = moved if skew is None else skew + moved
-        skew_ref[tile] = skew
+        for side_of in range(2):
+            start = (side_of * tiles + tile) * per_tile * 8
+            skew_ref[pl.ds(pl.multiple_of(start, 8), per_tile * 8)] = skew[
+                :, LANES * side_of : LANES * (side_of + 1)
+            ]
 
     def grads(tile, side, _):
         at = tile_lanes(tile)
@@ -379,12 +391,20 @@
             out_ref[8 * i + count : 8 * i + 8, at] = jnp.zeros((8 - count, LANES), F32)
 
     in_groups(tiles, beside, (stack, middle, grads))
-    skew = skew_ref[...].reshape(tiles * per_tile * 8, 2 * LANES)
-    row_index = lax.broadcasted_iota(jnp.int32, skew.shape, 0)
-    for bit in range(3):
-        moved = pltpu.roll(skew, 2 * LANES - (1 << bit), 1)
-        skew = jnp.where((row_index >> bit) & 1 == 1, moved, skew)
-    totals = jnp.sum(skew[:, 0:LANES].reshape(tiles * per_tile, 8, LANES), axis=1)
+    lane = lax.broadcasted_iota(jnp.int32, (2 * LANES, LANES), 0)
+    tap = lax.broadcasted_iota(jnp.int32, (2 * LANES, LANES), 1)
+    groups = tiles * per_tile
+    totals = None
+    for u in range(8):
+        rows_u = jnp.concatenate(
+            [skew_ref[pl.ds(8 * groups * i + u, groups, stride=8)] for i in range(2)], axis=1
+        )
+        high = rows_u.astype(BF16)
+        low = (rows_u - high.astype(F32)).astype(BF16)
+        pick = jnp.where(lane + tap == LANES + u, 1.0, 0.0).astype(BF16)
+        term = dot(jnp.concatenate([high, low], axis=0), pick, ((1,), (0,)))
+        totals = term if totals is None else totals + term
+    totals = totals[0:groups] + totals[groups:]
     for tile in range(tiles):
         out_ref[24 : 24 + per_tile, LANES * tile : LANES * (tile + 1)] = totals[
             per_tile * tile : per_tile * (tile + 1)
@@ -401,10 +421,7 @@
     flat = jnp.concatenate(
         [total[24:, t * LANES : (t + 1) * LANES] for t in range(channels // LANES)], axis=0
     )
-    tap = lax.broadcasted_iota(jnp.int32, (LANES, LANES), 0)
-    lane = lax.broadcasted_iota(jnp.int32, (LANES, LANES), 1)
-    flip = jnp.where(tap + lane == LANES - 1, 1.0, 0.0).astype(F32)
-    mr_ref[...] = dot(flat, flip, ((1,), (0,)), lax.Precision.HIGHEST)
+    mr_ref[...] = flat
 
 
 def swapped(value, axis, distance):
@@ -538,7 +555,7 @@
         ),
         in_specs=[spec()] * 10,
         out_specs=(spec(),) * 8,
-        scratch_shapes=[pltpu.VMEM((beside, (own - 1) * BLOCK + 2 * LANES, LANES), BF16)],
+        scratch_shapes=[pltpu.VMEM((beside, window * BLOCK, LANES), BF16)],
         compiler_params=pltpu.CompilerParams(vmem_limit_bytes=LIMIT),
         cost_estimate=cost(2.0),
         name="forward",
@@ -553,7 +570,7 @@
         scratch_shapes=[
             pltpu.VMEM((beside, own // 2, stack, 2 * LANES), BF16),
             pltpu.VMEM((beside, window * BLOCK, LANES), F32),
-            pltpu.VMEM((tiles, per_tile * 8, 2 * LANES), F32),
+            pltpu.VMEM((2 * groups * 8, LANES), F32),
             pltpu.VMEM((rows, LANES), F32),
         ],
         compiler_params=pltpu.CompilerParams(vmem_limit_bytes=LIMIT),

time: 27.5 us -> 27.3 us (level)
  Pallas kernels: 8.8 us -> 8.42 us
where the time goes in v5:
time: 27.3 us; the launch traced here: 27.1 us
  starting transfers between devices  12.5 us (46%)
  Pallas kernels  8.42 us (31%)
  waiting for transfers between devices  5.37 us (20%)
  between operations  0.77 us (3%)
    ppermute x6, starting transfers between devices, swapped(): return lax.ppermute(value, axis, [(i, i ^ distance) for i in range(count)])  7.88 us
    ppermute x6, waiting for transfers between devices, swapped(): return lax.ppermute(value, axis, [(i, i ^ distance) for i in range(count)])  5.36 us
    ppermute x3, starting transfers between devices, moved_up(): lax.ppermute(value, axis, [(i, (i + steps) % count) for i in range(count)])  4.65 us
    pallas_call x1, Pallas kernels, on_device(): pl.pallas_call(functools.partial(backward_kernel, float(channels * lax.ax...  3.23 us
    pallas_call x1, Pallas kernels, on_device(): pl.pallas_call(functools.partial(forward_kernel, beside), out_shape=(jax....  1.89 us
    pallas_call x1, Pallas kernels, on_device(): pl.pallas_call(functools.partial(first_kernel, span), out_shape=(jax.Shap...  1.16 us
    pallas_call x1, Pallas kernels, on_device(): pl.pallas_call(band_kernel, out_shape=(jax.ShapeDtypeStruct((tiles, stack...  0.96 us
    pallas_call x1, Pallas kernels, on_device(): pl.pallas_call(functools.partial(last_kernel, 1.0 / rows), out_shape=(jax...  0.68 us
  transfers between devices with their start and end apart: 9, of which 5 were waited for; matrix products, arithmetic and copies ran while one was open for 0% of the time, Pallas kernels for 17%

profile of v5, /device:TPU:0, one launch (start us, length us, event | category | flops | bytes accessed | tf_op | source)
XLA Modules:
  0.0 27.1 jit_solution(9874783752425935559)
XLA Ops:
  0.7 0.5 %collective-permute-start.1 = (bf16[128,1024]{1,0:T(8,128)(2,1)}, bf16[128,1024]{1,0:T(8,128)(2,1)S(1)}, u32[]{:S(2)}, u32[]{:S(2)}) collective-permute-start(bf16[128,1024]{1,0:T(8,128)(2,1)} %k_ref.3), channel_id=1, source_target_pairs={{0,4},{4,8},{8,12},{12,16},{16,20},{20,24},{24,28},{28,0},{1,5},{5... | collective-permute-start | bytes 786440 | tf_op jit(solution)/shard_map/ppermute | solution.py:460
  1.2 1.2 %first.1 = (bf16[144,1024]{1,0:T(8,128)(2,1)S(1)}, bf16[16,1024]{1,0:T(8,128)(2,1)S(1)}, f32[64,128]{1,0:T(8,128)S(1)}, f32[25,128]{1,0:T(8,128)S(1)}, bf16[64,1...) custom-call(s32[4]{0:T(128)} %lengths_ref.1, s32[1,128]{1,0:T(1,128)} %bitcast.4, bf16[128,1024]{1,0:T(8,128)(2,1)} %q_ref.3, ...), custom_call_target="tpu_custom_call" | custom-call | flops 1 | bytes 4320000 | tf_op jit(solution)/shard_map/first/pallas_call | solution.py:477
  2.3 2.7 %collective-permute-start.2 = (bf16[144,1024]{1,0:T(8,128)(2,1)S(1)}, bf16[144,1024]{1,0:T(8,128)(2,1)S(1)}, u32[]{:S(2)}, u32[]{:S(2)}) collective-permute-start(bf16[144,1024]{1,0:T(8,128)(2,1)S(1)} %get-tuple-element.37), channel_id=1, source_target_pairs={{0,4},{4,8},{8,12},{12,16},{16,20},{20,24},{24,28},{28,0},{1,5},{5... | collective-permute-start | bytes 884744 | tf_op jit(solution)/shard_map/ppermute | solution.py:460
  5.0 1.6 %collective-permute-start = (f32[64,128]{1,0:T(8,128)S(1)}, f32[64,128]{1,0:T(8,128)S(1)}, u32[]{:S(2)}, u32[]{:S(2)}) collective-permute-start(f32[64,128]{1,0:T(8,128)S(1)} %get-tuple-element.27), channel_id=1, source_target_pairs={{0,1},{1,0},{2,3},{3,2},{4,5},{5,4},{6,7},{7,6},{8,9},{9,8},{10,11... | collective-permute-start | bytes 98312 | tf_op jit(solution)/shard_map/ppermute | solution.py:429
  6.6 1.5 %collective-permute-start.3 = (bf16[16,1024]{1,0:T(8,128)(2,1)S(1)}, bf16[16,1024]{1,0:T(8,128)(2,1)S(1)}, u32[]{:S(2)}, u32[]{:S(2)}) collective-permute-start(bf16[16,1024]{1,0:T(8,128)(2,1)S(1)} %get-tuple-element.38), channel_id=1, source_target_pairs={{0,8},{4,12},{8,16},{12,20},{16,24},{20,28},{24,0},{28,4},{1,9},{5... | collective-permute-start | bytes 98312 | tf_op jit(solution)/shard_map/ppermute | solution.py:460
  8.1 1.0 %band.1 = (bf16[8,256,256]{2,1,0:T(8,128)(2,1)S(1)}, bf16[8,160,256]{2,1,0:T(8,128)(2,1)S(1)}) custom-call(bf16[64,128]{1,0:T(8,128)(2,1)S(1)} %get-tuple-element.28.h_ref), custom_call_target="tpu_custom_call" | custom-call | flops 1 | bytes 3600000 | tf_op jit(solution)/shard_map/band/pallas_call | solution.py:517
  9.0 0.0 collective-permute-done.1.k_near_ref
  9.1 0.5 %keys.1 = (f32[8,280,128]{2,1,0:T(8,128)S(1)}, f32[8,224,128]{2,1,0:T(8,128)S(1)}) custom-call(bf16[128,1024]{1,0:T(8,128)(2,1)S(1)} %copy-done, bf16[128,1024]{1,0:T(8,128)(2,1)S(1)} %collective-permute-done.1.k_near_ref, f32[25,128]{1,0:T(8,128)S(1)} %get-tuple-element.31.note_ref, bf16[3,7,1024]{2,1,0:T(8,128)(2,1)S(1)} %get-tuple-element.32.se_ref), custom_call_target="tpu_custom_call" | custom-call | flops 1 | bytes 1800000 | tf_op jit(solution)/shard_map/keys/pallas_call | solution.py:531
  9.6 0.0 collective-permute-done
  9.6 2.7 %collective-permute-start.4 = (f32[64,128]{1,0:T(8,128)S(1)}, f32[64,128]{1,0:T(8,128)S(1)}, u32[]{:S(2)}, u32[]{:S(2)}) collective-permute-start(f32[64,128]{1,0:T(8,128)S(1)} %add.6.rest_0_), channel_id=1, source_target_pairs={{0,2},{1,3},{2,0},{3,1},{4,6},{5,7},{6,4},{7,5},{8,10},{9,11},{10,... | collective-permute-start | bytes 98312 | tf_op jit(solution)/shard_map/ppermute | solution.py:429
  12.3 0.0 collective-permute-done.3.far_ref
  12.3 0.0 collective-permute-done.2.near_ref
  12.3 1.9 %forward.1 = (f32[8,160,128]{2,1,0:T(8,128)S(1)}, f32[8,40,128]{2,1,0:T(8,128)S(1)}, f32[8,320,128]{2,1,0:T(8,128)S(1)}, f32[8,32,128]{2,1,0:T(8,128)S(1)}, f32[...) custom-call(bf16[128,1024]{1,0:T(8,128)(2,1)S(1)} %copy-done.1, ...), custom_call_target="tpu_custom_call" | custom-call | flops 1 | bytes 7200000 | tf_op jit(solution)/shard_map/forward/pallas_call | solution.py:544
  14.2 0.3 collective-permute-done.4.rest_1_
  14.5 3.2 %backward.1 = f32[32,1024]{1,0:T(8,128)S(1)} custom-call(f32[8,280,128]{2,1,0:T(8,128)S(1)} %get-tuple-element.35.xk_ref, f32[8,224,128]{2,1,0:T(8,128)S(1)} %get-tuple-element.36.ks_ref, f32[8,160,128]{2,1,0:T(8,128)S(1)} %get-tuple-element.40.xq_ref, f32[8,40,128]{2,1,0:T(8,128)S(1)} %get-tuple-element.41.xk_first_ref, ...), custom_call_target="tpu_custom_call" | custom-call | tf_op jit(solution)/shard_map/backward/pallas_call | solution.py:563
  17.7 0.1 collective-permute-start.5
  17.8 1.3 %collective-permute-done.5 = f32[32,1024]{1,0:T(8,128)S(1)} collective-permute-done((f32[32,1024]{1,0:T(8,128)S(1)}, f32[32,1024]{1,0:T(8,128)S(1)}, u32[]{:S(2)}, u32[]{:S(2)}) %collective-permute-start.5) | collective-permute-done | bytes 131104 | tf_op jit(solution)/shard_map/ppermute | solution.py:429
  19.1 1.7 %collective-permute-start.8 = (bf16[32,1024]{1,0:T(8,128)(2,1)S(1)}, bf16[32,1024]{1,0:T(8,128)(2,1)S(1)}, u32[]{:S(2)}, u32[]{:S(2)}) collective-permute-start(bf16[32,1024]{1,0:T(8,128)(2,1)S(1)} %add_convert_fusion.refs_0_), channel_id=1, source_target_pairs={{0,24},{4,28},{8,16},{12,20},{16,8},{20,12},{24,0},{28,4},{1,25},{... | collective-permute-start | bytes 196616 | tf_op jit(solution)/shard_map/ppermute | solution.py:429
  20.8 1.4 %collective-permute-start.7 = (bf16[32,1024]{1,0:T(8,128)(2,1)S(1)}, bf16[32,1024]{1,0:T(8,128)(2,1)S(1)}, u32[]{:S(2)}, u32[]{:S(2)}) collective-permute-start(bf16[32,1024]{1,0:T(8,128)(2,1)S(1)} %add_convert_fusion.refs_0_), channel_id=1, source_target_pairs={{0,16},{4,20},{8,24},{12,28},{16,0},{20,4},{24,8},{28,12},{1,17},{... | collective-permute-start | bytes 196616 | tf_op jit(solution)/shard_map/ppermute | solution.py:429
  22.2 0.5 %collective-permute-start.6 = (bf16[32,1024]{1,0:T(8,128)(2,1)S(1)}, bf16[32,1024]{1,0:T(8,128)(2,1)S(1)}, u32[]{:S(2)}, u32[]{:S(2)}) collective-permute-start(bf16[32,1024]{1,0:T(8,128)(2,1)S(1)} %add_convert_fusion.refs_0_), channel_id=1, source_target_pairs={{0,8},{4,12},{8,0},{12,4},{16,24},{20,28},{24,16},{28,20},{1,9},{5... | collective-permute-start | bytes 196616 | tf_op jit(solution)/shard_map/ppermute | solution.py:429
  22.7 1.7 %collective-permute-done.8.refs_3_ = bf16[32,1024]{1,0:T(8,128)(2,1)S(1)} collective-permute-done((bf16[32,1024]{1,0:T(8,128)(2,1)S(1)}, bf16[32,1024]{1,0:T(8,128)(2,1)S(1)}, u32[]{:S(2)}, u32[]{:S(2)}) %collective-permute-start.8) | collective-permute-done | bytes 65568 | tf_op jit(solution)/shard_map/ppermute | solution.py:429
  24.4 1.2 %collective-permute-done.7.refs_2_ = bf16[32,1024]{1,0:T(8,128)(2,1)S(1)} collective-permute-done((bf16[32,1024]{1,0:T(8,128)(2,1)S(1)}, bf16[32,1024]{1,0:T(8,128)(2,1)S(1)}, u32[]{:S(2)}, u32[]{:S(2)}) %collective-permute-start.7) | collective-permute-done | bytes 65568 | tf_op jit(solution)/shard_map/ppermute | solution.py:429
  25.7 0.8 %collective-permute-done.6.refs_1_ = bf16[32,1024]{1,0:T(8,128)(2,1)S(1)} collective-permute-done((bf16[32,1024]{1,0:T(8,128)(2,1)S(1)}, bf16[32,1024]{1,0:T(8,128)(2,1)S(1)}, u32[]{:S(2)}, u32[]{:S(2)}) %collective-permute-start.6) | collective-permute-done | bytes 65568 | tf_op jit(solution)/shard_map/ppermute | solution.py:429
  26.5 0.7 %last.1 = (f32[3,7,1024]{2,1,0:T(8,128)}, f32[64,128]{1,0:T(8,128)}) custom-call(bf16[32,1024]{1,0:T(8,128)(2,1)S(1)} %add_convert_fusion.refs_0_, bf16[32,1024]{1,0:T(8,128)(2,1)S(1)} %collective-permute-done.6.refs_1_, bf16[32,1024]{1,0:T(8,128)(2,1)S(1)} %collective-permute-done.7.refs_2_, bf16[32,1024]{1,0:T(8,128)(2,1)S(1)} %collective-permute-done.8.refs_3_), custom_call_target="tpu_custom_call" | custom-call | tf_op jit(solution)/shard_map/last/pallas_call | solution.py:581
  (10 shorter events, 0.0 us)
Async XLA Ops:
  0.6 8.4 %copy-start = (bf16[128,1024]{1,0:T(8,128)(2,1)S(1)}, bf16[128,1024]{1,0:T(8,128)(2,1)}, u32[]{:S(2)}) copy-start(bf16[128,1024]{1,0:T(8,128)(2,1)} %k_ref.3) | copy-start | bytes 786436
  0.6 11.6 %copy-start.3 = (bf16[128,1024]{1,0:T(8,128)(2,1)S(1)}, bf16[128,1024]{1,0:T(8,128)(2,1)}, u32[]{:S(2)}) copy-start(bf16[128,1024]{1,0:T(8,128)(2,1)} %up_ref.3) | copy-start | bytes 786436
  0.7 11.6 %copy-start.2 = (bf16[128,1024]{1,0:T(8,128)(2,1)S(1)}, bf16[128,1024]{1,0:T(8,128)(2,1)}, u32[]{:S(2)}) copy-start(bf16[128,1024]{1,0:T(8,128)(2,1)} %v_ref.3) | copy-start | bytes 786436
  0.7 11.6 %copy-start.1 = (bf16[128,1024]{1,0:T(8,128)(2,1)S(1)}, bf16[128,1024]{1,0:T(8,128)(2,1)}, u32[]{:S(2)}) copy-start(bf16[128,1024]{1,0:T(8,128)(2,1)} %q_ref.3) | copy-start | bytes 786436
  0.7 8.4 %collective-permute-start.1 = (bf16[128,1024]{1,0:T(8,128)(2,1)}, bf16[128,1024]{1,0:T(8,128)(2,1)S(1)}, u32[]{:S(2)}, u32[]{:S(2)}) collective-permute-start(bf16[128,1024]{1,0:T(8,128)(2,1)} %k_ref.3), channel_id=1, source_target_pairs={{0,4},{4,8},{8,12},{12,16},{16,20},{20,24},{24,28},{28,0},{1,5},{5... | collective-permute-start | bytes 786440 | tf_op jit(solution)/shard_map/ppermute | solution.py:460
  2.3 9.9 %collective-permute-start.2 = (bf16[144,1024]{1,0:T(8,128)(2,1)S(1)}, bf16[144,1024]{1,0:T(8,128)(2,1)S(1)}, u32[]{:S(2)}, u32[]{:S(2)}) collective-permute-start(bf16[144,1024]{1,0:T(8,128)(2,1)S(1)} %get-tuple-element.37), channel_id=1, source_target_pairs={{0,4},{4,8},{8,12},{12,16},{16,20},{20,24},{24,28},{28,0},{1,5},{5... | collective-permute-start | bytes 884744 | tf_op jit(solution)/shard_map/ppermute | solution.py:460
  5.0 4.6 %collective-permute-start = (f32[64,128]{1,0:T(8,128)S(1)}, f32[64,128]{1,0:T(8,128)S(1)}, u32[]{:S(2)}, u32[]{:S(2)}) collective-permute-start(f32[64,128]{1,0:T(8,128)S(1)} %get-tuple-element.27), channel_id=1, source_target_pairs={{0,1},{1,0},{2,3},{3,2},{4,5},{5,4},{6,7},{7,6},{8,9},{9,8},{10,11... | collective-permute-start | bytes 98312 | tf_op jit(solution)/shard_map/ppermute | solution.py:429
  6.6 5.7 %collective-permute-start.3 = (bf16[16,1024]{1,0:T(8,128)(2,1)S(1)}, bf16[16,1024]{1,0:T(8,128)(2,1)S(1)}, u32[]{:S(2)}, u32[]{:S(2)}) collective-permute-start(bf16[16,1024]{1,0:T(8,128)(2,1)S(1)} %get-tuple-element.38), channel_id=1, source_target_pairs={{0,8},{4,12},{8,16},{12,20},{16,24},{20,28},{24,0},{28,4},{1,9},{5... | collective-permute-start | bytes 98312 | tf_op jit(solution)/shard_map/ppermute | solution.py:460
  9.6 4.9 %collective-permute-start.4 = (f32[64,128]{1,0:T(8,128)S(1)}, f32[64,128]{1,0:T(8,128)S(1)}, u32[]{:S(2)}, u32[]{:S(2)}) collective-permute-start(f32[64,128]{1,0:T(8,128)S(1)} %add.6.rest_0_), channel_id=1, source_target_pairs={{0,2},{1,3},{2,0},{3,1},{4,6},{5,7},{6,4},{7,5},{8,10},{9,11},{10,... | collective-permute-start | bytes 98312 | tf_op jit(solution)/shard_map/ppermute | solution.py:429
  17.7 1.4 %collective-permute-start.5 = (f32[32,1024]{1,0:T(8,128)S(1)}, f32[32,1024]{1,0:T(8,128)S(1)}, u32[]{:S(2)}, u32[]{:S(2)}) collective-permute-start(f32[32,1024]{1,0:T(8,128)S(1)} %backward.1), channel_id=1, source_target_pairs={{0,4},{4,0},{8,12},{12,8},{16,20},{20,16},{24,28},{28,24},{1,5},{5... | collective-permute-start | bytes 393224 | tf_op jit(solution)/shard_map/ppermute | solution.py:429
  19.1 5.3 %collective-permute-start.8 = (bf16[32,1024]{1,0:T(8,128)(2,1)S(1)}, bf16[32,1024]{1,0:T(8,128)(2,1)S(1)}, u32[]{:S(2)}, u32[]{:S(2)}) collective-permute-start(bf16[32,1024]{1,0:T(8,128)(2,1)S(1)} %add_convert_fusion.refs_0_), channel_id=1, source_target_pairs={{0,24},{4,28},{8,16},{12,20},{16,8},{20,12},{24,0},{28,4},{1,25},{... | collective-permute-start | bytes 196616 | tf_op jit(solution)/shard_map/ppermute | solution.py:429
  20.8 4.9 %collective-permute-start.7 = (bf16[32,1024]{1,0:T(8,128)(2,1)S(1)}, bf16[32,1024]{1,0:T(8,128)(2,1)S(1)}, u32[]{:S(2)}, u32[]{:S(2)}) collective-permute-start(bf16[32,1024]{1,0:T(8,128)(2,1)S(1)} %add_convert_fusion.refs_0_), channel_id=1, source_target_pairs={{0,16},{4,20},{8,24},{12,28},{16,0},{20,4},{24,8},{28,12},{1,17},{... | collective-permute-start | bytes 196616 | tf_op jit(solution)/shard_map/ppermute | solution.py:429
  22.2 4.3 %collective-permute-start.6 = (bf16[32,1024]{1,0:T(8,128)(2,1)S(1)}, bf16[32,1024]{1,0:T(8,128)(2,1)S(1)}, u32[]{:S(2)}, u32[]{:S(2)}) collective-permute-start(bf16[32,1024]{1,0:T(8,128)(2,1)S(1)} %add_convert_fusion.refs_0_), channel_id=1, source_target_pairs={{0,8},{4,12},{8,0},{12,4},{16,24},{20,28},{24,16},{28,20},{1,9},{5... | collective-permute-start | bytes 196616 | tf_op jit(solution)/shard_map/ppermute | solution.py:429

commit v6 on v5

--- a/solution.py
+++ b/solution.py
@@ -528,6 +528,7 @@
         name="band",
     )(medium_taps)
 
+    squares, (band, band_t, k_near) = summed_small(sq, "fsdp", (band, band_t, k_near))
     keys = pl.pallas_call(
         functools.partial(key_kernel, beside),
         out_shape=(
@@ -540,7 +541,6 @@
         cost_estimate=cost(0.5),
         name="keys",
     )(key, k_near, notes, short_taps)
-    squares, (band, band_t, keys) = summed_small(sq, "fsdp", (band, band_t, keys))
     kept = pl.pallas_call(
         functools.partial(forward_kernel, beside),
         out_shape=(
@@ -570,7 +570,7 @@
         scratch_shapes=[
             pltpu.VMEM((beside, own // 2, stack, 2 * LANES), BF16),
             pltpu.VMEM((beside, window * BLOCK, LANES), F32),
-            pltpu.VMEM((2 * groups * 8, LANES), F32),
+            pltpu.VMEM((2 * groups * 8 + 8, LANES), F32),
             pltpu.VMEM((rows, LANES), F32),
         ],
         compiler_params=pltpu.CompilerParams(vmem_limit_bytes=LIMIT),

time: 27.3 us -> 27 us (0.989)
  waiting for transfers between devices: 5.37 us -> 5.07 us
    ppermute x6, waiting for transfers between devices: 5.36 us -> 5.07 us  [swapped(): return lax.ppermute(value, axis, [(i, i ^ distance) for i in range(count)])]
  transfers between devices with their start and end apart: 9 -> 9, of which waited for: 5 -> 4; matrix products, arithmetic and copies ran while one was open for 0% -> 0% of each run, Pallas kernels for 17% -> 17%
where the time goes in v6:
time: 27 us; the launch traced here: 26.9 us
  starting transfers between devices  12.5 us (46%)
  Pallas kernels  8.46 us (31%)
  waiting for transfers between devices  5.07 us (19%)
  between operations  0.79 us (3%)
    ppermute x6, starting transfers between devices, swapped(): return lax.ppermute(value, axis, [(i, i ^ distance) for i in range(count)])  7.86 us
    ppermute x6, waiting for transfers between devices, swapped(): return lax.ppermute(value, axis, [(i, i ^ distance) for i in range(count)])  5.07 us
    ppermute x3, starting transfers between devices, moved_up(): lax.ppermute(value, axis, [(i, (i + steps) % count) for i in range(count)])  4.65 us
    pallas_call x1, Pallas kernels, on_device(): pl.pallas_call(functools.partial(backward_kernel, float(channels * lax.ax...  3.27 us
    pallas_call x1, Pallas kernels, on_device(): pl.pallas_call(functools.partial(forward_kernel, beside), out_shape=(jax....  1.89 us
    pallas_call x1, Pallas kernels, on_device(): pl.pallas_call(functools.partial(first_kernel, span), out_shape=(jax.Shap...  1.16 us
    pallas_call x1, Pallas kernels, on_device(): pl.pallas_call(band_kernel, out_shape=(jax.ShapeDtypeStruct((tiles, stack...  0.96 us
    pallas_call x1, Pallas kernels, on_device(): pl.pallas_call(functools.partial(last_kernel, 1.0 / rows), out_shape=(jax...  0.68 us
  transfers between devices with their start and end apart: 9, of which 4 were waited for; matrix products, arithmetic and copies ran while one was open for 0% of the time, Pallas kernels for 17%

profile of v6, /device:TPU:0, one launch (start us, length us, event | category | flops | bytes accessed | tf_op | source)
XLA Modules:
  0.0 26.9 jit_solution(5528096218315555140)
XLA Ops:
  0.7 0.5 %collective-permute-start.1 = (bf16[128,1024]{1,0:T(8,128)(2,1)}, bf16[128,1024]{1,0:T(8,128)(2,1)S(1)}, u32[]{:S(2)}, u32[]{:S(2)}) collective-permute-start(bf16[128,1024]{1,0:T(8,128)(2,1)} %k_ref.3), channel_id=1, source_target_pairs={{0,4},{4,8},{8,12},{12,16},{16,20},{20,24},{24,28},{28,0},{1,5},{5... | collective-permute-start | bytes 786440 | tf_op jit(solution)/shard_map/ppermute | solution.py:460
  1.2 1.2 %first.1 = (bf16[144,1024]{1,0:T(8,128)(2,1)S(1)}, bf16[16,1024]{1,0:T(8,128)(2,1)S(1)}, f32[64,128]{1,0:T(8,128)S(1)}, f32[25,128]{1,0:T(8,128)S(1)}, bf16[64,1...) custom-call(s32[4]{0:T(128)} %lengths_ref.1, s32[1,128]{1,0:T(1,128)} %bitcast.4, bf16[128,1024]{1,0:T(8,128)(2,1)} %q_ref.3, ...), custom_call_target="tpu_custom_call" | custom-call | flops 1 | bytes 4320000 | tf_op jit(solution)/shard_map/first/pallas_call | solution.py:477
  2.3 2.7 %collective-permute-start.2 = (bf16[144,1024]{1,0:T(8,128)(2,1)S(1)}, bf16[144,1024]{1,0:T(8,128)(2,1)S(1)}, u32[]{:S(2)}, u32[]{:S(2)}) collective-permute-start(bf16[144,1024]{1,0:T(8,128)(2,1)S(1)} %get-tuple-element.35), channel_id=1, source_target_pairs={{0,4},{4,8},{8,12},{12,16},{16,20},{20,24},{24,28},{28,0},{1,5},{5... | collective-permute-start | bytes 884744 | tf_op jit(solution)/shard_map/ppermute | solution.py:460
  5.0 1.6 %collective-permute-start = (f32[64,128]{1,0:T(8,128)S(1)}, f32[64,128]{1,0:T(8,128)S(1)}, u32[]{:S(2)}, u32[]{:S(2)}) collective-permute-start(f32[64,128]{1,0:T(8,128)S(1)} %get-tuple-element.26), channel_id=1, source_target_pairs={{0,1},{1,0},{2,3},{3,2},{4,5},{5,4},{6,7},{7,6},{8,9},{9,8},{10,11... | collective-permute-start | bytes 98312 | tf_op jit(solution)/shard_map/ppermute | solution.py:429
  6.6 1.5 %collective-permute-start.3 = (bf16[16,1024]{1,0:T(8,128)(2,1)S(1)}, bf16[16,1024]{1,0:T(8,128)(2,1)S(1)}, u32[]{:S(2)}, u32[]{:S(2)}) collective-permute-start(bf16[16,1024]{1,0:T(8,128)(2,1)S(1)} %get-tuple-element.36), channel_id=1, source_target_pairs={{0,8},{4,12},{8,16},{12,20},{16,24},{20,28},{24,0},{28,4},{1,9},{5... | collective-permute-start | bytes 98312 | tf_op jit(solution)/shard_map/ppermute | solution.py:460
  8.1 1.0 %band.1 = (bf16[8,256,256]{2,1,0:T(8,128)(2,1)S(1)}, bf16[8,160,256]{2,1,0:T(8,128)(2,1)S(1)}) custom-call(bf16[64,128]{1,0:T(8,128)(2,1)S(1)} %get-tuple-element.27.h_ref), custom_call_target="tpu_custom_call" | custom-call | flops 1 | bytes 3600000 | tf_op jit(solution)/shard_map/band/pallas_call | solution.py:517
  9.0 0.0 collective-permute-done
  9.0 0.0 collective-permute-done.1.k_near_ref
  9.1 2.7 %collective-permute-start.4 = (f32[64,128]{1,0:T(8,128)S(1)}, f32[64,128]{1,0:T(8,128)S(1)}, u32[]{:S(2)}, u32[]{:S(2)}) collective-permute-start(f32[64,128]{1,0:T(8,128)S(1)} %add.6.rest_0_), channel_id=1, source_target_pairs={{0,2},{1,3},{2,0},{3,1},{4,6},{5,7},{6,4},{7,5},{8,10},{9,11},{10,... | collective-permute-start | bytes 98312 | tf_op jit(solution)/shard_map/ppermute | solution.py:429
  11.7 0.5 %keys.1 = (f32[8,280,128]{2,1,0:T(8,128)S(1)}, f32[8,224,128]{2,1,0:T(8,128)S(1)}) custom-call(bf16[128,1024]{1,0:T(8,128)(2,1)S(1)} %copy-done, bf16[128,1024]{1,0:T(8,128)(2,1)S(1)} %collective-permute-done.1.k_near_ref, f32[25,128]{1,0:T(8,128)S(1)} %get-tuple-element.31.note_ref, bf16[3,7,1024]{2,1,0:T(8,128)(2,1)S(1)} %get-tuple-element.32.se_ref), custom_call_target="tpu_custom_call" | custom-call | flops 1 | bytes 1800000 | tf_op jit(solution)/shard_map/keys/pallas_call | solution.py:532
  12.2 0.0 collective-permute-done.3.far_ref
  12.3 0.0 collective-permute-done.2.near_ref
  12.3 1.9 %forward.1 = (f32[8,160,128]{2,1,0:T(8,128)S(1)}, f32[8,40,128]{2,1,0:T(8,128)S(1)}, f32[8,320,128]{2,1,0:T(8,128)S(1)}, f32[8,32,128]{2,1,0:T(8,128)S(1)}, f32[...) custom-call(bf16[128,1024]{1,0:T(8,128)(2,1)S(1)} %copy-done.1, ...), custom_call_target="tpu_custom_call" | custom-call | flops 1 | bytes 7200000 | tf_op jit(solution)/shard_map/forward/pallas_call | solution.py:544
  14.2 0.0 collective-permute-done.4.rest_1_
  14.2 3.3 %backward.1 = f32[32,1024]{1,0:T(8,128)S(1)} custom-call(f32[8,280,128]{2,1,0:T(8,128)S(1)} %get-tuple-element.33.xk_ref, f32[8,224,128]{2,1,0:T(8,128)S(1)} %get-tuple-element.34.ks_ref, f32[8,160,128]{2,1,0:T(8,128)S(1)} %get-tuple-element.38.xq_ref, f32[8,40,128]{2,1,0:T(8,128)S(1)} %get-tuple-element.39.xk_first_ref, ...), custom_call_target="tpu_custom_call" | custom-call | tf_op jit(solution)/shard_map/backward/pallas_call | solution.py:563
  17.5 0.1 collective-permute-start.5
  17.6 1.3 %collective-permute-done.5 = f32[32,1024]{1,0:T(8,128)S(1)} collective-permute-done((f32[32,1024]{1,0:T(8,128)S(1)}, f32[32,1024]{1,0:T(8,128)S(1)}, u32[]{:S(2)}, u32[]{:S(2)}) %collective-permute-start.5) | collective-permute-done | bytes 131104 | tf_op jit(solution)/shard_map/ppermute | solution.py:429
  18.9 1.9 %collective-permute-start.8 = (bf16[32,1024]{1,0:T(8,128)(2,1)S(1)}, bf16[32,1024]{1,0:T(8,128)(2,1)S(1)}, u32[]{:S(2)}, u32[]{:S(2)}) collective-permute-start(bf16[32,1024]{1,0:T(8,128)(2,1)S(1)} %add_convert_fusion.refs_0_), channel_id=1, source_target_pairs={{0,24},{4,28},{8,16},{12,20},{16,8},{20,12},{24,0},{28,4},{1,25},{... | collective-permute-start | bytes 196616 | tf_op jit(solution)/shard_map/ppermute | solution.py:429
  20.8 1.1 %collective-permute-start.7 = (bf16[32,1024]{1,0:T(8,128)(2,1)S(1)}, bf16[32,1024]{1,0:T(8,128)(2,1)S(1)}, u32[]{:S(2)}, u32[]{:S(2)}) collective-permute-start(bf16[32,1024]{1,0:T(8,128)(2,1)S(1)} %add_convert_fusion.refs_0_), channel_id=1, source_target_pairs={{0,16},{4,20},{8,24},{12,28},{16,0},{20,4},{24,8},{28,12},{1,17},{... | collective-permute-start | bytes 196616 | tf_op jit(solution)/shard_map/ppermute | solution.py:429
  21.9 0.5 %collective-permute-start.6 = (bf16[32,1024]{1,0:T(8,128)(2,1)S(1)}, bf16[32,1024]{1,0:T(8,128)(2,1)S(1)}, u32[]{:S(2)}, u32[]{:S(2)}) collective-permute-start(bf16[32,1024]{1,0:T(8,128)(2,1)S(1)} %add_convert_fusion.refs_0_), channel_id=1, source_target_pairs={{0,8},{4,12},{8,0},{12,4},{16,24},{20,28},{24,16},{28,20},{1,9},{5... | collective-permute-start | bytes 196616 | tf_op jit(solution)/shard_map/ppermute | solution.py:429
  22.5 1.8 %collective-permute-done.8.refs_3_ = bf16[32,1024]{1,0:T(8,128)(2,1)S(1)} collective-permute-done((bf16[32,1024]{1,0:T(8,128)(2,1)S(1)}, bf16[32,1024]{1,0:T(8,128)(2,1)S(1)}, u32[]{:S(2)}, u32[]{:S(2)}) %collective-permute-start.8) | collective-permute-done | bytes 65568 | tf_op jit(solution)/shard_map/ppermute | solution.py:429
  24.2 1.2 %collective-permute-done.7.refs_2_ = bf16[32,1024]{1,0:T(8,128)(2,1)S(1)} collective-permute-done((bf16[32,1024]{1,0:T(8,128)(2,1)S(1)}, bf16[32,1024]{1,0:T(8,128)(2,1)S(1)}, u32[]{:S(2)}, u32[]{:S(2)}) %collective-permute-start.7) | collective-permute-done | bytes 65568 | tf_op jit(solution)/shard_map/ppermute | solution.py:429
  25.4 0.8 %collective-permute-done.6.refs_1_ = bf16[32,1024]{1,0:T(8,128)(2,1)S(1)} collective-permute-done((bf16[32,1024]{1,0:T(8,128)(2,1)S(1)}, bf16[32,1024]{1,0:T(8,128)(2,1)S(1)}, u32[]{:S(2)}, u32[]{:S(2)}) %collective-permute-start.6) | collective-permute-done | bytes 65568 | tf_op jit(solution)/shard_map/ppermute | solution.py:429
  26.2 0.7 %last.1 = (f32[3,7,1024]{2,1,0:T(8,128)}, f32[64,128]{1,0:T(8,128)}) custom-call(bf16[32,1024]{1,0:T(8,128)(2,1)S(1)} %add_convert_fusion.refs_0_, bf16[32,1024]{1,0:T(8,128)(2,1)S(1)} %collective-permute-done.6.refs_1_, bf16[32,1024]{1,0:T(8,128)(2,1)S(1)} %collective-permute-done.7.refs_2_, bf16[32,1024]{1,0:T(8,128)(2,1)S(1)} %collective-permute-done.8.refs_3_), custom_call_target="tpu_custom_call" | custom-call | tf_op jit(solution)/shard_map/last/pallas_call | solution.py:581
  (10 shorter events, 0.0 us)
Async XLA Ops:
  0.6 11.1 %copy-start = (bf16[128,1024]{1,0:T(8,128)(2,1)S(1)}, bf16[128,1024]{1,0:T(8,128)(2,1)}, u32[]{:S(2)}) copy-start(bf16[128,1024]{1,0:T(8,128)(2,1)} %k_ref.3) | copy-start | bytes 786436
  0.6 11.6 %copy-start.3 = (bf16[128,1024]{1,0:T(8,128)(2,1)S(1)}, bf16[128,1024]{1,0:T(8,128)(2,1)}, u32[]{:S(2)}) copy-start(bf16[128,1024]{1,0:T(8,128)(2,1)} %up_ref.3) | copy-start | bytes 786436
  0.7 11.6 %copy-start.2 = (bf16[128,1024]{1,0:T(8,128)(2,1)S(1)}, bf16[128,1024]{1,0:T(8,128)(2,1)}, u32[]{:S(2)}) copy-start(bf16[128,1024]{1,0:T(8,128)(2,1)} %v_ref.3) | copy-start | bytes 786436
  0.7 11.6 %copy-start.1 = (bf16[128,1024]{1,0:T(8,128)(2,1)S(1)}, bf16[128,1024]{1,0:T(8,128)(2,1)}, u32[]{:S(2)}) copy-start(bf16[128,1024]{1,0:T(8,128)(2,1)} %q_ref.3) | copy-start | bytes 786436
  0.7 8.4 %collective-permute-start.1 = (bf16[128,1024]{1,0:T(8,128)(2,1)}, bf16[128,1024]{1,0:T(8,128)(2,1)S(1)}, u32[]{:S(2)}, u32[]{:S(2)}) collective-permute-start(bf16[128,1024]{1,0:T(8,128)(2,1)} %k_ref.3), channel_id=1, source_target_pairs={{0,4},{4,8},{8,12},{12,16},{16,20},{20,24},{24,28},{28,0},{1,5},{5... | collective-permute-start | bytes 786440 | tf_op jit(solution)/shard_map/ppermute | solution.py:460
  2.3 9.9 %collective-permute-start.2 = (bf16[144,1024]{1,0:T(8,128)(2,1)S(1)}, bf16[144,1024]{1,0:T(8,128)(2,1)S(1)}, u32[]{:S(2)}, u32[]{:S(2)}) collective-permute-start(bf16[144,1024]{1,0:T(8,128)(2,1)S(1)} %get-tuple-element.35), channel_id=1, source_target_pairs={{0,4},{4,8},{8,12},{12,16},{16,20},{20,24},{24,28},{28,0},{1,5},{5... | collective-permute-start | bytes 884744 | tf_op jit(solution)/shard_map/ppermute | solution.py:460
  5.0 4.0 %collective-permute-start = (f32[64,128]{1,0:T(8,128)S(1)}, f32[64,128]{1,0:T(8,128)S(1)}, u32[]{:S(2)}, u32[]{:S(2)}) collective-permute-start(f32[64,128]{1,0:T(8,128)S(1)} %get-tuple-element.26), channel_id=1, source_target_pairs={{0,1},{1,0},{2,3},{3,2},{4,5},{5,4},{6,7},{7,6},{8,9},{9,8},{10,11... | collective-permute-start | bytes 98312 | tf_op jit(solution)/shard_map/ppermute | solution.py:429
  6.6 5.7 %collective-permute-start.3 = (bf16[16,1024]{1,0:T(8,128)(2,1)S(1)}, bf16[16,1024]{1,0:T(8,128)(2,1)S(1)}, u32[]{:S(2)}, u32[]{:S(2)}) collective-permute-start(bf16[16,1024]{1,0:T(8,128)(2,1)S(1)} %get-tuple-element.36), channel_id=1, source_target_pairs={{0,8},{4,12},{8,16},{12,20},{16,24},{20,28},{24,0},{28,4},{1,9},{5... | collective-permute-start | bytes 98312 | tf_op jit(solution)/shard_map/ppermute | solution.py:460
  9.1 5.1 %collective-permute-start.4 = (f32[64,128]{1,0:T(8,128)S(1)}, f32[64,128]{1,0:T(8,128)S(1)}, u32[]{:S(2)}, u32[]{:S(2)}) collective-permute-start(f32[64,128]{1,0:T(8,128)S(1)} %add.6.rest_0_), channel_id=1, source_target_pairs={{0,2},{1,3},{2,0},{3,1},{4,6},{5,7},{6,4},{7,5},{8,10},{9,11},{10,... | collective-permute-start | bytes 98312 | tf_op jit(solution)/shard_map/ppermute | solution.py:429
  17.5 1.4 %collective-permute-start.5 = (f32[32,1024]{1,0:T(8,128)S(1)}, f32[32,1024]{1,0:T(8,128)S(1)}, u32[]{:S(2)}, u32[]{:S(2)}) collective-permute-start(f32[32,1024]{1,0:T(8,128)S(1)} %backward.1), channel_id=1, source_target_pairs={{0,4},{4,0},{8,12},{12,8},{16,20},{20,16},{24,28},{28,24},{1,5},{5... | collective-permute-start | bytes 393224 | tf_op jit(solution)/shard_map/ppermute | solution.py:429
  18.9 5.3 %collective-permute-start.8 = (bf16[32,1024]{1,0:T(8,128)(2,1)S(1)}, bf16[32,1024]{1,0:T(8,128)(2,1)S(1)}, u32[]{:S(2)}, u32[]{:S(2)}) collective-permute-start(bf16[32,1024]{1,0:T(8,128)(2,1)S(1)} %add_convert_fusion.refs_0_), channel_id=1, source_target_pairs={{0,24},{4,28},{8,16},{12,20},{16,8},{20,12},{24,0},{28,4},{1,25},{... | collective-permute-start | bytes 196616 | tf_op jit(solution)/shard_map/ppermute | solution.py:429
  20.8 4.6 %collective-permute-start.7 = (bf16[32,1024]{1,0:T(8,128)(2,1)S(1)}, bf16[32,1024]{1,0:T(8,128)(2,1)S(1)}, u32[]{:S(2)}, u32[]{:S(2)}) collective-permute-start(bf16[32,1024]{1,0:T(8,128)(2,1)S(1)} %add_convert_fusion.refs_0_), channel_id=1, source_target_pairs={{0,16},{4,20},{8,24},{12,28},{16,0},{20,4},{24,8},{28,12},{1,17},{... | collective-permute-start | bytes 196616 | tf_op jit(solution)/shard_map/ppermute | solution.py:429
  21.9 4.3 %collective-permute-start.6 = (bf16[32,1024]{1,0:T(8,128)(2,1)S(1)}, bf16[32,1024]{1,0:T(8,128)(2,1)S(1)}, u32[]{:S(2)}, u32[]{:S(2)}) collective-permute-start(bf16[32,1024]{1,0:T(8,128)(2,1)S(1)} %add_convert_fusion.refs_0_), channel_id=1, source_target_pairs={{0,8},{4,12},{8,0},{12,4},{16,24},{20,28},{24,16},{28,20},{1,9},{5... | collective-permute-start | bytes 196616 | tf_op jit(solution)/shard_map/ppermute | solution.py:429

commit v7 on v6

--- a/solution.py
+++ b/solution.py
@@ -412,16 +412,25 @@
 
 
 def last_kernel(scale, *refs):
-    *part_refs, se_ref, mr_ref = refs
-    total = summed([ref[...].astype(F32) for ref in part_refs]) * scale
-    tap_count = se_ref.shape[1]
-    channels = total.shape[1]
+    *part_refs, se_ref, mr_ref, se_here, mr_here, sems = refs
+    tap_count, channels = se_here.shape[1:]
+
+    def total_of(rows):
+        return summed([ref[rows].astype(F32) for ref in part_refs]) * scale
+
+    low = total_of(slice(24, None))
+    mr_here[...] = jnp.concatenate(
+        [low[:, t * LANES : (t + 1) * LANES] for t in range(channels // LANES)], axis=0
+    )
+    copies = [pltpu.make_async_copy(mr_here, mr_ref, sems.at[3])]
+    copies[0].start()
     for i in range(3):
-        se_ref[i] = total[8 * i : 8 * i + tap_count]
-    flat = jnp.concatenate(
-        [total[24:, t * LANES : (t + 1) * LANES] for t in range(channels // LANES)], axis=0
-    )
-    mr_ref[...] = flat
+        se_here[i] = total_of(slice(8 * i, 8 * (i + 1)))[0:tap_count]
+        copy = pltpu.make_async_copy(se_here.at[i], se_ref.at[i], sems.at[i])
+        copy.start()
+        copies.append(copy)
+    for copy in copies:
+        copy.wait()
 
 
 def swapped(value, axis, distance):
@@ -585,7 +594,12 @@
             jax.ShapeDtypeStruct((groups, taps), F32),
         ),
         in_specs=[spec()] * len(parts),
-        out_specs=(spec(),) * 2,
+        out_specs=(spec(pl.ANY),) * 2,
+        scratch_shapes=[
+            pltpu.VMEM((3, tap_count, channels), F32),
+            pltpu.VMEM((groups, taps), F32),
+            pltpu.SemaphoreType.DMA((4,)),
+        ],
         compiler_params=pltpu.CompilerParams(vmem_limit_bytes=LIMIT),
         name="last",
     )(*parts)

time: 27 us -> 27 us (level)
  no operation moved by 1% of the time
where the time goes in v7:
time: 27 us; the launch traced here: 26.9 us
  starting transfers between devices  12.5 us (46%)
  Pallas kernels  8.47 us (31%)
  waiting for transfers between devices  5.07 us (19%)
  between operations  0.79 us (3%)
    ppermute x6, starting transfers between devices, swapped(): return lax.ppermute(value, axis, [(i, i ^ distance) for i in range(count)])  7.86 us
    ppermute x6, waiting for transfers between devices, swapped(): return lax.ppermute(value, axis, [(i, i ^ distance) for i in range(count)])  5.07 us
    ppermute x3, starting transfers between devices, moved_up(): lax.ppermute(value, axis, [(i, (i + steps) % count) for i in range(count)])  4.65 us
    pallas_call x1, Pallas kernels, on_device(): pl.pallas_call(functools.partial(backward_kernel, float(channels * lax.ax...  3.27 us
    pallas_call x1, Pallas kernels, on_device(): pl.pallas_call(functools.partial(forward_kernel, beside), out_shape=(jax....  1.89 us
    pallas_call x1, Pallas kernels, on_device(): pl.pallas_call(functools.partial(first_kernel, span), out_shape=(jax.Shap...  1.16 us
    pallas_call x1, Pallas kernels, on_device(): pl.pallas_call(band_kernel, out_shape=(jax.ShapeDtypeStruct((tiles, stack...  0.96 us
    pallas_call x1, Pallas kernels, on_device(): pl.pallas_call(functools.partial(last_kernel, 1.0 / rows), out_shape=(jax...  0.69 us
  transfers between devices with their start and end apart: 9, of which 4 were waited for; matrix products, arithmetic and copies ran while one was open for 0% of the time, Pallas kernels for 17%

profile of v7, /device:TPU:0, one launch (start us, length us, event | category | flops | bytes accessed | tf_op | source)
XLA Modules:
  0.0 26.9 jit_solution(17991672462577851591)
XLA Ops:
  0.7 0.5 %collective-permute-start.1 = (bf16[128,1024]{1,0:T(8,128)(2,1)}, bf16[128,1024]{1,0:T(8,128)(2,1)S(1)}, u32[]{:S(2)}, u32[]{:S(2)}) collective-permute-start(bf16[128,1024]{1,0:T(8,128)(2,1)} %k_ref.3), channel_id=1, source_target_pairs={{0,4},{4,8},{8,12},{12,16},{16,20},{20,24},{24,28},{28,0},{1,5},{5... | collective-permute-start | bytes 786440 | tf_op jit(solution)/shard_map/ppermute | solution.py:469
  1.2 1.2 %first.1 = (bf16[144,1024]{1,0:T(8,128)(2,1)S(1)}, bf16[16,1024]{1,0:T(8,128)(2,1)S(1)}, f32[64,128]{1,0:T(8,128)S(1)}, f32[25,128]{1,0:T(8,128)S(1)}, bf16[64,1...) custom-call(s32[4]{0:T(128)} %lengths_ref.1, s32[1,128]{1,0:T(1,128)} %bitcast.4, bf16[128,1024]{1,0:T(8,128)(2,1)} %q_ref.3, ...), custom_call_target="tpu_custom_call" | custom-call | flops 1 | bytes 4320000 | tf_op jit(solution)/shard_map/first/pallas_call | solution.py:486
  2.3 2.7 %collective-permute-start.2 = (bf16[144,1024]{1,0:T(8,128)(2,1)S(1)}, bf16[144,1024]{1,0:T(8,128)(2,1)S(1)}, u32[]{:S(2)}, u32[]{:S(2)}) collective-permute-start(bf16[144,1024]{1,0:T(8,128)(2,1)S(1)} %get-tuple-element.35), channel_id=1, source_target_pairs={{0,4},{4,8},{8,12},{12,16},{16,20},{20,24},{24,28},{28,0},{1,5},{5... | collective-permute-start | bytes 884744 | tf_op jit(solution)/shard_map/ppermute | solution.py:469
  5.0 1.6 %collective-permute-start = (f32[64,128]{1,0:T(8,128)S(1)}, f32[64,128]{1,0:T(8,128)S(1)}, u32[]{:S(2)}, u32[]{:S(2)}) collective-permute-start(f32[64,128]{1,0:T(8,128)S(1)} %get-tuple-element.26), channel_id=1, source_target_pairs={{0,1},{1,0},{2,3},{3,2},{4,5},{5,4},{6,7},{7,6},{8,9},{9,8},{10,11... | collective-permute-start | bytes 98312 | tf_op jit(solution)/shard_map/ppermute | solution.py:438
  6.6 1.5 %collective-permute-start.3 = (bf16[16,1024]{1,0:T(8,128)(2,1)S(1)}, bf16[16,1024]{1,0:T(8,128)(2,1)S(1)}, u32[]{:S(2)}, u32[]{:S(2)}) collective-permute-start(bf16[16,1024]{1,0:T(8,128)(2,1)S(1)} %get-tuple-element.36), channel_id=1, source_target_pairs={{0,8},{4,12},{8,16},{12,20},{16,24},{20,28},{24,0},{28,4},{1,9},{5... | collective-permute-start | bytes 98312 | tf_op jit(solution)/shard_map/ppermute | solution.py:469
  8.1 1.0 %band.1 = (bf16[8,256,256]{2,1,0:T(8,128)(2,1)S(1)}, bf16[8,160,256]{2,1,0:T(8,128)(2,1)S(1)}) custom-call(bf16[64,128]{1,0:T(8,128)(2,1)S(1)} %get-tuple-element.27.h_ref), custom_call_target="tpu_custom_call" | custom-call | flops 1 | bytes 3600000 | tf_op jit(solution)/shard_map/band/pallas_call | solution.py:526
  9.0 0.0 collective-permute-done
  9.0 0.0 collective-permute-done.1.k_near_ref
  9.1 2.7 %collective-permute-start.4 = (f32[64,128]{1,0:T(8,128)S(1)}, f32[64,128]{1,0:T(8,128)S(1)}, u32[]{:S(2)}, u32[]{:S(2)}) collective-permute-start(f32[64,128]{1,0:T(8,128)S(1)} %add.6.rest_0_), channel_id=1, source_target_pairs={{0,2},{1,3},{2,0},{3,1},{4,6},{5,7},{6,4},{7,5},{8,10},{9,11},{10,... | collective-permute-start | bytes 98312 | tf_op jit(solution)/shard_map/ppermute | solution.py:438
  11.7 0.5 %keys.1 = (f32[8,280,128]{2,1,0:T(8,128)S(1)}, f32[8,224,128]{2,1,0:T(8,128)S(1)}) custom-call(bf16[128,1024]{1,0:T(8,128)(2,1)S(1)} %copy-done, bf16[128,1024]{1,0:T(8,128)(2,1)S(1)} %collective-permute-done.1.k_near_ref, f32[25,128]{1,0:T(8,128)S(1)} %get-tuple-element.31.note_ref, bf16[3,7,1024]{2,1,0:T(8,128)(2,1)S(1)} %get-tuple-element.32.se_ref), custom_call_target="tpu_custom_call" | custom-call | flops 1 | bytes 1800000 | tf_op jit(solution)/shard_map/keys/pallas_call | solution.py:541
  12.2 0.0 collective-permute-done.3.far_ref
  12.3 0.0 collective-permute-done.2.near_ref
  12.3 1.9 %forward.1 = (f32[8,160,128]{2,1,0:T(8,128)S(1)}, f32[8,40,128]{2,1,0:T(8,128)S(1)}, f32[8,320,128]{2,1,0:T(8,128)S(1)}, f32[8,32,128]{2,1,0:T(8,128)S(1)}, f32[...) custom-call(bf16[128,1024]{1,0:T(8,128)(2,1)S(1)} %copy-done.1, ...), custom_call_target="tpu_custom_call" | custom-call | flops 1 | bytes 7200000 | tf_op jit(solution)/shard_map/forward/pallas_call | solution.py:553
  14.2 0.0 collective-permute-done.4.rest_1_
  14.2 3.3 %backward.1 = f32[32,1024]{1,0:T(8,128)S(1)} custom-call(f32[8,280,128]{2,1,0:T(8,128)S(1)} %get-tuple-element.33.xk_ref, f32[8,224,128]{2,1,0:T(8,128)S(1)} %get-tuple-element.34.ks_ref, f32[8,160,128]{2,1,0:T(8,128)S(1)} %get-tuple-element.38.xq_ref, f32[8,40,128]{2,1,0:T(8,128)S(1)} %get-tuple-element.39.xk_first_ref, ...), custom_call_target="tpu_custom_call" | custom-call | tf_op jit(solution)/shard_map/backward/pallas_call | solution.py:572
  17.5 0.1 collective-permute-start.5
  17.6 1.3 %collective-permute-done.5 = f32[32,1024]{1,0:T(8,128)S(1)} collective-permute-done((f32[32,1024]{1,0:T(8,128)S(1)}, f32[32,1024]{1,0:T(8,128)S(1)}, u32[]{:S(2)}, u32[]{:S(2)}) %collective-permute-start.5) | collective-permute-done | bytes 131104 | tf_op jit(solution)/shard_map/ppermute | solution.py:438
  18.9 1.9 %collective-permute-start.8 = (bf16[32,1024]{1,0:T(8,128)(2,1)S(1)}, bf16[32,1024]{1,0:T(8,128)(2,1)S(1)}, u32[]{:S(2)}, u32[]{:S(2)}) collective-permute-start(bf16[32,1024]{1,0:T(8,128)(2,1)S(1)} %add_convert_fusion.refs_0_), channel_id=1, source_target_pairs={{0,24},{4,28},{8,16},{12,20},{16,8},{20,12},{24,0},{28,4},{1,25},{... | collective-permute-start | bytes 196616 | tf_op jit(solution)/shard_map/ppermute | solution.py:438
  20.8 1.1 %collective-permute-start.7 = (bf16[32,1024]{1,0:T(8,128)(2,1)S(1)}, bf16[32,1024]{1,0:T(8,128)(2,1)S(1)}, u32[]{:S(2)}, u32[]{:S(2)}) collective-permute-start(bf16[32,1024]{1,0:T(8,128)(2,1)S(1)} %add_convert_fusion.refs_0_), channel_id=1, source_target_pairs={{0,16},{4,20},{8,24},{12,28},{16,0},{20,4},{24,8},{28,12},{1,17},{... | collective-permute-start | bytes 196616 | tf_op jit(solution)/shard_map/ppermute | solution.py:438
  21.9 0.5 %collective-permute-start.6 = (bf16[32,1024]{1,0:T(8,128)(2,1)S(1)}, bf16[32,1024]{1,0:T(8,128)(2,1)S(1)}, u32[]{:S(2)}, u32[]{:S(2)}) collective-permute-start(bf16[32,1024]{1,0:T(8,128)(2,1)S(1)} %add_convert_fusion.refs_0_), channel_id=1, source_target_pairs={{0,8},{4,12},{8,0},{12,4},{16,24},{20,28},{24,16},{28,20},{1,9},{5... | collective-permute-start | bytes 196616 | tf_op jit(solution)/shard_map/ppermute | solution.py:438
  22.5 1.8 %collective-permute-done.8.refs_3_ = bf16[32,1024]{1,0:T(8,128)(2,1)S(1)} collective-permute-done((bf16[32,1024]{1,0:T(8,128)(2,1)S(1)}, bf16[32,1024]{1,0:T(8,128)(2,1)S(1)}, u32[]{:S(2)}, u32[]{:S(2)}) %collective-permute-start.8) | collective-permute-done | bytes 65568 | tf_op jit(solution)/shard_map/ppermute | solution.py:438
  24.2 1.2 %collective-permute-done.7.refs_2_ = bf16[32,1024]{1,0:T(8,128)(2,1)S(1)} collective-permute-done((bf16[32,1024]{1,0:T(8,128)(2,1)S(1)}, bf16[32,1024]{1,0:T(8,128)(2,1)S(1)}, u32[]{:S(2)}, u32[]{:S(2)}) %collective-permute-start.7) | collective-permute-done | bytes 65568 | tf_op jit(solution)/shard_map/ppermute | solution.py:438
  25.4 0.8 %collective-permute-done.6.refs_1_ = bf16[32,1024]{1,0:T(8,128)(2,1)S(1)} collective-permute-done((bf16[32,1024]{1,0:T(8,128)(2,1)S(1)}, bf16[32,1024]{1,0:T(8,128)(2,1)S(1)}, u32[]{:S(2)}, u32[]{:S(2)}) %collective-permute-start.6) | collective-permute-done | bytes 65568 | tf_op jit(solution)/shard_map/ppermute | solution.py:438
  26.2 0.7 %last.1 = (f32[3,7,1024]{2,1,0:T(8,128)}, f32[64,128]{1,0:T(8,128)}) custom-call(bf16[32,1024]{1,0:T(8,128)(2,1)S(1)} %add_convert_fusion.refs_0_, bf16[32,1024]{1,0:T(8,128)(2,1)S(1)} %collective-permute-done.6.refs_1_, bf16[32,1024]{1,0:T(8,128)(2,1)S(1)} %collective-permute-done.7.refs_2_, bf16[32,1024]{1,0:T(8,128)(2,1)S(1)} %collective-permute-done.8.refs_3_), custom_call_target="tpu_custom_call" | custom-call | tf_op jit(solution)/shard_map/last/pallas_call | solution.py:590
  (10 shorter events, 0.0 us)
Async XLA Ops:
  0.6 11.1 %copy-start = (bf16[128,1024]{1,0:T(8,128)(2,1)S(1)}, bf16[128,1024]{1,0:T(8,128)(2,1)}, u32[]{:S(2)}) copy-start(bf16[128,1024]{1,0:T(8,128)(2,1)} %k_ref.3) | copy-start | bytes 786436
  0.6 11.6 %copy-start.3 = (bf16[128,1024]{1,0:T(8,128)(2,1)S(1)}, bf16[128,1024]{1,0:T(8,128)(2,1)}, u32[]{:S(2)}) copy-start(bf16[128,1024]{1,0:T(8,128)(2,1)} %up_ref.3) | copy-start | bytes 786436
  0.7 11.6 %copy-start.2 = (bf16[128,1024]{1,0:T(8,128)(2,1)S(1)}, bf16[128,1024]{1,0:T(8,128)(2,1)}, u32[]{:S(2)}) copy-start(bf16[128,1024]{1,0:T(8,128)(2,1)} %v_ref.3) | copy-start | bytes 786436
  0.7 11.6 %copy-start.1 = (bf16[128,1024]{1,0:T(8,128)(2,1)S(1)}, bf16[128,1024]{1,0:T(8,128)(2,1)}, u32[]{:S(2)}) copy-start(bf16[128,1024]{1,0:T(8,128)(2,1)} %q_ref.3) | copy-start | bytes 786436
  0.7 8.4 %collective-permute-start.1 = (bf16[128,1024]{1,0:T(8,128)(2,1)}, bf16[128,1024]{1,0:T(8,128)(2,1)S(1)}, u32[]{:S(2)}, u32[]{:S(2)}) collective-permute-start(bf16[128,1024]{1,0:T(8,128)(2,1)} %k_ref.3), channel_id=1, source_target_pairs={{0,4},{4,8},{8,12},{12,16},{16,20},{20,24},{24,28},{28,0},{1,5},{5... | collective-permute-start | bytes 786440 | tf_op jit(solution)/shard_map/ppermute | solution.py:469
  2.3 9.9 %collective-permute-start.2 = (bf16[144,1024]{1,0:T(8,128)(2,1)S(1)}, bf16[144,1024]{1,0:T(8,128)(2,1)S(1)}, u32[]{:S(2)}, u32[]{:S(2)}) collective-permute-start(bf16[144,1024]{1,0:T(8,128)(2,1)S(1)} %get-tuple-element.35), channel_id=1, source_target_pairs={{0,4},{4,8},{8,12},{12,16},{16,20},{20,24},{24,28},{28,0},{1,5},{5... | collective-permute-start | bytes 884744 | tf_op jit(solution)/shard_map/ppermute | solution.py:469
  5.0 4.0 %collective-permute-start = (f32[64,128]{1,0:T(8,128)S(1)}, f32[64,128]{1,0:T(8,128)S(1)}, u32[]{:S(2)}, u32[]{:S(2)}) collective-permute-start(f32[64,128]{1,0:T(8,128)S(1)} %get-tuple-element.26), channel_id=1, source_target_pairs={{0,1},{1,0},{2,3},{3,2},{4,5},{5,4},{6,7},{7,6},{8,9},{9,8},{10,11... | collective-permute-start | bytes 98312 | tf_op jit(solution)/shard_map/ppermute | solution.py:438
  6.6 5.7 %collective-permute-start.3 = (bf16[16,1024]{1,0:T(8,128)(2,1)S(1)}, bf16[16,1024]{1,0:T(8,128)(2,1)S(1)}, u32[]{:S(2)}, u32[]{:S(2)}) collective-permute-start(bf16[16,1024]{1,0:T(8,128)(2,1)S(1)} %get-tuple-element.36), channel_id=1, source_target_pairs={{0,8},{4,12},{8,16},{12,20},{16,24},{20,28},{24,0},{28,4},{1,9},{5... | collective-permute-start | bytes 98312 | tf_op jit(solution)/shard_map/ppermute | solution.py:469
  9.1 5.1 %collective-permute-start.4 = (f32[64,128]{1,0:T(8,128)S(1)}, f32[64,128]{1,0:T(8,128)S(1)}, u32[]{:S(2)}, u32[]{:S(2)}) collective-permute-start(f32[64,128]{1,0:T(8,128)S(1)} %add.6.rest_0_), channel_id=1, source_target_pairs={{0,2},{1,3},{2,0},{3,1},{4,6},{5,7},{6,4},{7,5},{8,10},{9,11},{10,... | collective-permute-start | bytes 98312 | tf_op jit(solution)/shard_map/ppermute | solution.py:438
  17.5 1.4 %collective-permute-start.5 = (f32[32,1024]{1,0:T(8,128)S(1)}, f32[32,1024]{1,0:T(8,128)S(1)}, u32[]{:S(2)}, u32[]{:S(2)}) collective-permute-start(f32[32,1024]{1,0:T(8,128)S(1)} %backward.1), channel_id=1, source_target_pairs={{0,4},{4,0},{8,12},{12,8},{16,20},{20,16},{24,28},{28,24},{1,5},{5... | collective-permute-start | bytes 393224 | tf_op jit(solution)/shard_map/ppermute | solution.py:438
  18.9 5.3 %collective-permute-start.8 = (bf16[32,1024]{1,0:T(8,128)(2,1)S(1)}, bf16[32,1024]{1,0:T(8,128)(2,1)S(1)}, u32[]{:S(2)}, u32[]{:S(2)}) collective-permute-start(bf16[32,1024]{1,0:T(8,128)(2,1)S(1)} %add_convert_fusion.refs_0_), channel_id=1, source_target_pairs={{0,24},{4,28},{8,16},{12,20},{16,8},{20,12},{24,0},{28,4},{1,25},{... | collective-permute-start | bytes 196616 | tf_op jit(solution)/shard_map/ppermute | solution.py:438
  20.8 4.6 %collective-permute-start.7 = (bf16[32,1024]{1,0:T(8,128)(2,1)S(1)}, bf16[32,1024]{1,0:T(8,128)(2,1)S(1)}, u32[]{:S(2)}, u32[]{:S(2)}) collective-permute-start(bf16[32,1024]{1,0:T(8,128)(2,1)S(1)} %add_convert_fusion.refs_0_), channel_id=1, source_target_pairs={{0,16},{4,20},{8,24},{12,28},{16,0},{20,4},{24,8},{28,12},{1,17},{... | collective-permute-start | bytes 196616 | tf_op jit(solution)/shard_map/ppermute | solution.py:438
  21.9 4.3 %collective-permute-start.6 = (bf16[32,1024]{1,0:T(8,128)(2,1)S(1)}, bf16[32,1024]{1,0:T(8,128)(2,1)S(1)}, u32[]{:S(2)}, u32[]{:S(2)}) collective-permute-start(bf16[32,1024]{1,0:T(8,128)(2,1)S(1)} %add_convert_fusion.refs_0_), channel_id=1, source_target_pairs={{0,8},{4,12},{8,0},{12,4},{16,24},{20,28},{24,16},{28,20},{1,9},{5... | collective-permute-start | bytes 196616 | tf_op jit(solution)/shard_map/ppermute | solution.py:438
